TPU v7x, 32 devices: a whole 2x2x4 slice. The times are simulated.
32 devices in a mesh: seq: 16 (over z, y, x), dp: 2 (over core).
Axes of the slice: x: 2, y: 2, z: 4, core: 2. Of those that a mesh axis runs over, the one named last changes fastest.
Arguments:
- tokens: bfloat16 [2, 65536, 1024], P('dp', 'seq'), may hold values from -6 to 6
- lengths: int32 [2, 64], P('dp', 'seq'), may hold values from 512 to 1024, as said below
- routed_index: int32 [2, 64, 128], P('dp', 'seq'), may hold values from 0 to 1023, as said below
- out_grad: bfloat16 [2, 65536, 1024], P('dp', 'seq'), may hold values from -6 to 6
- gain_attn: bfloat16 [1024], replicated, may hold values from 0.099609375 to 1.8984375
- w_router: bfloat16 [1024], replicated, may hold values from -0.1875 to 0.1875
- w_query: bfloat16 [1024, 1024], replicated, may hold values from -0.25 to 0.25
- w_key: bfloat16 [1024, 1024], replicated, may hold values from -0.25 to 0.25
- w_value: bfloat16 [1024, 1024], replicated, may hold values from -0.1875 to 0.1875
- w_out: bfloat16 [1024, 1024], replicated, may hold values from -0.5 to 0.5
- gain_mlp: bfloat16 [1024], replicated, may hold values from 0.099609375 to 1.8984375
- w_up: bfloat16 [1024, 4096], replicated, may hold values from -0.1875 to 0.1875
- w_down: bfloat16 [4096, 1024], replicated, may hold values from -0.09375 to 0.09375
Outputs:
- mixed_out: bfloat16 [2, 65536, 1024], P('dp', 'seq')
- token_grad: float32 [2, 65536, 1024], P('dp', 'seq')
- grad_gain_attn: float32 [1024], P(('seq', 'dp'))
- grad_router: float32 [1024], P(('seq', 'dp'))
- grad_query: float32 [1024, 1024], P(None, ('seq', 'dp'))
- grad_key: float32 [1024, 1024], P(None, ('seq', 'dp'))
- grad_value: float32 [1024, 1024], P(None, ('seq', 'dp'))
- grad_out: float32 [1024, 1024], P(None, ('seq', 'dp'))
- grad_gain_mlp: float32 [1024], P(('seq', 'dp'))
- grad_up: float32 [1024, 4096], P(None, ('seq', 'dp'))
- grad_down: float32 [4096, 1024], P(None, ('seq', 'dp'))
Inputs may be any that keep to these rules, and one draw needn't show every extreme that they name: Multiples of 8. In each row (a group of 64 sequences) the lengths sum to exactly 49152, and some length equals 1024. `routed_index`: for a sequence of length n the first n // 8 entries are distinct positions below n in increasing order; the remaining entries are positions below n that are not routed.
All inputs are finite; a program needn't handle non-finite values.
Results may differ from a plain program's by a relative error of at most 0.012.
The roundings to bfloat16 on the way count: a program that leaves them out, or rounds other values in their place, can miss the bound.
Values may be sent and summed in bfloat16 or wider, within the bound.
No kernel may reach another device: no remote copies, remote signals or barrier semaphores. Data moves between devices by JAX's collectives and lax.ppermute only.
A program may use at most 256 MiB of HBM per device.

v0:
```python
import jax
import jax.numpy as jnp
from jax import lax
from jax.sharding import PartitionSpec as P

H = 16


norm_eps = 1e-05


def norm_rows(values):
    inv_scale = lax.rsqrt(jnp.mean(values * values, axis=-1, keepdims=True) + norm_eps)
    return (values * inv_scale, inv_scale)


def norm_back(grad_in, normed, inv_scale):
    return inv_scale * (grad_in - normed * jnp.mean(grad_in * normed, axis=-1, keepdims=True))


def plain_dot(left_side, right_side):
    return jnp.dot(left_side, right_side, preferred_element_type=jnp.float32)


def first_dot(left_side, right_side):
    return lax.dot_general(
        left_side, right_side, (((0,), (0,)), ((), ())), preferred_element_type=jnp.float32
    )


def last_dot(left_side, right_side):
    return lax.dot_general(
        left_side, right_side, (((1,), (1,)), ((), ())), preferred_element_type=jnp.float32
    )


def gelu_slope(values):
    normal_cdf = 0.5 * (1.0 + lax.erf(values * 0.7071067811865476))
    return normal_cdf + values * jnp.exp(-0.5 * values * values) * 0.3989422804014327


def on_device(
    tokens,
    lengths,
    routed_index,
    out_grad,
    gain_attn,
    w_router,
    w_query,
    w_key,
    w_value,
    w_out,
    gain_mlp,
    w_up,
    w_down,
):
    seq_count = lengths.shape[1]
    slot_count = routed_index.shape[2]
    seq_slots = tokens.shape[1] // seq_count
    model_width = tokens.shape[2]
    head_size = model_width // H
    row_count = seq_count * slot_count
    inputs = tokens[0].reshape(seq_count, seq_slots, model_width)
    routed = lengths[0] // 8
    slot_index = routed_index[0]
    slot_ids = jnp.arange(slot_count, dtype=jnp.int32)
    live_slot = slot_ids[None, :] < routed[:, None]
    places = jnp.arange(seq_slots, dtype=jnp.int32)
    picked = slot_index[:, :, None] == places[None, None, :]
    pick_all = picked.astype(jnp.bfloat16)
    pick_live = (picked & live_slot[:, :, None]).astype(jnp.bfloat16)
    chosen = jnp.einsum(
        "ecl,eld->ecd", pick_all, inputs, preferred_element_type=jnp.float32
    ).astype(jnp.bfloat16)
    chosen_wide = chosen.astype(jnp.float32)
    router_logit = jnp.einsum("ecd,d->ec", chosen, w_router, preferred_element_type=jnp.float32)
    router_score = jax.nn.sigmoid(router_logit)
    normed_one, scale_one = norm_rows(chosen_wide)
    first_in = (
        (normed_one * gain_attn.astype(jnp.float32))
        .astype(jnp.bfloat16)
        .reshape(row_count, model_width)
    )
    queries = (
        (plain_dot(first_in, w_query) * 0.125)
        .astype(jnp.bfloat16)
        .reshape(seq_count, slot_count, H, head_size)
    )
    key_rows = (
        plain_dot(first_in, w_key).astype(jnp.bfloat16).reshape(seq_count, slot_count, H, head_size)
    )
    value_rows = (
        plain_dot(first_in, w_value)
        .astype(jnp.bfloat16)
        .reshape(seq_count, slot_count, H, head_size)
    )
    raw_scores = jnp.einsum(
        "eihk,ejhk->ehij", queries, key_rows, preferred_element_type=jnp.float32
    )
    allowed = (slot_ids[None, :] <= slot_ids[:, None])[None, None] & live_slot[:, None, None, :]
    masked = jnp.where(allowed, raw_scores, -1e30)
    row_peak = jnp.max(masked, axis=-1, keepdims=True)
    exp_scores = jnp.exp(masked - row_peak)
    attn_probs = exp_scores / jnp.sum(exp_scores, axis=-1, keepdims=True)
    probs_low = attn_probs.astype(jnp.bfloat16)
    attn_mix = (
        jnp.einsum("ehij,ejhk->eihk", probs_low, value_rows, preferred_element_type=jnp.float32)
        .astype(jnp.bfloat16)
        .reshape(row_count, model_width)
    )
    attn_out = plain_dot(attn_mix, w_out).reshape(seq_count, slot_count, model_width)
    after_attn = chosen_wide + attn_out
    normed_two, scale_two = norm_rows(after_attn)
    second_in = (
        (normed_two * gain_mlp.astype(jnp.float32))
        .astype(jnp.bfloat16)
        .reshape(row_count, model_width)
    )
    node_count = lax.axis_size("seq")
    pair_slots = -(-row_count // node_count)
    own_node = lax.axis_index("seq")
    total_here = jnp.sum(routed)
    counts = lax.all_gather(total_here[None], "seq", axis=0, tiled=True)
    offsets = jnp.cumsum(counts) - counts
    node_ids = jnp.arange(node_count, dtype=jnp.int32)
    own_offset = jnp.sum(jnp.where(node_ids == own_node, offsets, 0))
    seq_start = jnp.cumsum(routed) - routed
    slot_rank = (seq_start[:, None] + slot_ids[None, :]).reshape(row_count)
    slot_alive = live_slot.reshape(row_count)
    target_ids = jnp.arange(node_count * pair_slots, dtype=jnp.int32)
    dest_node = target_ids // pair_slots
    turn_slot = target_ids % pair_slots
    wanted = (dest_node - own_offset) % node_count + node_count * turn_slot
    send_sel = ((wanted[:, None] == slot_rank[None, :]) & slot_alive[None, :]).astype(jnp.bfloat16)
    source_hot = dest_node[:, None] == node_ids[None, :]
    src_offset = jnp.sum(jnp.where(source_hot, offsets[None, :], 0), axis=1)
    src_count = jnp.sum(jnp.where(source_hot, counts[None, :], 0), axis=1)
    got_rank = (own_node - src_offset) % node_count + node_count * turn_slot
    live_in = got_rank < src_count
    place_row = (src_offset + got_rank) // node_count
    batch_rows = seq_count * 3 * seq_slots // 32
    batch_ids = jnp.arange(batch_rows, dtype=jnp.int32)
    recv_sel = ((place_row[None, :] == batch_ids[:, None]) & live_in[None, :]).astype(jnp.bfloat16)
    sent_rows = (
        plain_dot(send_sel, second_in)
        .astype(jnp.bfloat16)
        .reshape(node_count, pair_slots, model_width)
    )
    arrived = lax.all_to_all(sent_rows, "seq", split_axis=0, concat_axis=0, tiled=True).reshape(
        node_count * pair_slots, model_width
    )
    mlp_in = plain_dot(recv_sel, arrived).astype(jnp.bfloat16)
    hidden_pre = plain_dot(mlp_in, w_up)
    hidden_act = jax.nn.gelu(hidden_pre, approximate=False).astype(jnp.bfloat16)
    mlp_rows = plain_dot(hidden_act, w_down).astype(jnp.bfloat16)
    going_home = (
        first_dot(recv_sel, mlp_rows)
        .astype(jnp.bfloat16)
        .reshape(node_count, pair_slots, model_width)
    )
    returned = lax.all_to_all(going_home, "seq", split_axis=0, concat_axis=0, tiled=True).reshape(
        node_count * pair_slots, model_width
    )
    mlp_out = first_dot(send_sel, returned)
    branch_sum = attn_out + mlp_out.reshape(seq_count, slot_count, model_width)
    weighted = router_score[..., None] * branch_sum
    pick_wide = pick_live.astype(jnp.float32)
    result = inputs.astype(jnp.float32) + jnp.einsum(
        "ecl,ecd->eld", pick_wide, weighted, precision=lax.Precision.HIGHEST
    )
    mixed_out = result.astype(jnp.bfloat16).reshape(1, seq_count * seq_slots, model_width)
    cotangent = out_grad[0].reshape(seq_count, seq_slots, model_width)
    pulled = jnp.einsum("ecl,eld->ecd", pick_live, cotangent, preferred_element_type=jnp.float32)
    score_pull = jnp.sum(pulled * branch_sum, axis=-1)
    logit_grad = score_pull * router_score * (1.0 - router_score)
    delta_grad = router_score[..., None] * pulled
    mlp_grad = delta_grad.astype(jnp.bfloat16).reshape(row_count, model_width)
    outgoing = (
        plain_dot(send_sel, mlp_grad)
        .astype(jnp.bfloat16)
        .reshape(node_count, pair_slots, model_width)
    )
    incoming = lax.all_to_all(outgoing, "seq", split_axis=0, concat_axis=0, tiled=True).reshape(
        node_count * pair_slots, model_width
    )
    mlp_grad_rows = plain_dot(recv_sel, incoming).astype(jnp.bfloat16)
    resend = (
        plain_dot(send_sel, second_in)
        .astype(jnp.bfloat16)
        .reshape(node_count, pair_slots, model_width)
    )
    again_rows = lax.all_to_all(resend, "seq", split_axis=0, concat_axis=0, tiled=True).reshape(
        node_count * pair_slots, model_width
    )
    mlp_in = plain_dot(recv_sel, again_rows).astype(jnp.bfloat16)
    hidden_pre = plain_dot(mlp_in, w_up)
    hidden_act = jax.nn.gelu(hidden_pre, approximate=False).astype(jnp.bfloat16)
    down_grad = first_dot(hidden_act, mlp_grad_rows)
    act_grad = last_dot(mlp_grad_rows, w_down)
    pre_grad = (act_grad * gelu_slope(hidden_pre)).astype(jnp.bfloat16)
    up_grad = first_dot(mlp_in, pre_grad)
    in_grad = last_dot(pre_grad, w_up).astype(jnp.bfloat16)
    grad_home = (
        first_dot(recv_sel, in_grad)
        .astype(jnp.bfloat16)
        .reshape(node_count, pair_slots, model_width)
    )
    grad_back = lax.all_to_all(grad_home, "seq", split_axis=0, concat_axis=0, tiled=True).reshape(
        node_count * pair_slots, model_width
    )
    second_grad = first_dot(send_sel, grad_back)
    second_grad = second_grad.reshape(seq_count, slot_count, model_width)
    gain_mlp_grad = jnp.sum(second_grad * normed_two, axis=(0, 1))
    after_grad = norm_back(second_grad * gain_mlp.astype(jnp.float32), normed_two, scale_two)
    attn_grad = (delta_grad + after_grad).astype(jnp.bfloat16).reshape(row_count, model_width)
    out_w_grad = first_dot(attn_mix, attn_grad)
    mix_grad = (
        last_dot(attn_grad, w_out).astype(jnp.bfloat16).reshape(seq_count, slot_count, H, head_size)
    )
    prob_grad = jnp.einsum(
        "eihk,ejhk->ehij", mix_grad, value_rows, preferred_element_type=jnp.float32
    )
    score_grad = (
        attn_probs * (prob_grad - jnp.sum(prob_grad * attn_probs, axis=-1, keepdims=True))
    ).astype(jnp.bfloat16)
    value_grad = (
        jnp.einsum("ehij,eihk->ejhk", probs_low, mix_grad, preferred_element_type=jnp.float32)
        .astype(jnp.bfloat16)
        .reshape(row_count, model_width)
    )
    query_grad = (
        jnp.einsum("ehij,ejhk->eihk", score_grad, key_rows, preferred_element_type=jnp.float32)
        .astype(jnp.bfloat16)
        .reshape(row_count, model_width)
    )
    key_grad = (
        jnp.einsum("ehij,eihk->ejhk", score_grad, queries, preferred_element_type=jnp.float32)
        .astype(jnp.bfloat16)
        .reshape(row_count, model_width)
    )
    query_w_grad = first_dot(first_in, query_grad) * 0.125
    key_w_grad = first_dot(first_in, key_grad)
    value_w_grad = first_dot(first_in, value_grad)
    first_grad = (
        last_dot(query_grad, w_query) * 0.125
        + last_dot(key_grad, w_key)
        + last_dot(value_grad, w_value)
    )
    first_grad = first_grad.reshape(seq_count, slot_count, model_width)
    gain_attn_grad = jnp.sum(first_grad * normed_one, axis=(0, 1))
    chosen_grad = (
        norm_back(first_grad * gain_attn.astype(jnp.float32), normed_one, scale_one)
        + after_grad
        + logit_grad[..., None] * w_router.astype(jnp.float32)
    )
    router_grad = jnp.einsum("ec,ecd->d", logit_grad, chosen_wide, precision=lax.Precision.HIGHEST)
    token_grad = cotangent.astype(jnp.float32) + jnp.einsum(
        "ecl,ecd->eld", pick_wide, chosen_grad, precision=lax.Precision.HIGHEST
    )
    token_grad = token_grad.reshape(1, seq_count * seq_slots, model_width)
    terms = (
        gain_attn_grad,
        router_grad,
        query_w_grad,
        key_w_grad,
        value_w_grad,
        out_w_grad,
        gain_mlp_grad,
        up_grad,
        down_grad,
    )
    summed = (
        lax.psum_scatter(terms[0], ("seq", "dp"), scatter_dimension=0, tiled=True),
        lax.psum_scatter(terms[1], ("seq", "dp"), scatter_dimension=0, tiled=True),
        lax.psum_scatter(terms[2], ("seq", "dp"), scatter_dimension=1, tiled=True),
        lax.psum_scatter(terms[3], ("seq", "dp"), scatter_dimension=1, tiled=True),
        lax.psum_scatter(terms[4], ("seq", "dp"), scatter_dimension=1, tiled=True),
        lax.psum_scatter(terms[5], ("seq", "dp"), scatter_dimension=1, tiled=True),
        lax.psum_scatter(terms[6], ("seq", "dp"), scatter_dimension=0, tiled=True),
        lax.psum_scatter(terms[7], ("seq", "dp"), scatter_dimension=1, tiled=True),
        lax.psum_scatter(terms[8], ("seq", "dp"), scatter_dimension=1, tiled=True),
    )
    return (
        mixed_out,
        token_grad,
        summed[0],
        summed[1],
        summed[2],
        summed[3],
        summed[4],
        summed[5],
        summed[6],
        summed[7],
        summed[8],
    )


def solution(mesh):
    in_specs = (
        P("dp", "seq", None),
        P("dp", "seq"),
        P("dp", "seq", None),
        P("dp", "seq", None),
        P(),
        P(),
        P(),
        P(),
        P(),
        P(),
        P(),
        P(),
        P(),
    )
    out_specs = (
        P("dp", "seq", None),
        P("dp", "seq", None),
        P(("seq", "dp")),
        P(("seq", "dp")),
        P(None, ("seq", "dp")),
        P(None, ("seq", "dp")),
        P(None, ("seq", "dp")),
        P(None, ("seq", "dp")),
        P(("seq", "dp")),
        P(None, ("seq", "dp")),
        P(None, ("seq", "dp")),
    )
    return jax.shard_map(
        on_device, mesh=mesh, in_specs=in_specs, out_specs=out_specs, check_vma=False
    )
```

profile of v0, /device:TPU:0, one launch (start us, length us, event | category | flops | bytes accessed | tf_op | source)
XLA Modules:
  0.0 1194.4 jit_solution(7100424244832348069)
XLA Ops:
  9.3 5.1 fusion.32
  52.0 16.7 %all-reduce = s32[16]{0:T(128)S(1)} all-reduce(s32[16]{0:T(128)S(1)} %dynamic-update-slice), channel_id=1, replica_groups=mesh['seq'=16,'dp'=2] {'seq'}, use_global_device_ids=true, to_apply=%add | all-reduce | flops 16 | bytes 128
  86.9 6.2 multiply_convert_fusion.3
  94.8 14.0 %all-to-all-done = bf16[16,32,1024]{2,1,0:T(8,128)(2,1)} async-done(((bf16[16,32,1024]{2,1,0:T(8,128)(2,1)}), bf16[16,32,1024]{2,1,0:T(8,128)(2,1)}, u32[]{:S(2)}, u32[]{:S(2)}) %all-to-all-start) | async-done | bytes 1048608 | tf_op jit(solution)/shard_map/all_to_all | solution.py:149
  116.7 19.8 %all-to-all-done.2 = bf16[16,32,1024]{2,1,0:T(8,128)(2,1)} async-done(((bf16[16,32,1024]{2,1,0:T(8,128)(2,1)}), bf16[16,32,1024]{2,1,0:T(8,128)(2,1)}, u32[]{:S(2)}, u32[]{:S(2)}) %all-to-all-start.2) | async-done | bytes 1048608 | tf_op jit(solution)/shard_map/all_to_all | solution.py:183
  138.3 19.3 %fusion.3 = (bf16[384,4096]{1,0:T(8,128)(2,1)}, f32[384,4096]{1,0:T(8,128)S(1)}) fusion(bf16[384,1024]{1,0:T(8,128)(2,1)} %convolution_convert_fusion.14, bf16[1024,4096]{1,0:T(8,128)(2,1)} %param.24), kind=kOutput, calls=%fused_computation.7 | convolution fusion | flops 3323461632 | bytes 18612224 | tf_op jit(solution)/shard_map/dot_general | solution.py:22
  157.6 8.3 fusion.9
  166.0 9.3 convolution_convert_fusion.4
  175.3 5.9 all-to-all-start.3
  181.2 9.3 convolution_convert_fusion.6
  190.5 13.7 %all-to-all-done.3 = bf16[16,32,1024]{2,1,0:T(8,128)(2,1)} async-done(((bf16[16,32,1024]{2,1,0:T(8,128)(2,1)}), bf16[16,32,1024]{2,1,0:T(8,128)(2,1)}, u32[]{:S(2)}, u32[]{:S(2)}) %all-to-all-start.3) | async-done | bytes 1048608 | tf_op jit(solution)/shard_map/all_to_all | solution.py:208
  204.2 6.0 all-to-all-start.1
  214.6 18.5 %all-to-all-done.1 = bf16[16,32,1024]{2,1,0:T(8,128)(2,1)} async-done(((bf16[16,32,1024]{2,1,0:T(8,128)(2,1)}), bf16[16,32,1024]{2,1,0:T(8,128)(2,1)}, u32[]{:S(2)}, u32[]{:S(2)}) %all-to-all-start.1) | async-done | bytes 1048608 | tf_op jit(solution)/shard_map/all_to_all | solution.py:161
  282.2 10.1 fusion.135
  293.4 10.0 fusion.136
  311.8 41.4 %all-reduce.4 = (f32[1024]{0:T(1024)S(1)}, f32[1024]{0:T(1024)S(1)}, f32[1024]{0:T(1024)S(1)}) all-reduce(f32[1024]{0:T(1024)S(1)} %get-tuple-element.13, f32[1024]{0:T(1024)S(1)} %bitcast.193, f32[1024]{0:T(1024)S(1)} %get-tuple-element.11), channel_id=2, replica_groups=mesh['seq'=16,'dp'=2] {'seq','dp'}, use_global_device_ids=true, to_apply=%region_15.16.clone | all-reduce | flops 3072 | bytes 24576
  355.0 13.2 %add_convert_fusion = bf16[4,1024,1024]{2,1,0:T(8,128)(2,1)} fusion(bf16[4,1024,1024]{2,1,0:T(8,128)(2,1)} %bitcast.161, f32[4,128,1024]{2,1,0:T(8,128)} %get-tuple-element.41, f32[4,128]{1,0:T(4,128)S(1)} %get-tuple-element.45, s32[4,128]{1,0:T(4,128)S(1)} %bitcast.188, pred[4,128]{1,0:T(4,128)(4,1)S(1)} %get-tuple-element.29), kind=kOutput, calls=%fused_computation.2 | convolution fusion | flops 6456606720 | bytes 18878976 | tf_op jit(solution)/shard_map/ecl,ecd->eld/dot_general | solution.py:168
  368.2 14.0 %convert_add_fusion = f32[4,1024,1024]{2,1,0:T(8,128)} fusion(bf16[4,1024,1024]{2,1,0:T(8,128)(2,1)} %bitcast.156, bf16[4,128,1024]{2,1,0:T(8,128)(2,1)S(1)} %get-tuple-element.31, f32[4,128,1024]{2,1,0:T(8,128)S(1)} %bitcast.158, f32[1024]{0:T(1024)S(1)} %convert_element_type.153, f32[4,128]{1,0:T(4,128)S(1)} %subtract_multiply_fusion.2, ...), kind=kOutput, calls=%fused_computation.1 | convolution fusion | flops 6459752448 | bytes 32530944 | tf_op jit(solution)/shard_map/ecl,ecd->eld/dot_general | solution.py:257
  382.2 17.8 %reduce-scatter.7.cloned.1.call-done = f32[1024,32]{0,1:T(8,128)} async-done(((f32[1024,1024]{0,1:T(8,128)}), f32[1024,32]{0,1:T(8,128)}) %reduce-scatter.7.cloned.1.call-update) | async-done | bytes 131088 | tf_op jit(solution)/shard_map/reduce_scatter | solution.py:275
  400.0 139.8 %reduce-scatter.9.cloned.1.call-done = f32[1024,32]{0,1:T(8,128)} async-done(((f32[1024,1024]{0,1:T(8,128)}), f32[1024,32]{0,1:T(8,128)}) %reduce-scatter.9.cloned.1.call-update) | async-done | bytes 131088 | tf_op jit(solution)/shard_map/reduce_scatter | solution.py:276
  539.8 139.5 %reduce-scatter.13.cloned.1.call-done = f32[1024,32]{0,1:T(8,128)} async-done(((f32[1024,1024]{0,1:T(8,128)}), f32[1024,32]{0,1:T(8,128)}) %reduce-scatter.13.cloned.1.call-update) | async-done | bytes 131088 | tf_op jit(solution)/shard_map/reduce_scatter | solution.py:278
  679.2 139.5 %reduce-scatter.11.cloned.1.call-done = f32[1024,32]{0,1:T(8,128)} async-done(((f32[1024,1024]{0,1:T(8,128)}), f32[1024,32]{0,1:T(8,128)}) %reduce-scatter.11.cloned.1.call-update) | async-done | bytes 131088 | tf_op jit(solution)/shard_map/reduce_scatter | solution.py:277
  818.7 181.4 %reduce-scatter.15.cloned.1.call-done = f32[1024,128]{1,0:T(8,128)} async-done(((f32[1024,4096]{1,0:T(8,128)}), f32[1024,128]{1,0:T(8,128)}) %reduce-scatter.15.cloned.1.call-update) | async-done | bytes 524304 | tf_op jit(solution)/shard_map/reduce_scatter | solution.py:280
  1000.1 187.2 %reduce-scatter.17.cloned.1.call-done = f32[4096,32]{0,1:T(8,128)} async-done(((f32[4096,1024]{0,1:T(8,128)}), f32[4096,32]{0,1:T(8,128)}) %reduce-scatter.17.cloned.1.call-update) | async-done | bytes 524304 | tf_op jit(solution)/shard_map/reduce_scatter | solution.py:281
  (170 shorter events, 133.6 us)
Async XLA Ops:
  7.2 71.8 %copy-start = (bf16[1024,1024]{1,0:T(8,128)(2,1)S(1)}, bf16[1024,1024]{1,0:T(8,128)(2,1)}, u32[]{:S(2)}) copy-start(bf16[1024,1024]{1,0:T(8,128)(2,1)} %param.22) | copy-start | bytes 6291460
  9.3 7.0 copy-start.13
  42.0 7.6 copy-start.35
  42.0 8.0 copy-start.38
  42.0 8.0 copy-start.40
  80.7 6.1 copy-start.29
  82.5 26.3 %all-to-all-start = ((bf16[16,32,1024]{2,1,0:T(8,128)(2,1)}), bf16[16,32,1024]{2,1,0:T(8,128)(2,1)}, u32[]{:S(2)}, u32[]{:S(2)}) async-start(bf16[16,32,1024]{2,1,0:T(8,128)(2,1)} %bitcast.183), calls=%async_computation | async-start | bytes 2097152 | tf_op jit(solution)/shard_map/all_to_all | solution.py:149
  108.8 27.7 %all-to-all-start.2 = ((bf16[16,32,1024]{2,1,0:T(8,128)(2,1)}), bf16[16,32,1024]{2,1,0:T(8,128)(2,1)}, u32[]{:S(2)}, u32[]{:S(2)}) async-start(bf16[16,32,1024]{2,1,0:T(8,128)(2,1)} %bitcast.181), calls=%async_computation.2 | async-start | bytes 2097152 | tf_op jit(solution)/shard_map/all_to_all | solution.py:183
  138.3 19.3 %copy-start.26 = (bf16[384,1024]{1,0:T(8,128)(2,1)}, bf16[384,1024]{1,0:T(8,128)(2,1)S(1)}, u32[]{:S(2)}) copy-start(bf16[384,1024]{1,0:T(8,128)(2,1)S(1)} %convolution_convert_fusion.12) | copy-start | bytes 2359300
  175.3 28.9 %all-to-all-start.3 = ((bf16[16,32,1024]{2,1,0:T(8,128)(2,1)}), bf16[16,32,1024]{2,1,0:T(8,128)(2,1)}, u32[]{:S(2)}, u32[]{:S(2)}) async-start(bf16[16,32,1024]{2,1,0:T(8,128)(2,1)} %bitcast.184), calls=%async_computation.3 | async-start | bytes 2097152 | tf_op jit(solution)/shard_map/all_to_all | solution.py:208
  204.2 28.9 %all-to-all-start.1 = ((bf16[16,32,1024]{2,1,0:T(8,128)(2,1)}), bf16[16,32,1024]{2,1,0:T(8,128)(2,1)}, u32[]{:S(2)}, u32[]{:S(2)}) async-start(bf16[16,32,1024]{2,1,0:T(8,128)(2,1)} %bitcast.182), calls=%async_computation.1 | async-start | bytes 2097152 | tf_op jit(solution)/shard_map/all_to_all | solution.py:161
  210.2 189.8 %reduce-scatter.7.cloned.1.call-start = ((), (), s32[]{:S(2)}) async-start(), calls=%async_computation.10 | async-start | bytes 4325376 | tf_op jit(solution)/shard_map/reduce_scatter | solution.py:275
  258.2 281.6 %reduce-scatter.9.cloned.1.call-start = ((), (), s32[]{:S(2)}) async-start(), calls=%async_computation.11 | async-start | bytes 4325376 | tf_op jit(solution)/shard_map/reduce_scatter | solution.py:276
  266.6 412.6 %reduce-scatter.13.cloned.1.call-start = ((), (), s32[]{:S(2)}) async-start(), calls=%async_computation.13 | async-start | bytes 4325376 | tf_op jit(solution)/shard_map/reduce_scatter | solution.py:278
  272.0 5.9 copy-start.21
  272.0 546.7 %reduce-scatter.11.cloned.1.call-start = ((), (), s32[]{:S(2)}) async-start(), calls=%async_computation.12 | async-start | bytes 4325376 | tf_op jit(solution)/shard_map/reduce_scatter | solution.py:277
  281.1 719.0 %reduce-scatter.15.cloned.1.call-start = ((), (), s32[]{:S(2)}) async-start(), calls=%async_computation.14 | async-start | bytes 17301504 | tf_op jit(solution)/shard_map/reduce_scatter | solution.py:280
  292.3 895.0 %reduce-scatter.17.cloned.1.call-start = ((), (), s32[]{:S(2)}) async-start(), calls=%async_computation.15 | async-start | bytes 17301504 | tf_op jit(solution)/shard_map/reduce_scatter | solution.py:281
  311.1 43.9 %copy-start.4 = (f32[512,1024]{1,0:T(8,128)}, f32[512,1024]{1,0:T(8,128)S(1)}, u32[]{:S(2)}) copy-start(f32[512,1024]{1,0:T(8,128)S(1)} %add_add_fusion) | copy-start | bytes 6291460
  311.1 43.9 %copy-start.30 = (s32[1,4,128]{2,1,0:T(4,128)S(1)}, s32[1,4,128]{2,1,0:T(4,128)}, u32[]{:S(2)}) copy-start(s32[1,4,128]{2,1,0:T(4,128)} %param.15) | copy-start | bytes 6148
  355.0 13.2 %copy-start.3 = (f32[4,128,1024]{2,1,0:T(8,128)S(1)}, f32[4,128,1024]{2,1,0:T(8,128)}, u32[]{:S(2)}) copy-start(f32[4,128,1024]{2,1,0:T(8,128)} %copy-done.2) | copy-start | bytes 6291460
  355.0 13.2 %copy-start.5 = (f32[512,1024]{1,0:T(8,128)S(1)}, f32[512,1024]{1,0:T(8,128)}, u32[]{:S(2)}) copy-start(f32[512,1024]{1,0:T(8,128)} %copy-done.4) | copy-start | bytes 6291460
  355.0 13.2 %copy-start.6 = (f32[4,128,1024]{2,1,0:T(8,128)S(1)}, f32[4,128,1024]{2,1,0:T(8,128)}, u32[]{:S(2)}) copy-start(f32[4,128,1024]{2,1,0:T(8,128)} %get-tuple-element.40) | copy-start | bytes 6291460
  368.2 819.1 %copy-start.1 = (bf16[1024,1024]{1,0:T(8,128)(2,1)S(1)}, bf16[1024,1024]{1,0:T(8,128)(2,1)}, u32[]{:S(2)}) copy-start(bf16[1024,1024]{1,0:T(8,128)(2,1)} %param.22) | copy-start | bytes 6291460
  (27 other events, 51.1 us)
Sparse Core Ops, SparseCore 0:
  258.3 141.6 reduce-scatter.6
  402.8 136.8 reduce-scatter.8
  542.6 136.5 reduce-scatter.12
  682.0 136.7 reduce-scatter.10
  821.4 178.6 reduce-scatter.14
  1002.8 184.4 reduce-scatter.16
where the time goes:
time: 1200 us; the launch traced here: 1190 us
  waiting for transfers between devices  871 us (73%)
  matrix products  176 us (15%)
  blocking collectives  58.1 us (5%)
  local copies, waits for them, and re-layouts  45.6 us (4%)
  starting transfers between devices  22.1 us (2%)
  between operations  14.9 us (1%)
    reduce_scatter x1, waiting for transfers between devices, on_device(): lax.psum_scatter(terms[8], ('seq', 'dp'), scatter_dimension=1, tiled=True)  187 us
    reduce_scatter x1, waiting for transfers between devices, on_device(): lax.psum_scatter(terms[7], ('seq', 'dp'), scatter_dimension=1, tiled=True)  181 us
    reduce_scatter x1, waiting for transfers between devices, on_device(): lax.psum_scatter(terms[3], ('seq', 'dp'), scatter_dimension=1, tiled=True)  140 us
    reduce_scatter x1, waiting for transfers between devices, on_device(): lax.psum_scatter(terms[5], ('seq', 'dp'), scatter_dimension=1, tiled=True)  139 us
    reduce_scatter x1, waiting for transfers between devices, on_device(): lax.psum_scatter(terms[4], ('seq', 'dp'), scatter_dimension=1, tiled=True)  139 us
    dot_general x10, matrix products, first_dot(): lax.dot_general(left_side, right_side, (((0,), (0,)), ((), ())), preferre...  61 us
    unnamed x2, blocking collectives  58.1 us
    dot_general x9, matrix products, plain_dot(): return jnp.dot(left_side, right_side, preferred_element_type=jnp.float32)  39.2 us
  transfers between devices with their start and end apart: 10, of which 10 were waited for; matrix products, arithmetic and copies ran while one was open for 8% of the time, Pallas kernels for 0%

commit v1 on v0

v1 whole, which is shorter than its diff:
```python
import functools

import jax
import jax.experimental.pallas as pl
import jax.experimental.pallas.tpu as pltpu
import jax.numpy as jnp
from jax import lax
from jax.sharding import PartitionSpec as P

H = 16
norm_eps = 1e-05
f32 = jnp.float32
bf16 = jnp.bfloat16
VMEM_BYTES = 58 * 1024 * 1024


def params(count=1):
    return pltpu.CompilerParams(
        dimension_semantics=("arbitrary",) * count, vmem_limit_bytes=VMEM_BYTES
    )


def cost(micros):
    return pl.CostEstimate(
        flops=int(micros * 1e9), bytes_accessed=int(micros * 3.5e6), transcendentals=0
    )


def call(kernel, arrays, waits=(), scalars=(), **rest):
    first = len(scalars) + len(arrays)

    def body(*refs):
        kernel(*refs[:first], *refs[first + len(waits) :])

    grid = pltpu.PrefetchScalarGridSpec(
        num_scalar_prefetch=len(scalars),
        grid=rest.pop("grid"),
        in_specs=list(rest.pop("in_specs")) + [pl.BlockSpec(memory_space=pl.ANY)] * len(waits),
        out_specs=rest.pop("out_specs"),
        scratch_shapes=rest.pop("scratch_shapes", ()),
    )
    return pl.pallas_call(body, grid_spec=grid, **rest)(*scalars, *arrays, *waits)


def whole(array):
    rank = len(array.shape)
    return pl.BlockSpec(array.shape, lambda *_: (0,) * rank, pipeline_mode=pl.Buffered(1))


def dot_nn(left, right):
    return lax.dot_general(left, right, (((1,), (0,)), ((), ())), preferred_element_type=f32)


def dot_nt(left, right):
    return lax.dot_general(left, right, (((1,), (1,)), ((), ())), preferred_element_type=f32)


def dot_tn(left, right):
    return lax.dot_general(left, right, (((0,), (0,)), ((), ())), preferred_element_type=f32)


def inv_rms(values):
    return lax.rsqrt(jnp.mean(values * values, axis=-1, keepdims=True) + norm_eps)


GROUP = 4


def stacked(rows, head):
    lane_head = lax.broadcasted_iota(jnp.int32, rows.shape, 1) // head
    zero = jnp.zeros_like(rows)
    return jnp.concatenate([jnp.where(lane_head == h, rows, zero) for h in range(GROUP)], axis=0)


def unstacked(rows, head):
    slots = rows.shape[0] // GROUP
    lane_head = lax.broadcasted_iota(jnp.int32, (slots, rows.shape[1]), 1) // head
    out = rows[:slots]
    for h in range(1, GROUP):
        out = jnp.where(lane_head == h, rows[h * slots : (h + 1) * slots], out)
    return out


def front_kernel(
    routed_ref, index_ref, tokens_ref, cotangent_ref, gain_one_ref, router_ref, gain_two_ref,
    query_hbm, key_hbm, value_hbm, out_hbm,
    chosen_ref, first_ref, query_ref, key_ref, value_ref, probs_ref, mix_ref, attn_ref,
    second_ref, pulled_ref, mlp_grad_ref, score_ref,
    query_w, key_w, value_w, out_w, sems,
):
    seq = pl.program_id(0)
    weights = ((query_hbm, query_w), (key_hbm, key_w), (value_hbm, value_w), (out_hbm, out_w))
    copies = [pltpu.make_async_copy(src, dst, sems.at[i]) for i, (src, dst) in enumerate(weights)]

    @pl.when(seq == 0)
    def _():
        for copy in copies:
            copy.start()

    slots, places = index_ref.shape[1], tokens_ref.shape[0]
    width = tokens_ref.shape[1]
    head = width // H
    routed = routed_ref[seq]
    slot_id = lax.broadcasted_iota(jnp.int32, (slots, places), 0)
    place_id = lax.broadcasted_iota(jnp.int32, (slots, places), 1)
    pick = ((index_ref[0] == place_id) & (slot_id < routed)).astype(bf16)
    chosen = dot_nn(pick, tokens_ref[...])
    pulled = dot_nn(pick, cotangent_ref[...])
    chosen_ref[...] = chosen.astype(bf16)
    pulled_ref[...] = pulled.astype(bf16)
    logit = jnp.sum(chosen * router_ref[...].astype(f32), axis=-1, keepdims=True)
    score = 1.0 / (1.0 + jnp.exp(-logit))
    score_ref[...] = jnp.broadcast_to(score, score_ref.shape)
    mlp_grad_ref[...] = (score * pulled).astype(bf16)
    first = (chosen * inv_rms(chosen) * gain_one_ref[...].astype(f32)).astype(bf16)
    first_ref[...] = first

    @pl.when(seq == 0)
    def _():
        for copy in copies:
            copy.wait()

    query_ref[...] = (dot_nn(first, query_w[...]) * 0.125).astype(bf16)
    key_ref[...] = dot_nn(first, key_w[...]).astype(bf16)
    value_ref[...] = dot_nn(first, value_w[...]).astype(bf16)
    rows = GROUP * slots
    row_id = lax.broadcasted_iota(jnp.int32, (rows, slots), 0) % slots
    col_id = lax.broadcasted_iota(jnp.int32, (rows, slots), 1)
    allowed = (col_id <= row_id) & (col_id < routed)
    for g in range(H // GROUP):
        lanes = pl.ds(g * GROUP * head, GROUP * head)
        scores = dot_nt(stacked(query_ref[:, lanes], head), key_ref[:, lanes])
        scores = jnp.where(allowed, scores, -1e30)
        exped = jnp.exp(scores - jnp.max(scores, axis=-1, keepdims=True))
        probs = exped / jnp.sum(exped, axis=-1, keepdims=True)
        probs_ref[0, g] = probs
        mixed = dot_nn(probs.astype(bf16), value_ref[:, lanes])
        mix_ref[:, lanes] = unstacked(mixed, head).astype(bf16)
    attn = dot_nn(mix_ref[...], out_w[...])
    attn_ref[...] = attn
    after = chosen + attn
    second_ref[...] = (after * inv_rms(after) * gain_two_ref[...].astype(f32)).astype(bf16)


def front(routed, index, tokens, cotangent, gain_one, router, gain_two, wq, wk, wv, wo, waits=()):
    seqs, slots = index.shape
    places, width = tokens.shape[0] // seqs, tokens.shape[1]
    rows = seqs * slots
    by_seq = lambda shape: pl.BlockSpec(shape, lambda i, *_: (i, 0))
    vec = pl.BlockSpec((1, width), lambda i, *_: (0, 0))
    hbm = pl.BlockSpec(memory_space=pl.ANY)
    low = jax.ShapeDtypeStruct((rows, width), bf16)
    row_spec = by_seq((slots, width))
    return call(
        front_kernel,
        [index[:, :, None], tokens, cotangent, gain_one[None], router[None], gain_two[None], wq, wk, wv, wo],
        waits,
        [routed],
        grid=(seqs,),
        in_specs=[
            pl.BlockSpec((1, slots, 1), lambda i, *_: (i, 0, 0)),
            by_seq((places, width)),
            by_seq((places, width)),
            vec, vec, vec, hbm, hbm, hbm, hbm,
        ],
        out_specs=[row_spec] * 5
        + [
            pl.BlockSpec((1, H // GROUP, GROUP * slots, slots), lambda i, *_: (i, 0, 0, 0)),
            row_spec, row_spec, row_spec, row_spec, row_spec,
            by_seq((slots, 128)),
        ],
        scratch_shapes=[pltpu.VMEM((width, width), bf16)] * 4 + [pltpu.SemaphoreType.DMA((4,))],
        out_shape=[low] * 5
        + [
            jax.ShapeDtypeStruct((seqs, H // GROUP, GROUP * slots, slots), f32),
            low, jax.ShapeDtypeStruct((rows, width), f32), low, low, low,
            jax.ShapeDtypeStruct((rows, 128), f32),
        ],
        compiler_params=params(),
        name="front",
        cost_estimate=cost(20),
    )


def gelu_both(z):
    x = jnp.abs(z) * 0.7071067811865476
    t = 1.0 / (1.0 + 0.3275911 * x)
    bell = jnp.exp(-0.5 * z * z)
    poly = t * (
        0.254829592
        + t * (-0.284496736 + t * (1.421413741 + t * (-1.453152027 + t * 1.061405429)))
    )
    tail = 0.5 * poly * bell
    cdf = jnp.where(z < 0, tail, 1.0 - tail)
    return z * cdf, cdf + z * bell * 0.3989422804014327


def turn(rel, flat):
    bits = flat.bit_length() - 1
    half = bits // 2
    return rel // (1 << half) + rel % (1 << half) * (1 << (bits - half))


def place_blocks(me_ref, source, put_send, put_keep, size, nodes):
    core, node = me_ref[0], me_ref[1]
    flat = nodes // 4
    for rel in range(flat):
        for z in range(4):
            owner = lax.bitwise_xor(node, turn(z, 4) * flat + rel) * 2
            for put, side in ((put_keep, core), (put_send, 1 - core)):
                start = pl.multiple_of((owner + side) * size, size)
                put(rel, z, source[pl.ds(start, size), :].astype(bf16))


def up_kernel(
    me_ref, second_ref, mlp_grad_ref, up_ref, down_ref, act_ref, pre_ref, send_ref, keep_ref,
    turned_ref, terms_ref, *, nodes, blocks,
):
    @pl.when(pl.program_id(0) == 0)
    def _():
        turned_ref[...] = mlp_grad_ref[...].T

    hidden = dot_nn(second_ref[...], up_ref[...])
    act, slope = gelu_both(hidden)
    act = act.astype(bf16)
    act_ref[...] = act
    pre_ref[...] = (dot_nt(mlp_grad_ref[...], down_ref[...]) * slope).astype(bf16)
    terms_ref[...] = dot_nn(turned_ref[...], act)
    first_part = pl.program_id(0) < blocks // 2

    def put(ref):
        def store(rel, z, values):
            ref[0, jnp.where(first_part, turn(rel, nodes // 4), rel) * 4 + z] = values

        return store

    place_blocks(me_ref, terms_ref, put(send_ref), put(keep_ref), send_ref.shape[2], nodes)


def up_all(me, second, mlp_grad, w_up, w_down, nodes, block=512, waits=()):
    rows, width = second.shape
    hidden = w_up.shape[1]
    blocks = hidden // block
    half = blocks // 2
    size = width // (2 * nodes)
    held = whole(second)
    term_spec = pl.BlockSpec((1, nodes, size, block), lambda i, *_: (i // half, 0, 0, i % half))
    return call(
        functools.partial(up_kernel, nodes=nodes, blocks=blocks),
        [second, mlp_grad, w_up, w_down],
        waits,
        [me],
        grid=(blocks,),
        in_specs=[
            held,
            held,
            pl.BlockSpec((width, block), lambda i, *_: (0, i)),
            pl.BlockSpec((block, width), lambda i, *_: (i, 0)),
        ],
        out_specs=[pl.BlockSpec((rows, block), lambda i, *_: (0, i))] * 2 + [term_spec] * 2,
        scratch_shapes=[pltpu.VMEM((width, rows), bf16), pltpu.VMEM((width, block), f32)],
        out_shape=[jax.ShapeDtypeStruct((rows, hidden), bf16)] * 2
        + [jax.ShapeDtypeStruct((2, nodes, size, hidden // 2), bf16)] * 2,
        compiler_params=params(),
        name="up_all",
        cost_estimate=cost(22),
    )


def up_grad_kernel(me_ref, pre_ref, second_ref, send_ref, keep_ref):
    core = me_ref[0]
    size = keep_ref.shape[2]
    terms = dot_tn(pre_ref[...], second_ref[...])
    low, high = terms[:size].astype(bf16), terms[size:].astype(bf16)
    keep_ref[0, 0] = jnp.where(core == 0, low, high)
    send_ref[0, 0] = jnp.where(core == 0, high, low)


def up_grad(me, pre, second, nodes, waits=()):
    rows, hidden = pre.shape
    width = second.shape[1]
    size = hidden // (2 * nodes)
    flat = nodes // 4
    if 2 * size % 128:
        return plain_order(me, dot_tn(pre, second).astype(bf16).reshape(nodes, 2, size, width))

    def source(part, spot, me):
        xy = jnp.where(part == 0, turn(spot // 4, flat), spot // 4)
        return (0, lax.bitwise_xor(turn(spot % 4, 4) * flat + xy, me[1]))

    out = pl.BlockSpec((1, 1, size, width // 2), lambda part, spot, me: (part, spot, 0, 0))
    shape = jax.ShapeDtypeStruct((2, nodes, size, width // 2), bf16)
    return call(
        up_grad_kernel,
        [pre, second],
        waits,
        [me],
        grid=(2, nodes),
        in_specs=[
            pl.BlockSpec((rows, 2 * size), source),
            pl.BlockSpec((rows, width // 2), lambda part, spot, me: (0, part)),
        ],
        out_specs=[out, out],
        out_shape=[shape, shape],
        compiler_params=params(2),
        name="up_grad",
        cost_estimate=cost(12),
    )


def plain_order(me, terms):
    nodes = terms.shape[0]
    half = terms.shape[-1] // 2
    flat = nodes // 4
    spots = jnp.arange(nodes)
    rel_a, rel_b = turn(spots // 4, flat), spots // 4
    sides = []
    for side in (1 - me[0], me[0]):
        held = lax.dynamic_index_in_dim(terms, side, 1, keepdims=False)
        from_node = lambda rel: (turn(spots % 4, 4) * flat + rel) ^ me[1]
        sides.append(
            jnp.stack(
                [
                    jnp.take(held[..., :half], from_node(rel_a), axis=0),
                    jnp.take(held[..., half:], from_node(rel_b), axis=0),
                ]
            )
        )
    return sides


def back_kernel(
    chosen_ref, attn_ref, score_ref, pulled_ref, second_grad_ref, gain_ref, query_ref, key_ref,
    value_ref, probs_ref, out_ref,
    query_grad_ref, key_grad_ref, value_grad_ref, attn_grad_ref, after_grad_ref, gain_grad_ref,
):
    slots, width = chosen_ref.shape
    head = width // H
    after = chosen_ref[...].astype(f32) + attn_ref[...]
    inv = inv_rms(after)
    normed = after * inv
    arrived = second_grad_ref[...].astype(f32)
    gain_sum = jnp.sum((arrived * normed).reshape(slots // 8, 8, width), axis=0)

    @pl.when(pl.program_id(0) == 0)
    def _():
        gain_grad_ref[...] = gain_sum

    @pl.when(pl.program_id(0) > 0)
    def _():
        gain_grad_ref[...] += gain_sum

    weighted = arrived * gain_ref[...].astype(f32)
    after_grad = inv * (weighted - normed * jnp.mean(weighted * normed, axis=-1, keepdims=True))
    after_grad_ref[...] = after_grad
    delta = score_ref[:, :1] * pulled_ref[...].astype(f32)
    attn_grad = (delta + after_grad).astype(bf16)
    attn_grad_ref[...] = attn_grad
    mix_grad = dot_nt(attn_grad, out_ref[...]).astype(bf16)
    for g in range(H // GROUP):
        lanes = slice(g * GROUP * head, (g + 1) * GROUP * head)
        probs = probs_ref[0, g]
        keys, values = key_ref[:, lanes], value_ref[:, lanes]
        queries = stacked(query_ref[:, lanes], head)
        grads = stacked(mix_grad[:, lanes], head)
        prob_grad = dot_nt(grads, values)
        total = jnp.sum(prob_grad * probs, axis=-1, keepdims=True)
        score_grad = (probs * (prob_grad - total)).astype(bf16)
        value_grad_ref[:, lanes] = dot_tn(probs.astype(bf16), grads).astype(bf16)
        key_grad_ref[:, lanes] = dot_tn(score_grad, queries).astype(bf16)
        query_grad_ref[:, lanes] = unstacked(dot_nn(score_grad, keys), head).astype(bf16)


def back(chosen, attn, score, pulled, second_grad, gain, queries, keys, values, probs, w_out, waits=()):
    rows, width = chosen.shape
    seqs, groups, stack, slots = probs.shape
    row = pl.BlockSpec((slots, width), lambda i: (i, 0))
    low = jax.ShapeDtypeStruct((rows, width), bf16)
    return call(
        back_kernel,
        [chosen, attn, score, pulled, second_grad, gain[None], queries, keys, values, probs, w_out],
        waits,
        grid=(seqs,),
        in_specs=[
            row, row, pl.BlockSpec((slots, 128), lambda i: (i, 0)), row, row,
            pl.BlockSpec((1, width), lambda i: (0, 0)), row, row, row,
            pl.BlockSpec((1, groups, stack, slots), lambda i: (i, 0, 0, 0)), whole(w_out),
        ],
        out_specs=[row] * 5 + [pl.BlockSpec((8, width), lambda i: (0, 0))],
        out_shape=[low] * 4
        + [jax.ShapeDtypeStruct((rows, width), f32), jax.ShapeDtypeStruct((8, width), f32)],
        compiler_params=params(),
        name="back",
        cost_estimate=cost(14),
    )


def square_kernel(
    me_ref, query_ref, key_ref, value_ref, attn_ref, left_ref, right_ref, send_ref, keep_ref,
    terms_ref, *, nodes,
):
    half = send_ref.shape[4]
    for which, grads in enumerate((query_ref, key_ref, value_ref, attn_ref)):

        @pl.when(pl.program_id(0) == which)
        def _():
            rows = right_ref if which == 3 else left_ref
            terms = dot_tn(grads[...], rows[...])
            terms_ref[...] = terms * 0.125 if which == 0 else terms

    def put(ref):
        def store(rel, z, values):
            ref[0, turn(rel, nodes // 4) * 4 + z, 0] = values[:, :half]
            ref[1, rel * 4 + z, 0] = values[:, half:]

        return store

    place_blocks(me_ref, terms_ref, put(send_ref), put(keep_ref), send_ref.shape[3], nodes)


def square_grads(me, query_grad, key_grad, value_grad, attn_grad, first, mix, nodes, waits=()):
    rows, width = first.shape
    size = width // (2 * nodes)
    out = pl.BlockSpec((2, nodes, 1, size, width // 2), lambda i, *_: (0, 0, i, 0, 0))
    shape = jax.ShapeDtypeStruct((2, nodes, 4, size, width // 2), bf16)
    return call(
        functools.partial(square_kernel, nodes=nodes),
        [query_grad, key_grad, value_grad, attn_grad, first, mix],
        waits,
        [me],
        grid=(4,),
        in_specs=[whole(first)] * 6,
        out_specs=[out, out],
        scratch_shapes=[pltpu.VMEM((width, width), f32)],
        out_shape=[shape, shape],
        compiler_params=params(),
        name="square_grads",
        cost_estimate=cost(10),
    )


def hidden_sum_kernel(rows_ref, weight_ref, out_ref, total_ref, *, turned):
    step = pl.program_id(0)
    term = (dot_nt if turned else dot_nn)(rows_ref[...], weight_ref[...])

    @pl.when(step == 0)
    def _():
        total_ref[...] = term

    @pl.when(step > 0)
    def _():
        total_ref[...] += term

    @pl.when(step == pl.num_programs(0) - 1)
    def _():
        out_ref[...] = total_ref[...].astype(bf16)


def hidden_sum(rows, weight, turned, block=1024, waits=()):
    count, hidden = rows.shape
    width = weight.shape[0] if turned else weight.shape[1]
    spec = (
        pl.BlockSpec((width, block), lambda i: (0, i))
        if turned
        else pl.BlockSpec((block, width), lambda i: (i, 0))
    )
    return call(
        functools.partial(hidden_sum_kernel, turned=turned),
        [rows, weight],
        waits,
        grid=(hidden // block,),
        in_specs=[pl.BlockSpec((count, block), lambda i: (0, i)), spec],
        out_specs=pl.BlockSpec((count, width), lambda i: (0, 0)),
        out_shape=jax.ShapeDtypeStruct((count, width), bf16),
        scratch_shapes=[pltpu.VMEM((count, width), f32)],
        compiler_params=params(),
        name="hidden_sum",
        cost_estimate=cost(9),
    )


def last_kernel(
    chosen_ref, attn_ref, mlp_ref, score_ref, pulled_ref, after_grad_ref, query_grad_ref,
    key_grad_ref, value_grad_ref, gain_ref, router_ref, query_w, key_w, value_w,
    weighted_ref, chosen_grad_ref, gain_grad_ref, router_grad_ref,
):
    rows, width = chosen_ref.shape
    chosen = chosen_ref[...].astype(f32)
    score = score_ref[:, :1]
    branch = attn_ref[...] + mlp_ref[...].astype(f32)
    weighted_ref[...] = score * branch
    pull = jnp.sum(pulled_ref[...].astype(f32) * branch, axis=-1, keepdims=True)
    logit_grad = pull * score * (1.0 - score)
    first_grad = dot_nt(query_grad_ref[...], query_w[...]) * 0.125
    first_grad += dot_nt(key_grad_ref[...], key_w[...])
    first_grad += dot_nt(value_grad_ref[...], value_w[...])
    inv = inv_rms(chosen)
    normed = chosen * inv
    weighted = first_grad * gain_ref[...].astype(f32)
    chosen_grad_ref[...] = (
        inv * (weighted - normed * jnp.mean(weighted * normed, axis=-1, keepdims=True))
        + after_grad_ref[...]
        + logit_grad * router_ref[...].astype(f32)
    )
    fold = lambda values: jnp.sum(values.reshape(rows // 8, 8, width), axis=0)
    gain_sum, router_sum = fold(first_grad * normed), fold(logit_grad * chosen)

    @pl.when(pl.program_id(0) == 0)
    def _():
        gain_grad_ref[...] = gain_sum
        router_grad_ref[...] = router_sum

    @pl.when(pl.program_id(0) > 0)
    def _():
        gain_grad_ref[...] += gain_sum
        router_grad_ref[...] += router_sum


def last(
    chosen, attn, mlp, score, pulled, after_grad, dq, dk, dv, gain, router, wq, wk, wv, block=256, waits=()):
    rows, width = chosen.shape
    row = pl.BlockSpec((block, width), lambda i: (i, 0))
    vec = pl.BlockSpec((1, width), lambda i: (0, 0))
    sums = pl.BlockSpec((8, width), lambda i: (0, 0))
    wide = jax.ShapeDtypeStruct((rows, width), f32)
    return call(
        last_kernel,
        [chosen, attn, mlp, score, pulled, after_grad, dq, dk, dv, gain[None], router[None], wq, wk, wv],
        waits,
        grid=(rows // block,),
        in_specs=[row] * 3
        + [pl.BlockSpec((block, 128), lambda i: (i, 0))]
        + [row] * 5
        + [vec, vec]
        + [whole(wq)] * 3,
        out_specs=[row, row, sums, sums],
        out_shape=[wide, wide] + [jax.ShapeDtypeStruct((8, width), f32)] * 2,
        compiler_params=params(),
        name="last",
        cost_estimate=cost(11),
    )


def split_terms(values):
    high = values.astype(bf16)
    rest = values - high.astype(f32)
    middle = rest.astype(bf16)
    return jnp.concatenate([high, middle, (rest - middle.astype(f32)).astype(bf16)], axis=0)


def spread_kernel(routed_ref, index_ref, base_ref, delta_ref, out_ref, terms_ref):
    @pl.when(pl.program_id(1) == 0)
    def _():
        terms_ref[...] = split_terms(delta_ref[...])

    places, slots = base_ref.shape[0], delta_ref.shape[0]
    place = pl.program_id(1) * places + lax.broadcasted_iota(jnp.int32, (places, slots), 0)
    slot_id = lax.broadcasted_iota(jnp.int32, (places, slots), 1)
    live = slot_id < routed_ref[pl.program_id(0)]
    pick = ((index_ref[0] == place) & live).astype(bf16)
    pick = jnp.concatenate([pick] * 3, axis=1)
    added = dot_nn(pick, terms_ref[...])
    out_ref[...] = (base_ref[...].astype(f32) + added).astype(out_ref.dtype)


def spread(routed, index, base, delta, dtype, cuts=2, waits=()):
    seqs, slots = index.shape
    rows, width = base.shape
    block = rows // seqs // cuts
    big = pl.BlockSpec((block, width), lambda i, j, *_: (i * cuts + j, 0))
    return call(
        spread_kernel,
        [index[:, None, :], base, delta],
        waits,
        [routed],
        grid=(seqs, cuts),
        in_specs=[
            pl.BlockSpec((1, 1, slots), lambda i, j, *_: (i, 0, 0)),
            big,
            pl.BlockSpec((slots, width), lambda i, j, *_: (i, 0)),
        ],
        out_specs=big,
        scratch_shapes=[pltpu.VMEM((3 * slots, width), bf16)],
        out_shape=jax.ShapeDtypeStruct((rows, width), dtype),
        compiler_params=params(2),
        name="spread",
        cost_estimate=cost(13),
    )


def add_low(left, right):
    return (left.astype(f32) + right.astype(f32)).astype(bf16)


def swap_nodes(values, bit, nodes):
    return lax.ppermute(values, "seq", [(i, i ^ (1 << bit)) for i in range(nodes)])


def swap_cores(values):
    return lax.ppermute(values, "dp", [(0, 1), (1, 0)])


def halved(kept, got):
    count = kept.shape[0] // 2
    return add_low(kept[count:], got[count:]), add_low(kept[:count], got[:count])


class Chain:
    def __init__(self, send, keep, nodes):
        self.nodes, self.keep = nodes, keep
        self.bits = (nodes // 4).bit_length() - 1
        self.got = swap_cores(send)

    def swap(self):
        for part in range(2):
            top = self.bits - 1 - self.step
            bit = (top + self.bits // 2) % self.bits if part == 0 else top
            self.got[part] = swap_nodes(self.gone[part], bit, self.nodes)
        return list(self.gone)

    def first(self):
        pairs = [halved(self.keep[part], self.got[part]) for part in range(2)]
        self.gone, self.kept = [p[0] for p in pairs], [p[1] for p in pairs]
        self.got, self.step = [None, None], 0
        return self.swap()

    def second(self):
        sent = []
        while self.step < self.bits - 1:
            pairs = [halved(self.kept[part], self.got[part]) for part in range(2)]
            self.gone, self.kept = [p[0] for p in pairs], [p[1] for p in pairs]
            self.step += 1
            sent = self.swap()
        return sent

    def third(self):
        pairs = [halved(self.kept[part], self.got[part]) for part in range(2)]
        gone = jnp.stack([p[0] for p in pairs], axis=1)
        self.kept = [p[1] for p in pairs]
        self.got = swap_nodes(gone, self.bits, self.nodes)
        return [gone]

    def fourth(self):
        pairs = [halved(self.kept[part], self.got[:, part]) for part in range(2)]
        gone = jnp.stack([p[0] for p in pairs], axis=1)
        self.kept = [p[1] for p in pairs]
        self.got = swap_nodes(gone, self.bits + 1, self.nodes)
        return [gone]

    def sums(self):
        return [
            self.kept[part][0].astype(f32) + self.got[0, part].astype(f32) for part in range(2)
        ]


def on_device(
    tokens,
    lengths,
    routed_index,
    out_grad,
    gain_attn,
    w_router,
    w_query,
    w_key,
    w_value,
    w_out,
    gain_mlp,
    w_up,
    w_down,
):
    nodes = lax.axis_size("seq")
    width = tokens.shape[2]
    me = jnp.stack([lax.axis_index("dp"), lax.axis_index("seq")]).astype(jnp.int32)
    routed = lengths[0] // 8
    index = routed_index[0]
    inputs, cotangent = tokens[0], out_grad[0]
    (
        chosen, first_in, queries, keys, values, probs, mix, attn_out, second_in, pulled, mlp_grad, score,
    ) = front(
        routed, index, inputs, cotangent, gain_attn, w_router, gain_mlp, w_query, w_key, w_value, w_out
    )
    hidden_act, pre_grad, down_send, down_keep = up_all(
        me, second_in, mlp_grad, w_up, w_down, nodes
    )
    down = Chain(down_send, down_keep, nodes)
    second_grad = hidden_sum(pre_grad, w_up, True)
    query_grad, key_grad, value_grad, attn_grad, after_grad, gain_mlp_sum = back(
        chosen, attn_out, score, pulled, second_grad, gain_mlp, queries, keys, values, probs, w_out,
        waits=down.first(),
    )
    square_send, square_keep = square_grads(
        me, query_grad, key_grad, value_grad, attn_grad, first_in, mix, nodes
    )
    flatten = lambda terms: terms.reshape(2, nodes, -1, width // 2)
    square = Chain(flatten(square_send), flatten(square_keep), nodes)
    up_send, up_keep = up_grad(me, pre_grad, second_in, nodes, waits=down.second())
    up = Chain(up_send, up_keep, nodes)
    mlp_out = hidden_sum(hidden_act, w_down, False, waits=down.third() + square.first())
    weighted, chosen_grad, gain_attn_sum, router_sum = last(
        chosen, attn_out, mlp_out, score, pulled, after_grad, query_grad, key_grad, value_grad,
        gain_attn, w_router, w_query, w_key, w_value, waits=down.fourth() + up.first(),
    )
    vectors = jnp.sum(jnp.stack([gain_attn_sum, router_sum, gain_mlp_sum]), axis=1)
    vectors = vectors.reshape(3, 2 * nodes, -1).transpose(1, 0, 2)
    vectors = lax.all_to_all(vectors, ("seq", "dp"), 0, 0, tiled=True)
    mixed_out = spread(routed, index, inputs, weighted, bf16, waits=square.second())
    token_grad = spread(
        routed, index, cotangent, chosen_grad, f32, waits=square.third() + up.second()
    )
    square.fourth()
    up.third()
    up.fourth()
    vectors = jnp.sum(vectors, axis=0)
    down_sum, up_sum = down.sums(), up.sums()
    square_sum = [part.reshape(4, -1, width // 2) for part in square.sums()]
    turned = lambda parts: jnp.concatenate([part.T for part in parts], axis=0)
    return (
        mixed_out[None],
        token_grad[None],
        vectors[0],
        vectors[1],
        turned([part[0] for part in square_sum]),
        turned([part[1] for part in square_sum]),
        turned([part[2] for part in square_sum]),
        turned([part[3] for part in square_sum]),
        vectors[2],
        turned(up_sum),
        turned(down_sum),
    )


def solution(mesh):
    in_specs = (
        P("dp", "seq", None),
        P("dp", "seq"),
        P("dp", "seq", None),
        P("dp", "seq", None),
        P(),
        P(),
        P(),
        P(),
        P(),
        P(),
        P(),
        P(),
        P(),
    )
    out_specs = (
        P("dp", "seq", None),
        P("dp", "seq", None),
        P(("seq", "dp")),
        P(("seq", "dp")),
        P(None, ("seq", "dp")),
        P(None, ("seq", "dp")),
        P(None, ("seq", "dp")),
        P(None, ("seq", "dp")),
        P(("seq", "dp")),
        P(None, ("seq", "dp")),
        P(None, ("seq", "dp")),
    )
    return jax.shard_map(
        on_device, mesh=mesh, in_specs=in_specs, out_specs=out_specs, check_vma=False
    )
```

time: 1200 us -> 288 us (0.24)
  waiting for transfers between devices: 871 us -> 58.9 us
  matrix products: 176 us -> 0 us
  Pallas kernels: 0 us -> 156 us
  blocking collectives: 58.1 us -> 0 us
  local copies, waits for them, and re-layouts: 45.6 us -> 10.3 us
  other arithmetic: 6.91 us -> 30.2 us
  between operations: 14.9 us -> 1.06 us
    reduce_scatter x6 -> x0, waiting for transfers between devices: 805 us -> none  [the longest x1 187 us: on_device(): lax.psum_scatter(terms[8], ('seq', 'dp'), scatter_dimension=1, tiled=True)]
    dot_general x35 -> x0, matrix products: 170 us -> none  [the longest x10 61 us: first_dot(): lax.dot_general(left_side, right_side, (((0,), (0,)), ((), ())), preferre...]
    pallas_call x0 -> x10, Pallas kernels: none -> 156 us  [call(): pl.pallas_call(body, grid_spec=grid, **rest)(*scalars, *arrays, *waits)]
    all_to_all x4 -> x1, waiting for transfers between devices: 66 us -> 0.16 us  [on_device(): vectors = lax.all_to_all(vectors, ('seq', 'dp'), 0, 0, tiled=True)]
    ppermute x0 -> x21, waiting for transfers between devices: none -> 58.7 us  [the longest x18 58.7 us: swap_nodes(): lax.ppermute(values, 'seq', [(i, i ^ 1 << bit) for i in range(nodes)])]
    unnamed x2 -> x0, blocking collectives: 58.1 us -> none
    reshape x8 -> x1, local copies, waits for them, and re-layouts: 28.1 us -> 0.09 us  [on_device(): vectors = vectors.reshape(3, 2 * nodes, -1).transpose(1, 0, 2)]
    ppermute x0 -> x21, starting transfers between devices: none -> 26.2 us  [the longest x18 25.7 us: swap_nodes(): lax.ppermute(values, 'seq', [(i, i ^ 1 << bit) for i in range(nodes)])]
  transfers between devices with their start and end apart: 10 -> 22, of which waited for: 10 -> 8; matrix products, arithmetic and copies ran while one was open for 8% -> 10% of each run, Pallas kernels for 0% -> 39%
where the time goes in v1:
time: 288 us; the launch traced here: 286 us
  Pallas kernels  156 us (54%)
  waiting for transfers between devices  58.9 us (20%)
  other arithmetic  30.2 us (10%)
  starting transfers between devices  29.8 us (10%)
  local copies, waits for them, and re-layouts  10.3 us (4%)
    pallas_call x10, Pallas kernels, call(): pl.pallas_call(body, grid_spec=grid, **rest)(*scalars, *arrays, *waits)  156 us
    ppermute x18, waiting for transfers between devices, swap_nodes(): lax.ppermute(values, 'seq', [(i, i ^ 1 << bit) for i in range(nodes)])  58.7 us
    ppermute x18, starting transfers between devices, swap_nodes(): lax.ppermute(values, 'seq', [(i, i ^ 1 << bit) for i in range(nodes)])  25.7 us
    convert_element_type x15, other arithmetic, add_low(): return (left.astype(f32) + right.astype(f32)).astype(bf16)  23.3 us
  transfers between devices with their start and end apart: 22, of which 8 were waited for; matrix products, arithmetic and copies ran while one was open for 10% of the time, Pallas kernels for 39%

profile of v1, /device:TPU:0, one launch (start us, length us, event | category | flops | bytes accessed | tf_op | source)
XLA Modules:
  0.0 286.2 jit_solution(12904604717068494983)
XLA Ops:
  7.8 21.6 %front.1 = (bf16[512,1024]{1,0:T(8,128)(2,1)}, bf16[512,1024]{1,0:T(8,128)(2,1)}, bf16[512,1024]{1,0:T(8,128)(2,1)}, bf16[512,1024]{1,0:T(8,128)(2,1)}, bf16[512...) custom-call(s32[4]{0:T(128)} %and_select_fusion.refs_0_, ...), custom_call_target="tpu_custom_call" | custom-call | flops 20000000000 | bytes 70000000 | tf_op jit(solution)/shard_map/front/pallas_call | solution.py:42
  29.5 23.8 %up_all.1 = (bf16[512,4096]{1,0:T(8,128)(2,1)}, bf16[512,4096]{1,0:T(8,128)(2,1)}, bf16[2,16,32,2048]{3,2,1,0:T(8,128)(2,1)}, bf16[2,16,32,2048]{3,2,1,0:T(8,128)(2,1)}) custom-call(s32[2]{0:T(128)} %pad_add_fusion.refs_0_, bf16[512,1024]{1,0:T(8,128)(2,1)} %get-tuple-element.43.refs_1_.refs_2_, bf16[512,1024]{1,0:T(8,128)(2,1)} %get-tuple-element.44.refs_2_, ...), custom_call_target="tpu_custom_call" | custom-call | flops 22000001024 | bytes 77000000 | tf_op jit(solution)/shard_map/up_all/pallas_call | solution.py:42
  53.8 9.6 %hidden_sum.2.refs_4_ = bf16[512,1024]{1,0:T(8,128)(2,1)} custom-call(bf16[512,4096]{1,0:T(8,128)(2,1)} %get-tuple-element.50.refs_0_.refs_1_, bf16[1024,4096]{1,0:T(8,128)(2,1)} %refs_1_.2), custom_call_target="tpu_custom_call" | custom-call | flops 8999999488 | bytes 31500000 | tf_op jit(solution)/shard_map/hidden_sum/pallas_call | solution.py:42
  63.3 4.1 %add_convert_fusion.7 = (bf16[1,8,32,2048]{3,2,1,0:T(8,128)(2,1)S(1)}, bf16[8,32,2048]{2,1,0:T(8,128)(2,1)}, bf16[1,8,32,2048]{3,2,1,0:T(8,128)(2,1)}, bf16[8,32,2048]{2,1,0:T(8,128)(2,1)}) fusion(bf16[2,16,32,2048]{3,2,1,0:T(8,128)(2,1)} %collective-permute-done, bf16[2,16,32,2048]{3,2,1,0:T(8,128)(2,1)S(1)} %copy-done.1), kind=kLoop, calls=%fused_computation.15 | loop fusion | flops 8388608 | bytes 12582912 | tf_op jit(solution)/shard_map/convert_element_type | solution.py:592
  67.4 2.5 collective-permute-start.3
  71.4 14.9 %back.1 = (bf16[512,1024]{1,0:T(8,128)(2,1)}, bf16[512,1024]{1,0:T(8,128)(2,1)}, bf16[512,1024]{1,0:T(8,128)(2,1)}, bf16[512,1024]{1,0:T(8,128)(2,1)}, f32[512,1024]{1,0:T(8,128)}, /*index=5*/f32[8,1024]{1,0:T(8,128)}) custom-call(bf16[512,1024]{1,0:T(8,128)(2,1)} %get-tuple-element.41.refs_0_, f32[512,1024]{1,0:T(8,128)} %get-tuple-element.42.refs_1_, ...), custom_call_target="tpu_custom_call" | custom-call | flops 14000000000 | bytes 49000000 | tf_op jit(solution)/shard_map/back/pallas_call | solution.py:42
  86.4 7.6 %collective-permute-done.3 = bf16[8,32,2048]{2,1,0:T(8,128)(2,1)S(1)} collective-permute-done((bf16[8,32,2048]{2,1,0:T(8,128)(2,1)}, bf16[8,32,2048]{2,1,0:T(8,128)(2,1)S(1)}, u32[]{:S(2)}, u32[]{:S(2)}) %collective-permute-start.3) | collective-permute-done | bytes 1048608 | tf_op jit(solution)/shard_map/ppermute | solution.py:596
  98.1 11.2 %square_grads.1 = (bf16[2,16,4,32,512]{4,3,2,1,0:T(8,128)(2,1)}, bf16[2,16,4,32,512]{4,3,2,1,0:T(8,128)(2,1)}) custom-call(s32[2]{0:T(128)} %pad_add_fusion.refs_0_, bf16[512,1024]{1,0:T(8,128)(2,1)} %get-tuple-element.55.refs_1_.refs_6_, bf16[512,1024]{1,0:T(8,128)(2,1)} %get-tuple-element.56.refs_2_.refs_7_, ...), custom_call_target="tpu_custom_call" | custom-call | flops 10000000000 | bytes 35000000 | tf_op jit(solution)/shard_map/square_grads/pallas_call | solution.py:42
  111.8 24.7 %up_grad.1 = (bf16[2,16,128,512]{3,2,1,0:T(8,128)(2,1)}, bf16[2,16,128,512]{3,2,1,0:T(8,128)(2,1)}) custom-call(s32[2]{0:T(128)} %pad_add_fusion.refs_0_, bf16[512,4096]{1,0:T(8,128)(2,1)} %get-tuple-element.50.refs_0_.refs_1_, bf16[512,1024]{1,0:T(8,128)(2,1)} %get-tuple-element.43.refs_1_.refs_2_, bf16[4,32,2048]{2,1,0:T(8,128)(2,1)} %copy-done.8, ...), custom_call_target="tpu_custom_call" | custom-call | flops 12000000000 | bytes 42000000 | tf_op jit(solution)/shard_map/up_grad/pallas_call | solution.py:42
  136.6 2.7 collective-permute-start.20
  139.3 2.5 fusion.50
  141.8 10.0 %collective-permute-done.20 = bf16[1,2,32,2048]{3,2,1,0:T(8,128)(2,1)S(1)} collective-permute-done((bf16[1,2,32,2048]{3,2,1,0:T(8,128)(2,1)S(1)}, bf16[1,2,32,2048]{3,2,1,0:T(8,128)(2,1)S(1)}, u32[]{:S(2)}, u32[]{:S(2)}) %collective-permute-start.20) | collective-permute-done | bytes 262176 | tf_op jit(solution)/shard_map/ppermute | solution.py:596
  151.9 4.9 %fusion = (bf16[8,128,512]{2,1,0:T(8,128)(2,1)}, bf16[8,128,512]{2,1,0:T(8,128)(2,1)S(1)}, bf16[8,128,512]{2,1,0:T(8,128)(2,1)}, bf16[8,128,512]{2,1,0:T(8,128)(2,1)}) fusion(bf16[8,128,512]{2,1,0:T(8,128)(2,1)S(1)} %bitcast.275, bf16[2,16,128,512]{3,2,1,0:T(8,128)(2,1)} %collective-permute-done.5, bf16[8,128,512]{2,1,0:T(8,128)(2,1)S(1)} %bitcast.276, ...), kind=kLoop, calls=%fused_computation.1 | loop fusion | flops 8388608 | bytes 12582912 | tf_op jit(solution)/shard_map/convert_element_type | solution.py:592
  159.7 9.3 %hidden_sum.3.refs_2_ = bf16[512,1024]{1,0:T(8,128)(2,1)} custom-call(bf16[512,4096]{1,0:T(8,128)(2,1)} %get-tuple-element.45.refs_0_, bf16[4096,1024]{1,0:T(8,128)(2,1)} %refs_1_.3, bf16[2,2,32,2048]{3,2,1,0:T(8,128)(2,1)} %copy-done.5, bf16[8,128,512]{2,1,0:T(8,128)(2,1)} %get-tuple-element.126.refs_3_, bf16[8,128,512]{2,1,0:T(8,128)(2,1)} %get-tuple-element.125.refs_4_), custom_call_target="tpu_custom_call" | custom-call | flops 8999999488 | bytes 31500000 | tf_op jit(solution)/shard_map/hidden_sum/pallas_call | solution.py:42
  169.0 13.2 %collective-permute-done.9 = bf16[8,128,512]{2,1,0:T(8,128)(2,1)} collective-permute-done((bf16[8,128,512]{2,1,0:T(8,128)(2,1)}, bf16[8,128,512]{2,1,0:T(8,128)(2,1)}, u32[]{:S(2)}, u32[]{:S(2)}) %collective-permute-start.9) | collective-permute-done | bytes 1048608 | tf_op jit(solution)/shard_map/ppermute | solution.py:596
  182.2 2.8 add_convert_fusion.8
  193.9 11.7 %last.1 = (f32[512,1024]{1,0:T(8,128)}, f32[512,1024]{1,0:T(8,128)}, f32[8,1024]{1,0:T(8,128)}, f32[8,1024]{1,0:T(8,128)}) custom-call(bf16[512,1024]{1,0:T(8,128)(2,1)} %get-tuple-element.41.refs_0_, f32[512,1024]{1,0:T(8,128)} %get-tuple-element.42.refs_1_, bf16[512,1024]{1,0:T(8,128)(2,1)} %hidden_sum.3.refs_2_, ...), custom_call_target="tpu_custom_call" | custom-call | flops 11000000512 | bytes 38500000 | tf_op jit(solution)/shard_map/last/pallas_call | solution.py:42
  207.2 3.5 %all-to-all-start = ((f32[32,3,32]{2,1,0:T(4,128)}), f32[32,3,32]{2,1,0:T(4,128)S(1)}, u32[]{:S(2)}, u32[]{:S(2)}) async-start(f32[32,3,32]{2,1,0:T(4,128)} %copy.49), calls=%async_computation | async-start | bytes 131072 | tf_op jit(solution)/shard_map/all_to_all | solution.py:705
  210.7 13.6 %spread.2 = bf16[4096,1024]{1,0:T(8,128)(2,1)} custom-call(s32[4]{0:T(128)} %and_select_fusion.refs_0_, s32[4,1,128]{2,1,0:T(1,128)} %bitcast.284, bf16[4096,1024]{1,0:T(8,128)(2,1)} %bitcast.287, f32[512,1024]{1,0:T(8,128)} %get-tuple-element.66.refs_3_, bf16[4,128,512]{2,1,0:T(8,128)(2,1)} %get-tuple-element.136.refs_4_, ...), custom_call_target="tpu_custom_call" | custom-call | flops 12999999488 | bytes 45500000 | tf_op jit(solution)/shard_map/spread/pallas_call | solution.py:42
  235.4 15.4 %spread.3 = f32[4096,1024]{1,0:T(8,128)} custom-call(s32[4]{0:T(128)} %and_select_fusion.refs_0_, s32[4,1,128]{2,1,0:T(1,128)} %bitcast.285, bf16[4096,1024]{1,0:T(8,128)(2,1)} %bitcast.289, f32[512,1024]{1,0:T(8,128)} %get-tuple-element.67.refs_3_, bf16[2,2,128,512]{3,2,1,0:T(8,128)(2,1)} %copy-done.6, bf16[4,128,512]{2,1,0:T(8,128)(2,1)} %copy-done.10, ...), custom_call_target="tpu_custom_call" | custom-call | flops 12999999488 | bytes 45500000 | tf_op jit(solution)/shard_map/spread/pallas_call | solution.py:42
  250.9 2.5 collective-permute-start.15
  254.4 10.7 %collective-permute-done.15 = bf16[1,2,128,512]{3,2,1,0:T(8,128)(2,1)S(1)} collective-permute-done((bf16[1,2,128,512]{3,2,1,0:T(8,128)(2,1)S(1)}, bf16[1,2,128,512]{3,2,1,0:T(8,128)(2,1)S(1)}, u32[]{:S(2)}, u32[]{:S(2)}) %collective-permute-start.15) | collective-permute-done | bytes 262176 | tf_op jit(solution)/shard_map/ppermute | solution.py:596
  266.0 6.3 %collective-permute-done.18 = bf16[2,2,128,512]{3,2,1,0:T(8,128)(2,1)S(1)} collective-permute-done((bf16[2,2,128,512]{3,2,1,0:T(8,128)(2,1)S(1)}, bf16[2,2,128,512]{3,2,1,0:T(8,128)(2,1)S(1)}, u32[]{:S(2)}, u32[]{:S(2)}) %collective-permute-start.18) | collective-permute-done | bytes 524320 | tf_op jit(solution)/shard_map/ppermute | solution.py:596
  274.5 10.5 %collective-permute-done.19 = bf16[1,2,128,512]{3,2,1,0:T(8,128)(2,1)S(1)} collective-permute-done((bf16[1,2,128,512]{3,2,1,0:T(8,128)(2,1)S(1)}, bf16[1,2,128,512]{3,2,1,0:T(8,128)(2,1)S(1)}, u32[]{:S(2)}, u32[]{:S(2)}) %collective-permute-start.19) | collective-permute-done | bytes 262176 | tf_op jit(solution)/shard_map/ppermute | solution.py:596
  (105 shorter events, 45.2 us)
Async XLA Ops:
  53.3 10.0 %collective-permute-start = (bf16[2,16,32,2048]{3,2,1,0:T(8,128)(2,1)}, bf16[2,16,32,2048]{3,2,1,0:T(8,128)(2,1)}, u32[]{:S(2)}, u32[]{:S(2)}) collective-permute-start(bf16[2,16,32,2048]{3,2,1,0:T(8,128)(2,1)} %get-tuple-element.47), channel_id=1, source_target_pairs={{0,1},{1,0},{2,3},{3,2},{4,5},{5,4},{6,7},{7,6},{8,9},{9,8},{10,11... | collective-permute-start | bytes 12582920 | tf_op jit(solution)/shard_map/ppermute | solution.py:600
  67.4 26.6 %collective-permute-start.3 = (bf16[8,32,2048]{2,1,0:T(8,128)(2,1)}, bf16[8,32,2048]{2,1,0:T(8,128)(2,1)S(1)}, u32[]{:S(2)}, u32[]{:S(2)}) collective-permute-start(bf16[8,32,2048]{2,1,0:T(8,128)(2,1)} %get-tuple-element.120.refs_12_), channel_id=1, source_target_pairs={{0,4},{2,6},{4,0},{6,2},{8,12},{10,14},{12,8},{14,10},{16,20},{18,... | collective-permute-start | bytes 3145736 | tf_op jit(solution)/shard_map/ppermute | solution.py:596
  69.9 26.2 %collective-permute-start.1 = (bf16[8,32,2048]{2,1,0:T(8,128)(2,1)}, bf16[8,32,2048]{2,1,0:T(8,128)(2,1)S(1)}, u32[]{:S(2)}, u32[]{:S(2)}) collective-permute-start(bf16[8,32,2048]{2,1,0:T(8,128)(2,1)} %get-tuple-element.122.refs_11_), channel_id=1, source_target_pairs={{0,2},{2,0},{4,6},{6,4},{8,10},{10,8},{12,14},{14,12},{16,18},{18,... | collective-permute-start | bytes 3145736 | tf_op jit(solution)/shard_map/ppermute | solution.py:596
  71.4 22.5 %copy-start.3 = (bf16[1,8,32,2048]{3,2,1,0:T(8,128)(2,1)S(1)}, bf16[1,8,32,2048]{3,2,1,0:T(8,128)(2,1)}, u32[]{:S(2)}) copy-start(bf16[1,8,32,2048]{3,2,1,0:T(8,128)(2,1)} %get-tuple-element.121) | copy-start | bytes 3145732
  94.4 15.1 %collective-permute-start.4 = (bf16[4,32,2048]{2,1,0:T(8,128)(2,1)S(1)}, bf16[4,32,2048]{2,1,0:T(8,128)(2,1)S(1)}, u32[]{:S(2)}, u32[]{:S(2)}) collective-permute-start(bf16[4,32,2048]{2,1,0:T(8,128)(2,1)S(1)} %get-tuple-element.142.refs_4_), channel_id=1, source_target_pairs={{0,2},{2,0},{4,6},{6,4},{8,10},{10,8},{12,14},{14,12},{16,18},{18,... | collective-permute-start | bytes 1572872 | tf_op jit(solution)/shard_map/ppermute | solution.py:596
  96.5 13.3 %collective-permute-start.2 = (bf16[4,32,2048]{2,1,0:T(8,128)(2,1)S(1)}, bf16[4,32,2048]{2,1,0:T(8,128)(2,1)S(1)}, u32[]{:S(2)}, u32[]{:S(2)}) collective-permute-start(bf16[4,32,2048]{2,1,0:T(8,128)(2,1)S(1)} %get-tuple-element.140.refs_3_), channel_id=1, source_target_pairs={{0,4},{2,6},{4,0},{6,2},{8,12},{10,14},{12,8},{14,10},{16,20},{18,... | collective-permute-start | bytes 1572872 | tf_op jit(solution)/shard_map/ppermute | solution.py:596
  109.3 42.5 %collective-permute-start.5 = (bf16[2,16,128,512]{3,2,1,0:T(8,128)(2,1)}, bf16[2,16,128,512]{3,2,1,0:T(8,128)(2,1)}, u32[]{:S(2)}, u32[]{:S(2)}) collective-permute-start(bf16[2,16,128,512]{3,2,1,0:T(8,128)(2,1)} %bitcast.290), channel_id=1, source_target_pairs={{0,1},{1,0},{2,3},{3,2},{4,5},{5,4},{6,7},{7,6},{8,9},{9,8},{10,11... | collective-permute-start | bytes 12582920 | tf_op jit(solution)/shard_map/ppermute | solution.py:600
  110.1 26.4 %copy-start.5 = (bf16[2,2,32,2048]{3,2,1,0:T(8,128)(2,1)}, bf16[2,2,32,2048]{3,2,1,0:T(8,128)(2,1)S(1)}, u32[]{:S(2)}) copy-start(bf16[2,2,32,2048]{3,2,1,0:T(8,128)(2,1)S(1)} %copy.45.refs_2_) | copy-start | bytes 1572868
  110.1 26.4 %collective-permute-start.6 = (bf16[2,2,32,2048]{3,2,1,0:T(8,128)(2,1)S(1)}, bf16[2,2,32,2048]{3,2,1,0:T(8,128)(2,1)S(1)}, u32[]{:S(2)}, u32[]{:S(2)}) collective-permute-start(bf16[2,2,32,2048]{3,2,1,0:T(8,128)(2,1)S(1)} %copy.45.refs_2_), channel_id=1, source_target_pairs={{0,8},{2,10},{4,12},{6,14},{8,0},{10,2},{12,4},{14,6},{16,24},{18,... | collective-permute-start | bytes 1572872 | tf_op jit(solution)/shard_map/ppermute | solution.py:596
  136.5 53.1 %collective-permute-start.7 = (bf16[2,16,128,512]{3,2,1,0:T(8,128)(2,1)}, bf16[2,16,128,512]{3,2,1,0:T(8,128)(2,1)S(1)}, u32[]{:S(2)}, u32[]{:S(2)}) collective-permute-start(bf16[2,16,128,512]{3,2,1,0:T(8,128)(2,1)} %get-tuple-element.65), channel_id=1, source_target_pairs={{0,1},{1,0},{2,3},{3,2},{4,5},{5,4},{6,7},{7,6},{8,9},{9,8},{10,11... | collective-permute-start | bytes 12582920 | tf_op jit(solution)/shard_map/ppermute | solution.py:600
  136.6 15.2 %collective-permute-start.20 = (bf16[1,2,32,2048]{3,2,1,0:T(8,128)(2,1)S(1)}, bf16[1,2,32,2048]{3,2,1,0:T(8,128)(2,1)S(1)}, u32[]{:S(2)}, u32[]{:S(2)}) collective-permute-start(bf16[1,2,32,2048]{3,2,1,0:T(8,128)(2,1)S(1)} %pad_maximum_fusion.5.refs_14_), channel_id=1, source_target_pairs={{0,16},{2,18},{4,20},{6,22},{8,24},{10,26},{12,28},{14,30},{16,0},... | collective-permute-start | bytes 786440 | tf_op jit(solution)/shard_map/ppermute | solution.py:596
  156.8 25.5 %collective-permute-start.9 = (bf16[8,128,512]{2,1,0:T(8,128)(2,1)}, bf16[8,128,512]{2,1,0:T(8,128)(2,1)}, u32[]{:S(2)}, u32[]{:S(2)}) collective-permute-start(bf16[8,128,512]{2,1,0:T(8,128)(2,1)} %get-tuple-element.125.refs_4_), channel_id=1, source_target_pairs={{0,4},{2,6},{4,0},{6,2},{8,12},{10,14},{12,8},{14,10},{16,20},{18,... | collective-permute-start | bytes 3145736 | tf_op jit(solution)/shard_map/ppermute | solution.py:596
  159.1 26.6 %collective-permute-start.8 = (bf16[8,128,512]{2,1,0:T(8,128)(2,1)}, bf16[8,128,512]{2,1,0:T(8,128)(2,1)}, u32[]{:S(2)}, u32[]{:S(2)}) collective-permute-start(bf16[8,128,512]{2,1,0:T(8,128)(2,1)} %get-tuple-element.126.refs_3_), channel_id=1, source_target_pairs={{0,2},{2,0},{4,6},{6,4},{8,10},{10,8},{12,14},{14,12},{16,18},{18,... | collective-permute-start | bytes 3145736 | tf_op jit(solution)/shard_map/ppermute | solution.py:596
  185.0 40.0 %collective-permute-start.11 = (bf16[4,128,512]{2,1,0:T(8,128)(2,1)}, bf16[4,128,512]{2,1,0:T(8,128)(2,1)}, u32[]{:S(2)}, u32[]{:S(2)}) collective-permute-start(bf16[4,128,512]{2,1,0:T(8,128)(2,1)} %get-tuple-element.138.refs_5_), channel_id=1, source_target_pairs={{0,2},{2,0},{4,6},{6,4},{8,10},{10,8},{12,14},{14,12},{16,18},{18,... | collective-permute-start | bytes 1572872 | tf_op jit(solution)/shard_map/ppermute | solution.py:596
  188.3 38.1 %collective-permute-start.10 = (bf16[4,128,512]{2,1,0:T(8,128)(2,1)}, bf16[4,128,512]{2,1,0:T(8,128)(2,1)}, u32[]{:S(2)}, u32[]{:S(2)}) collective-permute-start(bf16[4,128,512]{2,1,0:T(8,128)(2,1)} %get-tuple-element.136.refs_4_), channel_id=1, source_target_pairs={{0,4},{2,6},{4,0},{6,2},{8,12},{10,14},{12,8},{14,10},{16,20},{18,... | collective-permute-start | bytes 1572872 | tf_op jit(solution)/shard_map/ppermute | solution.py:596
  191.9 40.5 %collective-permute-start.12 = (bf16[8,128,512]{2,1,0:T(8,128)(2,1)}, bf16[8,128,512]{2,1,0:T(8,128)(2,1)}, u32[]{:S(2)}, u32[]{:S(2)}) collective-permute-start(bf16[8,128,512]{2,1,0:T(8,128)(2,1)} %get-tuple-element.118.refs_15_), channel_id=1, source_target_pairs={{0,2},{2,0},{4,6},{6,4},{8,10},{10,8},{12,14},{14,12},{16,18},{18,... | collective-permute-start | bytes 3145736 | tf_op jit(solution)/shard_map/ppermute | solution.py:596
  193.4 35.9 %collective-permute-start.13 = (bf16[8,128,512]{2,1,0:T(8,128)(2,1)}, bf16[8,128,512]{2,1,0:T(8,128)(2,1)}, u32[]{:S(2)}, u32[]{:S(2)}) collective-permute-start(bf16[8,128,512]{2,1,0:T(8,128)(2,1)} %get-tuple-element.117.refs_16_), channel_id=1, source_target_pairs={{0,4},{2,6},{4,0},{6,2},{8,12},{10,14},{12,8},{14,10},{16,20},{18,... | collective-permute-start | bytes 3145736 | tf_op jit(solution)/shard_map/ppermute | solution.py:596
  207.2 17.3 %all-to-all-start = ((f32[32,3,32]{2,1,0:T(4,128)}), f32[32,3,32]{2,1,0:T(4,128)S(1)}, u32[]{:S(2)}, u32[]{:S(2)}) async-start(f32[32,3,32]{2,1,0:T(4,128)} %copy.49), calls=%async_computation | async-start | bytes 131072 | tf_op jit(solution)/shard_map/all_to_all | solution.py:705
  227.6 23.3 %collective-permute-start.14 = (bf16[2,2,128,512]{3,2,1,0:T(8,128)(2,1)S(1)}, bf16[2,2,128,512]{3,2,1,0:T(8,128)(2,1)S(1)}, u32[]{:S(2)}, u32[]{:S(2)}) collective-permute-start(bf16[2,2,128,512]{3,2,1,0:T(8,128)(2,1)S(1)} %pad_maximum_fusion.1.refs_4_), channel_id=1, source_target_pairs={{0,8},{2,10},{4,12},{6,14},{8,0},{10,2},{12,4},{14,6},{16,24},{18,... | collective-permute-start | bytes 1572872 | tf_op jit(solution)/shard_map/ppermute | solution.py:596
  230.8 22.7 %collective-permute-start.17 = (bf16[4,128,512]{2,1,0:T(8,128)(2,1)S(1)}, bf16[4,128,512]{2,1,0:T(8,128)(2,1)S(1)}, u32[]{:S(2)}, u32[]{:S(2)}) collective-permute-start(bf16[4,128,512]{2,1,0:T(8,128)(2,1)S(1)} %get-tuple-element.134.refs_6_), channel_id=1, source_target_pairs={{0,2},{2,0},{4,6},{6,4},{8,10},{10,8},{12,14},{14,12},{16,18},{18,... | collective-permute-start | bytes 1572872 | tf_op jit(solution)/shard_map/ppermute | solution.py:596
  233.9 19.7 %collective-permute-start.16 = (bf16[4,128,512]{2,1,0:T(8,128)(2,1)S(1)}, bf16[4,128,512]{2,1,0:T(8,128)(2,1)S(1)}, u32[]{:S(2)}, u32[]{:S(2)}) collective-permute-start(bf16[4,128,512]{2,1,0:T(8,128)(2,1)S(1)} %get-tuple-element.132.refs_5_), channel_id=1, source_target_pairs={{0,4},{2,6},{4,0},{6,2},{8,12},{10,14},{12,8},{14,10},{16,20},{18,... | collective-permute-start | bytes 1572872 | tf_op jit(solution)/shard_map/ppermute | solution.py:596
  250.9 14.2 %collective-permute-start.15 = (bf16[1,2,128,512]{3,2,1,0:T(8,128)(2,1)S(1)}, bf16[1,2,128,512]{3,2,1,0:T(8,128)(2,1)S(1)}, u32[]{:S(2)}, u32[]{:S(2)}) collective-permute-start(bf16[1,2,128,512]{3,2,1,0:T(8,128)(2,1)S(1)} %pad_maximum_fusion.6), channel_id=1, source_target_pairs={{0,16},{2,18},{4,20},{6,22},{8,24},{10,26},{12,28},{14,30},{16,0},... | collective-permute-start | bytes 786440 | tf_op jit(solution)/shard_map/ppermute | solution.py:596
  253.9 18.4 %collective-permute-start.18 = (bf16[2,2,128,512]{3,2,1,0:T(8,128)(2,1)S(1)}, bf16[2,2,128,512]{3,2,1,0:T(8,128)(2,1)S(1)}, u32[]{:S(2)}, u32[]{:S(2)}) collective-permute-start(bf16[2,2,128,512]{3,2,1,0:T(8,128)(2,1)S(1)} %copy.50), channel_id=1, source_target_pairs={{0,8},{2,10},{4,12},{6,14},{8,0},{10,2},{12,4},{14,6},{16,24},{18,... | collective-permute-start | bytes 1572872 | tf_op jit(solution)/shard_map/ppermute | solution.py:596
  272.4 12.6 %collective-permute-start.19 = (bf16[1,2,128,512]{3,2,1,0:T(8,128)(2,1)S(1)}, bf16[1,2,128,512]{3,2,1,0:T(8,128)(2,1)S(1)}, u32[]{:S(2)}, u32[]{:S(2)}) collective-permute-start(bf16[1,2,128,512]{3,2,1,0:T(8,128)(2,1)S(1)} %pad_maximum_fusion.7), channel_id=1, source_target_pairs={{0,16},{2,18},{4,20},{6,22},{8,24},{10,26},{12,28},{14,30},{16,0},... | collective-permute-start | bytes 786440 | tf_op jit(solution)/shard_map/ppermute | solution.py:596
  (11 other events, 93.9 us)

commit v2 on v0

v2 whole, which is shorter than its diff:
```python
import functools

import jax
import jax.experimental.pallas as pl
import jax.experimental.pallas.tpu as pltpu
import jax.numpy as jnp
from jax import lax
from jax.sharding import PartitionSpec as P

H = 16
norm_eps = 1e-05
f32 = jnp.float32
bf16 = jnp.bfloat16
VMEM_BYTES = 58 * 1024 * 1024


def params(count=1):
    return pltpu.CompilerParams(
        dimension_semantics=("arbitrary",) * count, vmem_limit_bytes=VMEM_BYTES
    )


def cost(micros):
    return pl.CostEstimate(
        flops=int(micros * 1e8), bytes_accessed=int(micros * 3.5e5), transcendentals=0
    )


def call(kernel, arrays, waits=(), scalars=(), **rest):
    first = len(scalars) + len(arrays)

    def body(*refs):
        kernel(*refs[:first], *refs[first + len(waits) :])

    grid = pltpu.PrefetchScalarGridSpec(
        num_scalar_prefetch=len(scalars),
        grid=rest.pop("grid"),
        in_specs=list(rest.pop("in_specs")) + [pl.BlockSpec(memory_space=pl.ANY)] * len(waits),
        out_specs=rest.pop("out_specs"),
        scratch_shapes=rest.pop("scratch_shapes", ()),
    )
    return pl.pallas_call(body, grid_spec=grid, **rest)(*scalars, *arrays, *waits)


def whole(array):
    rank = len(array.shape)
    return pl.BlockSpec(array.shape, lambda *_: (0,) * rank, pipeline_mode=pl.Buffered(1))


def dot_nn(left, right):
    return lax.dot_general(left, right, (((1,), (0,)), ((), ())), preferred_element_type=f32)


def dot_nt(left, right):
    return lax.dot_general(left, right, (((1,), (1,)), ((), ())), preferred_element_type=f32)


def dot_tn(left, right):
    return lax.dot_general(left, right, (((0,), (0,)), ((), ())), preferred_element_type=f32)


def inv_rms(values):
    return lax.rsqrt(jnp.mean(values * values, axis=-1, keepdims=True) + norm_eps)


GROUP = 4


def flat_row(ref):
    values = ref[...].astype(f32)
    return jnp.concatenate([values[i : i + 1] for i in range(values.shape[0])], axis=1)


def fold(values):
    rows, width = values.shape
    return jnp.sum(values.reshape(rows // 8, 8, width), axis=0)


class Copies:
    def __init__(self, sems):
        self.sems, self.count, self.sent = sems, 0, []

    def start(self, source, target):
        copy = pltpu.make_async_copy(source, target, self.sems.at[self.count])
        self.count += 1
        copy.start()
        return copy

    def send(self, source, target):
        self.sent.append(self.start(source, target))

    def finish(self):
        for copy in self.sent:
            copy.wait()


HBM = pl.BlockSpec(memory_space=pl.ANY)


def stacked(rows, head):
    lane_head = lax.broadcasted_iota(jnp.int32, rows.shape, 1) // head
    zero = jnp.zeros_like(rows)
    return jnp.concatenate([jnp.where(lane_head == h, rows, zero) for h in range(GROUP)], axis=0)


def unstacked(rows, head):
    slots = rows.shape[0] // GROUP
    lane_head = lax.broadcasted_iota(jnp.int32, (slots, rows.shape[1]), 1) // head
    out = rows[:slots]
    for h in range(1, GROUP):
        out = jnp.where(lane_head == h, rows[h * slots : (h + 1) * slots], out)
    return out


def front_kernel(
    lengths_ref, index_ref, gain_one_ref, router_ref, gain_two_ref,
    tokens_hbm, cotangent_hbm, query_hbm, key_hbm, value_hbm, out_hbm,
    chosen_out, lefts_out, queries_out, keys_out, values_out, probs_out, attn_out, feed_out, pulled_out,
    score_out,
    tokens, cotangent, query_w, key_w, value_w, out_w,
    chosen, lefts, queries, keys, values, probs, attn, feed, pulled, score, sems,
):
    copies = Copies(sems)
    seqs, _, slots = index_ref.shape
    places, width = tokens.shape[1], tokens.shape[2]
    head = width // H
    arriving = []
    for seq in range(seqs):
        part = pl.ds(seq * places, places)
        arriving.append(
            [
                copies.start(tokens_hbm.at[part], tokens.at[seq]),
                copies.start(cotangent_hbm.at[part], cotangent.at[seq]),
            ]
        )
    weights = [
        copies.start(*pair)
        for pair in (
            (query_hbm, query_w), (key_hbm, key_w), (value_hbm, value_w), (out_hbm, out_w),
        )
    ]
    gain_one, router, gain_two = [flat_row(r) for r in (gain_one_ref, router_ref, gain_two_ref)]
    slot_id = lax.broadcasted_iota(jnp.int32, (slots, places), 0)
    place_id = lax.broadcasted_iota(jnp.int32, (slots, places), 1)
    square = (slots, slots)
    diagonal = lax.broadcasted_iota(jnp.int32, square, 0) == lax.broadcasted_iota(jnp.int32, square, 1)
    for seq in range(seqs):
        rows = slice(seq * slots, (seq + 1) * slots)
        routed = lax.div(lengths_ref[0, seq], 8)
        index = jnp.sum(jnp.where(diagonal, index_ref[seq], 0), axis=1, keepdims=True)
        pick = ((index == place_id) & (slot_id < routed)).astype(bf16)
        arriving[seq][0].wait()
        wide = dot_nn(pick, tokens[seq])
        chosen[rows] = wide.astype(bf16)
        logit = jnp.sum(wide * router, axis=-1, keepdims=True)
        chance = 1.0 / (1.0 + jnp.exp(-logit))
        score[rows] = jnp.broadcast_to(chance, (slots, score.shape[1]))
        lefts[0, rows] = (wide * inv_rms(wide) * gain_one).astype(bf16)
        arriving[seq][1].wait()
        pull = dot_nn(pick, cotangent[seq])
        pulled[rows] = pull.astype(bf16)
        feed[1, rows] = (chance * pull).astype(bf16)
    copies.send(chosen, chosen_out)
    copies.send(pulled, pulled_out)
    copies.send(score, score_out)
    copies.send(feed.at[1], feed_out.at[1])
    copies.send(lefts.at[0], lefts_out.at[0])
    first = lefts[0]
    weights[0].wait()
    queries[...] = (dot_nn(first, query_w[...]) * 0.125).astype(bf16)
    copies.send(queries, queries_out)
    weights[1].wait()
    keys[...] = dot_nn(first, key_w[...]).astype(bf16)
    copies.send(keys, keys_out)
    weights[2].wait()
    values[...] = dot_nn(first, value_w[...]).astype(bf16)
    copies.send(values, values_out)
    stack = GROUP * slots
    row_id = lax.broadcasted_iota(jnp.int32, (stack, slots), 0) % slots
    col_id = lax.broadcasted_iota(jnp.int32, (stack, slots), 1)
    for seq in range(seqs):
        rows = slice(seq * slots, (seq + 1) * slots)
        allowed = (col_id <= row_id) & (col_id < lax.div(lengths_ref[0, seq], 8))
        for g in range(H // GROUP):
            lanes = slice(g * GROUP * head, (g + 1) * GROUP * head)
            scores = dot_nt(stacked(queries[rows, lanes], head), keys[rows, lanes])
            scores = jnp.where(allowed, scores, -1e30)
            exped = jnp.exp(scores - jnp.max(scores, axis=-1, keepdims=True))
            chances = (exped / jnp.sum(exped, axis=-1, keepdims=True)).astype(bf16)
            probs[seq, g] = chances
            mixed = dot_nn(chances, values[rows, lanes])
            lefts[1, rows, lanes] = unstacked(mixed, head).astype(bf16)
        copies.send(probs.at[seq], probs_out.at[seq])
    copies.send(lefts.at[1], lefts_out.at[1])
    weights[3].wait()
    attn[...] = dot_nn(lefts[1], out_w[...])
    copies.send(attn, attn_out)
    for seq in range(seqs):
        rows = slice(seq * slots, (seq + 1) * slots)
        after = chosen[rows].astype(f32) + attn[rows]
        feed[0, rows] = (after * inv_rms(after) * gain_two).astype(bf16)
    copies.send(feed.at[0], feed_out.at[0])
    copies.finish()


def front(lengths, index, tokens, cotangent, vectors, wq, wk, wv, wo):
    seqs, slots = index.shape
    places, width = tokens.shape[0] // seqs, tokens.shape[1]
    rows = seqs * slots
    low = ((rows, width), bf16)
    outs = [
        low, ((2, rows, width), bf16), low, low, low,
        ((seqs, H // GROUP, GROUP * slots, slots), bf16), ((rows, width), f32),
        ((2, rows, width), bf16), low, ((rows, 128), f32),
    ]
    small = [index[:, None, :], *vectors]
    return call(
        front_kernel,
        [*small, tokens, cotangent, wq, wk, wv, wo],
        (),
        [lengths],
        grid=(1,),
        in_specs=[whole(array) for array in small] + [HBM] * 6,
        out_specs=[HBM] * len(outs),
        scratch_shapes=[pltpu.VMEM((seqs, places, width), bf16)] * 2
        + [pltpu.VMEM((width, width), bf16)] * 4
        + [pltpu.VMEM(*out) for out in outs]
        + [pltpu.SemaphoreType.DMA((2 * seqs + 4 + 11 + seqs,))],
        out_shape=[jax.ShapeDtypeStruct(*out) for out in outs],
        compiler_params=params(),
        name="front",
        cost_estimate=cost(18),
    )


def gelu_both(z):
    cdf = 0.5 + 0.5 * lax.erf(z * 0.7071067811865476)
    return z * cdf, cdf + z * (jnp.exp(-0.5 * z * z) * 0.3989422804014327)


def link_bits(nodes):
    bits = nodes.bit_length() - 1
    half = (bits - 2) // 2
    return list(range(half)), list(range(half, bits - 2)), [bits - 2], [bits - 1]


def link_order(nodes, names):
    x, y, near, far = link_bits(nodes)
    return sum([{"x": x, "y": y, "n": near, "f": far}[name] for name in names], [])


def spot_of(rel, order):
    return sum(((rel >> bit) & 1) << (len(order) - 1 - i) for i, bit in enumerate(order))


def own_blocks(me_ref, source, size, nodes):
    core, node = me_ref[0], me_ref[1]
    for rel in range(nodes):
        owner = lax.bitwise_xor(node, rel) * 2
        starts = [pl.multiple_of((owner + side) * size, size) for side in (core, 1 - core)]
        yield rel, *[source[pl.ds(start, size), :].astype(bf16) for start in starts]


def held_type(size):
    return bf16 if size % 16 == 0 else f32


def feed_kernel(me_ref, own_ref, other_ref, *refs, nodes, pieces, orders):
    ups, downs, refs = refs[:pieces], refs[pieces : 2 * pieces], refs[2 * pieces :]
    (
        sums_ref, sent_ref, down_gone, down_kept, up_gone, up_kept,
        rows_ref, grads_ref, turned_ref, down_terms, up_terms, grad_sum, out_sum,
    ) = refs
    step, steps = pl.program_id(0), pl.num_programs(0)
    node = me_ref[1]
    flat = nodes // 4
    count = own_ref.shape[1]

    @pl.when(step == 0)
    def _():
        rows_ref[:count] = own_ref[0]
        rows_ref[count:] = other_ref[0]
        grads_ref[:count] = own_ref[1]
        grads_ref[count:] = other_ref[1]
        turned_ref[...] = grads_ref[...].T
        out_sum[...] = jnp.zeros_like(out_sum)
        grad_sum[...] = jnp.zeros_like(grad_sum)

    w_up = jnp.concatenate([ref[...] for ref in ups], axis=1)
    w_down = jnp.concatenate([ref[...] for ref in downs], axis=0)
    hidden = dot_nn(rows_ref[...], w_up)
    act, slope = gelu_both(hidden)
    act = act.astype(bf16)
    pre = (dot_nt(grads_ref[...], w_down) * slope).astype(bf16)

    down_terms[...] = dot_nn(turned_ref[...], act).astype(down_terms.dtype)
    size = down_terms.shape[0] // nodes
    for rel in range(nodes):
        spot = spot_of(rel, orders[0])
        start = pl.multiple_of(lax.bitwise_xor(node, rel) * size, size)
        values = down_terms[pl.ds(start, size), :].astype(bf16)
        (down_kept, down_gone)[spot // (nodes // 2)][spot % (nodes // 2)] = values

    up_terms[...] = dot_tn(pre, rows_ref[...]).astype(up_terms.dtype)
    size = up_kept.shape[2]
    for rel in range(flat):
        spot = spot_of(rel, orders[1][:-2])
        start = pl.multiple_of(lax.bitwise_xor(lax.rem(node, flat), rel) * size, size)
        values = up_terms[pl.ds(start, size), :].astype(bf16)
        (up_kept, up_gone)[spot // (flat // 2)][spot % (flat // 2), 0] = values

    out_sum[...] += dot_nn(act, w_down)
    grad_sum[...] += dot_nt(pre, w_up)

    @pl.when(step == steps - 1)
    def _():
        for i, total in enumerate((grad_sum, out_sum)):
            sums_ref[i] = total[:count].astype(bf16)
            sent_ref[i] = total[count:].astype(bf16)


def feed(me, own, other, w_up, w_down, nodes, orders, steps=4, waits=()):
    _, rows, width = own.shape
    hidden = w_up.shape[1]
    flat = nodes // 4
    size = hidden // (2 * nodes)
    block = hidden // 2 // steps
    if size % 128:
        w_up = lax.dynamic_index_in_dim(w_up.reshape(width, nodes, 2, size), me[0], 2, False)
        w_down = lax.dynamic_index_in_dim(w_down.reshape(nodes, 2, size, width), me[0], 1, False)
        w_up, w_down = w_up.reshape(width, -1), w_down.reshape(-1, width)
        pieces = 1
        place = lambda piece, i, me: i
    else:
        pieces = block // size
        place = lambda piece, i, me: (i * pieces + piece) * 2 + me[0]
    columns = block // pieces
    up_specs = [
        pl.BlockSpec((width, columns), lambda i, me, p=p: (0, place(p, i, me)))
        for p in range(pieces)
    ]
    down_specs = [
        pl.BlockSpec((columns, width), lambda i, me, p=p: (place(p, i, me), 0))
        for p in range(pieces)
    ]
    chunk = width // nodes
    down_spec = pl.BlockSpec((nodes // 2, chunk, block), lambda i, me: (0, 0, i))
    rel = lambda i, me: lax.bitwise_xor(i, lax.div(me[1], flat))
    up_spec = pl.BlockSpec(
        (flat // 2, 1, size, width),
        lambda i, me: (0, lax.rem(rel(i, me), 2) * 2 + lax.div(rel(i, me), 2), 0, 0),
    )
    pair = jax.ShapeDtypeStruct((2, rows, width), bf16)
    return call(
        functools.partial(feed_kernel, nodes=nodes, pieces=pieces, orders=orders),
        [own, other] + [w_up] * pieces + [w_down] * pieces,
        waits,
        [me],
        grid=(steps,),
        in_specs=[whole(own), whole(other)] + up_specs + down_specs,
        out_specs=[pl.BlockSpec((2, rows, width), lambda i, me: (0, 0, 0))] * 2
        + [down_spec, down_spec, up_spec, up_spec],
        scratch_shapes=[
            pltpu.VMEM((2 * rows, width), bf16),
            pltpu.VMEM((2 * rows, width), bf16),
            pltpu.VMEM((width, 2 * rows), bf16),
            pltpu.VMEM((width, block), held_type(chunk)),
            pltpu.VMEM((block, width), held_type(size)),
            pltpu.VMEM((2 * rows, width), f32),
            pltpu.VMEM((2 * rows, width), f32),
        ],
        out_shape=[pair] * 2
        + [jax.ShapeDtypeStruct((nodes // 2, chunk, hidden // 2), bf16)] * 2
        + [jax.ShapeDtypeStruct((flat // 2, 4, size, width), bf16)] * 2,
        compiler_params=params(),
        name="feed",
        cost_estimate=cost(34),
    )


def back_kernel(
    me_ref, gain_ref, chosen_hbm, attn_hbm, score_hbm, pulled_hbm, own_hbm, other_hbm, queries_hbm,
    keys_hbm, values_hbm, probs_hbm, lefts_hbm, out_hbm,
    grads_out, after_out, gain_out, send_gone_out, send_stay_out, keep_gone_out, keep_stay_out,
    send_b_out, keep_b_out,
    chosen, attn, score, pulled, own, other, queries, keys, values, probs, lefts, out_w,
    grads, after_grad, send_gone, send_stay, keep_gone, keep_stay, send_b, keep_b,
    attn_grad, mix_grad, terms, sems,
    *, nodes, orders,
):
    copies = Copies(sems)
    fetched = {}
    for name, source, target in (
        ("rows", chosen_hbm, chosen), ("rows", attn_hbm, attn), ("rows", own_hbm.at[0], own),
        ("rows", other_hbm.at[0], other), ("rows", score_hbm, score), ("rows", pulled_hbm, pulled),
        ("out", out_hbm, out_w), ("heads", queries_hbm, queries), ("heads", keys_hbm, keys),
        ("heads", values_hbm, values), ("heads", probs_hbm, probs), ("lefts", lefts_hbm, lefts),
    ):
        fetched.setdefault(name, []).append(copies.start(source, target))

    def arrive(name):
        for copy in fetched[name]:
            copy.wait()

    seqs, groups, stack, slots = probs.shape
    width = chosen.shape[1]
    head = width // H
    gain = flat_row(gain_ref)
    arrive("rows")
    for seq in range(seqs):
        rows = slice(seq * slots, (seq + 1) * slots)
        after = chosen[rows].astype(f32) + attn[rows]
        inv = inv_rms(after)
        normed = after * inv
        arrived = add_low(own[rows], other[rows]).astype(f32)
        total = fold(arrived * normed)
        gain_out[...] = total if seq == 0 else gain_out[...] + total
        weighted = arrived * gain
        back = inv * (weighted - normed * jnp.mean(weighted * normed, axis=-1, keepdims=True))
        after_grad[rows] = back
        delta = score[rows, :1] * pulled[rows].astype(f32)
        attn_grad[rows] = (delta + back).astype(bf16)
    copies.send(after_grad, after_out)
    arrive("out")
    mix_grad[...] = dot_nt(attn_grad[...], out_w[...]).astype(bf16)
    arrive("heads")
    for seq in range(seqs):
        rows = slice(seq * slots, (seq + 1) * slots)
        for g in range(groups):
            lanes = slice(g * GROUP * head, (g + 1) * GROUP * head)
            chances = probs[seq, g]
            wide = chances.astype(f32)
            stacked_queries = stacked(queries[rows, lanes], head)
            stacked_grads = stacked(mix_grad[rows, lanes], head)
            prob_grad = dot_nt(stacked_grads, values[rows, lanes])
            total = jnp.sum(prob_grad * wide, axis=-1, keepdims=True)
            score_grad = (wide * (prob_grad - total)).astype(bf16)
            grads[2, rows, lanes] = dot_tn(chances, stacked_grads).astype(bf16)
            grads[1, rows, lanes] = dot_tn(score_grad, stacked_queries).astype(bf16)
            grads[0, rows, lanes] = unstacked(dot_nn(score_grad, keys[rows, lanes]), head).astype(bf16)
    copies.send(grads, grads_out)
    arrive("lefts")
    half, cut = nodes // 2, send_gone.shape[3]
    outs = (
        (send_gone, send_gone_out), (keep_gone, keep_gone_out), (send_stay, send_stay_out),
        (keep_stay, keep_stay_out), (send_b, send_b_out), (keep_b, keep_b_out),
    )
    for which in range(4):
        if which < 3:
            product = dot_tn(grads[which], lefts[0])
        else:
            product = dot_tn(attn_grad[...], lefts[1])
        terms[...] = (product * 0.125 if which == 0 else product).astype(terms.dtype)
        for rel, kept, sent in own_blocks(me_ref, terms, send_b.shape[2], nodes):
            spot = spot_of(rel, orders[0])
            (keep_stay, keep_gone)[spot // half][spot % half, which] = kept[:, :cut]
            (send_stay, send_gone)[spot // half][spot % half, which] = sent[:, :cut]
            spot = spot_of(rel, orders[1])
            keep_b[spot, which] = kept[:, cut:]
            send_b[spot, which] = sent[:, cut:]
        for held, target in outs:
            copies.send(held.at[:, which], target.at[:, which])
    copies.finish()


def back(
    me, chosen, attn, score, pulled, own, other, gain, queries, keys, values, probs, lefts, w_out, nodes,
    orders, cut,
):
    rows, width = chosen.shape
    seqs, _, _, slots = probs.shape
    size = width // (2 * nodes)
    layout = [(nodes // 2, cut)] * 4 + [(nodes, width - cut)] * 2
    shapes = [((count, 4, size, columns), bf16) for count, columns in layout]
    outs = [((3, rows, width), bf16), ((rows, width), f32)]
    fetched = [chosen, attn, score, pulled, own, other, queries, keys, values, probs, lefts, w_out]
    held = [pltpu.VMEM(array.shape, array.dtype) for array in fetched]
    held[4] = held[5] = pltpu.VMEM((rows, width), bf16)
    return call(
        functools.partial(back_kernel, nodes=nodes, orders=orders),
        [gain, *fetched],
        (),
        [me],
        grid=(1,),
        in_specs=[whole(gain)] + [HBM] * len(fetched),
        out_specs=[HBM, HBM, pl.BlockSpec((8, width), lambda *_: (0, 0))] + [HBM] * 6,
        scratch_shapes=held
        + [pltpu.VMEM(*out) for out in outs + shapes]
        + [pltpu.VMEM((rows, width), bf16)] * 2
        + [pltpu.VMEM((width, width), held_type(size))]
        + [pltpu.SemaphoreType.DMA((len(fetched) + 2 + 24,))],
        out_shape=[jax.ShapeDtypeStruct(*out) for out in outs]
        + [jax.ShapeDtypeStruct((8, width), f32)]
        + [jax.ShapeDtypeStruct(*shape) for shape in shapes],
        compiler_params=params(),
        name="back",
        cost_estimate=cost(20),
    )


def last_kernel(
    gain_ref, router_ref, chosen_hbm, attn_hbm, own_hbm, other_hbm, score_hbm, pulled_hbm, after_hbm,
    grads_hbm, query_hbm, key_hbm, value_hbm,
    chosen_grad_out, gain_out, router_out,
    chosen, attn, own, other, score, pulled, after_grad, grads, query_w, key_w, value_w,
    first_grad, chosen_grad, sems,
):
    copies = Copies(sems)
    weights = ((query_hbm, query_w), (key_hbm, key_w), (value_hbm, value_w))
    pairs = [
        (copies.start(grads_hbm.at[i], grads.at[i]), copies.start(*weight))
        for i, weight in enumerate(weights)
    ]
    others = [
        copies.start(*pair)
        for pair in (
            (chosen_hbm, chosen), (attn_hbm, attn), (own_hbm.at[1], own), (other_hbm.at[1], other),
            (score_hbm, score), (pulled_hbm, pulled), (after_hbm, after_grad),
        )
    ]
    gain, router = flat_row(gain_ref), flat_row(router_ref)
    for i, pair in enumerate(pairs):
        for copy in pair:
            copy.wait()
        product = dot_nt(grads[i], weights[i][1][...])
        if i == 0:
            first_grad[...] = product * 0.125
        else:
            first_grad[...] += product
    for copy in others:
        copy.wait()
    rows = chosen.shape[0]
    block = rows // 4
    for i in range(4):
        part = slice(i * block, (i + 1) * block)
        wide = chosen[part].astype(f32)
        chance = score[part, :1]
        branch = attn[part] + add_low(own[part], other[part]).astype(f32)
        pull = jnp.sum(pulled[part].astype(f32) * branch, axis=-1, keepdims=True)
        logit_grad = pull * chance * (1.0 - chance)
        arrived = first_grad[part]
        inv = inv_rms(wide)
        normed = wide * inv
        weighted = arrived * gain
        chosen_grad[part] = (
            inv * (weighted - normed * jnp.mean(weighted * normed, axis=-1, keepdims=True))
            + after_grad[part]
            + logit_grad * router
        )
        copies.send(chosen_grad.at[pl.ds(i * block, block)], chosen_grad_out.at[pl.ds(i * block, block)])
        gain_sum, router_sum = fold(arrived * normed), fold(logit_grad * wide)
        gain_out[...] = gain_sum if i == 0 else gain_out[...] + gain_sum
        router_out[...] = router_sum if i == 0 else router_out[...] + router_sum
    copies.finish()


def last(
    chosen, attn, own, other, score, pulled, after_grad, grads, gain, router, wq, wk, wv, waits=()
):
    rows, width = chosen.shape
    fetched = [chosen, attn, own, other, score, pulled, after_grad, grads, wq, wk, wv]
    held = [pltpu.VMEM(array.shape, array.dtype) for array in fetched]
    held[2] = held[3] = pltpu.VMEM((rows, width), bf16)
    sums = pl.BlockSpec((8, width), lambda *_: (0, 0))
    return call(
        last_kernel,
        [gain, router, *fetched],
        waits,
        grid=(1,),
        in_specs=[whole(gain), whole(router)] + [HBM] * len(fetched),
        out_specs=[HBM, sums, sums],
        scratch_shapes=held
        + [pltpu.VMEM((rows, width), f32)] * 2
        + [pltpu.SemaphoreType.DMA((17,))],
        out_shape=[jax.ShapeDtypeStruct((rows, width), f32)]
        + [jax.ShapeDtypeStruct((8, width), f32)] * 2,
        compiler_params=params(),
        name="last",
        cost_estimate=cost(9),
    )


def spread_kernel(lengths_ref, index_ref, base_hbm, *refs, deltas, pieces):
    deltas_hbm, out_hbm, base, out = refs[:deltas], refs[deltas], refs[deltas + 1], refs[deltas + 2]
    held, sems = refs[deltas + 3 : -1], refs[-1]
    copies = Copies(sems)
    seqs, _, slots = index_ref.shape
    count = base.shape[1]
    arriving = []
    for seq in range(seqs):
        row = pl.ds(seq * slots, slots)
        steps = [
            copies.start(
                source.at[source.shape[0] - 1, row] if len(source.shape) == 3 else source.at[row],
                target.at[row],
            )
            for source, target in zip(deltas_hbm, held)
        ]
        for piece in range(seq * pieces, (seq + 1) * pieces):
            steps.append(copies.start(base_hbm.at[pl.ds(piece * count, count)], base.at[piece]))
        arriving.append(steps)
    for seq in range(seqs):
        rows = slice(seq * slots, (seq + 1) * slots)
        for copy in arriving[seq][:deltas]:
            copy.wait()
        if deltas == 1:
            delta = held[0][rows]
        else:
            score, attn, own, other = held
            delta = score[rows, :1] * (attn[rows] + add_low(own[rows], other[rows]).astype(f32))
        high = delta.astype(bf16)
        low = (delta - high.astype(f32)).astype(bf16)
        both = jnp.concatenate([high, low], axis=0)
        slot_id = lax.broadcasted_iota(jnp.int32, (count, slots), 1)
        live = slot_id < lax.div(lengths_ref[0, seq], 8)
        for piece in range(pieces):
            place = piece * count + lax.broadcasted_iota(jnp.int32, (count, slots), 0)
            pick = ((index_ref[seq] == place) & live).astype(bf16)
            at = seq * pieces + piece
            arriving[seq][deltas + piece].wait()
            added = dot_nn(jnp.concatenate([pick, pick], axis=1), both)
            out[at] = (base[at].astype(f32) + added).astype(out.dtype)
            copies.send(out.at[at], out_hbm.at[pl.ds(at * count, count)])
    copies.finish()


def spread(lengths, index, base, deltas, dtype, waits=(), pieces=2):
    seqs, slots = index.shape
    rows, width = base.shape
    steps = seqs * pieces
    index = index[:, None, :]
    held = [pltpu.VMEM(delta.shape[-2:], delta.dtype) for delta in deltas]
    return call(
        functools.partial(spread_kernel, deltas=len(deltas), pieces=pieces),
        [index, base, *deltas],
        waits,
        [lengths],
        grid=(1,),
        in_specs=[whole(index)] + [HBM] * (1 + len(deltas)),
        out_specs=HBM,
        scratch_shapes=[
            pltpu.VMEM((steps, rows // steps, width), bf16),
            pltpu.VMEM((steps, rows // steps, width), dtype),
            *held,
            pltpu.SemaphoreType.DMA((2 * steps + len(deltas) * seqs,)),
        ],
        out_shape=jax.ShapeDtypeStruct((rows, width), dtype),
        compiler_params=params(),
        name="spread",
        cost_estimate=cost(8),
    )


def add_low(left, right):
    return (left.astype(f32) + right.astype(f32)).astype(bf16)


def swap_nodes(values, bit, nodes):
    return lax.ppermute(values, "seq", [(i, i ^ (1 << bit)) for i in range(nodes)])


def swap_cores(values):
    return lax.ppermute(values, "dp", [(0, 1), (1, 0)])


class Part:
    def __init__(self, order, nodes):
        self.order, self.nodes = order, nodes

    @classmethod
    def halved(cls, gone, kept, order, nodes):
        part = cls(order, nodes)
        part.gone, part.kept = gone, kept
        part.swap()
        return part

    @classmethod
    def of_cores(cls, send, keep, order, nodes):
        part = cls(order, nodes)
        part.kept, part.got = keep, swap_cores(send)
        return part

    @classmethod
    def of_split_cores(cls, send_gone, send_stay, keep_gone, keep_stay, order, nodes):
        part = cls(order, nodes)
        part.halves = (keep_gone, swap_cores(send_gone)), (keep_stay, swap_cores(send_stay))
        return part

    halves = None

    def swap(self):
        self.got = swap_nodes(self.gone, self.order[0], self.nodes)
        self.order = self.order[1:]

    def halve(self, after=()):
        if self.halves:
            (keep_gone, got_gone), (keep_stay, got_stay), *_ = lax.optimization_barrier(
                (*self.halves, *after)
            )
            self.gone, self.kept = add_low(keep_gone, got_gone), add_low(keep_stay, got_stay)
            self.halves = None
            return
        if after:
            self.kept, self.got, *_ = lax.optimization_barrier((self.kept, self.got, *after))
        if self.kept.shape[0] == 1:
            self.kept, self.got = self.kept[0], self.got[0]
        count = self.kept.shape[0] // 2
        halves = [add_low(self.kept[c], self.got[c]) for c in (slice(count, None), slice(count))]
        self.gone, self.kept = [half[0] for half in halves] if count == 1 else halves

    def step(self, after=()):
        self.halve(after)
        self.swap()
        return self.gone


class Chain:
    def __init__(self, parts):
        self.parts = parts

    def step(self, count=1, after=()):
        sent = []
        for _ in range(count):
            sent = [part.step(after) for part in self.parts]
        return sent

    def final(self, after=()):
        for part in self.parts:
            part.halve(after)
        gone = jnp.concatenate([part.gone for part in self.parts], axis=-1)
        self.got = swap_nodes(gone, self.parts[0].order[0], self.parts[0].nodes)
        return [gone]

    def sum(self):
        kept = jnp.concatenate([part.kept for part in self.parts], axis=-1)
        return kept.astype(f32) + self.got.astype(f32)


def both_cores(core, rows, nodes):
    count = rows.shape[0] // 2
    mine, sent = [
        lax.dynamic_slice_in_dim(rows, side * count, count) for side in (core, 1 - core)
    ]
    got = swap_cores(sent)
    shape = (count, nodes, 1, rows.shape[1] // nodes)
    sides = [jnp.where(core == side, mine, got).reshape(shape) for side in (0, 1)]
    return jnp.concatenate(sides, axis=2).reshape(count, -1)


def on_device(
    tokens,
    lengths,
    routed_index,
    out_grad,
    gain_attn,
    w_router,
    w_query,
    w_key,
    w_value,
    w_out,
    gain_mlp,
    w_up,
    w_down,
):
    nodes = lax.axis_size("seq")
    width = tokens.shape[2]
    me = jnp.stack([lax.axis_index("dp"), lax.axis_index("seq")]).astype(jnp.int32)
    index = routed_index[0]
    inputs, cotangent = tokens[0], out_grad[0]
    vectors = [vector.reshape(-1, 128) for vector in (gain_attn, w_router, gain_mlp)]
    (
        chosen, lefts, queries, keys, values, probs, attn_out, feed_own, pulled, score,
    ) = front(
        lengths, index, inputs, cotangent, vectors, w_query, w_key, w_value, w_out
    )
    feed_other = swap_cores(feed_own)
    order = lambda names: link_order(nodes, names)
    span = len(order("x"))
    down_order, up_order = order("xynf"), order("yxnf")
    square_orders = [order("nxyf"), order("xynf")]
    own_sums, other_sums, *terms = feed(
        me, feed_own, feed_other, w_up, w_down, nodes, [down_order, up_order]
    )
    got_sums = swap_cores(other_sums)
    down = Chain([Part.halved(*terms[:2], down_order, nodes)])
    up = Chain([Part.halved(*terms[2:], up_order, nodes)])
    grads, after_grad, gain_mlp_sum, *square_terms = back(
        me, chosen, attn_out, score, pulled, own_sums, got_sums, vectors[2], queries, keys, values, probs,
        lefts, w_out, nodes, square_orders, width * 5 // 8,
    )
    square = Chain(
        [
            Part.of_split_cores(*square_terms[:4], square_orders[0], nodes),
            Part.of_cores(*square_terms[4:], square_orders[1], nodes),
        ]
    )
    mixed_out = spread(
        lengths, index, inputs, [score, attn_out, own_sums, got_sums], bf16, waits=square_terms[:1]
    )
    chosen_grad, gain_attn_sum, router_sum = last(
        chosen, attn_out, own_sums, got_sums, score, pulled, after_grad, grads,
        vectors[0], vectors[1], w_query, w_key, w_value, waits=[mixed_out],
    )
    sums = jnp.sum(jnp.stack([gain_attn_sum, router_sum, gain_mlp_sum]), axis=1)
    sums = sums.reshape(3, 2 * nodes, -1).transpose(1, 0, 2)
    gone = down.step(span, after=[chosen_grad])
    gone += up.step(span, after=gone)
    gone += square.step(after=gone)
    token_grad = spread(lengths, index, cotangent, [chosen_grad], f32, waits=gone)
    gone = down.step(span, after=[token_grad])
    gone = up.step(span, after=gone)
    gone = square.step(span, after=gone)
    gone = down.final(after=gone)
    gone = up.final(after=gone)
    gone = square.step(span, after=gone)
    down_sum, _ = lax.optimization_barrier((both_cores(me[0], down.sum(), nodes), gone[0]))
    gone = square.final(after=[up.sum()])
    sums, *_ = lax.optimization_barrier((sums, *gone))
    sums = jnp.sum(lax.all_to_all(sums, ("seq", "dp"), 0, 0, tiled=True), axis=0)
    square_sum = square.sum()
    return (
        mixed_out[None],
        token_grad[None],
        sums[0],
        sums[1],
        *[square_sum[which].T for which in range(4)],
        sums[2],
        up.sum().T,
        down_sum.T,
    )


def solution(mesh):
    in_specs = (
        P("dp", "seq", None),
        P("dp", "seq"),
        P("dp", "seq", None),
        P("dp", "seq", None),
        P(),
        P(),
        P(),
        P(),
        P(),
        P(),
        P(),
        P(),
        P(),
    )
    out_specs = (
        P("dp", "seq", None),
        P("dp", "seq", None),
        P(("seq", "dp")),
        P(("seq", "dp")),
        P(None, ("seq", "dp")),
        P(None, ("seq", "dp")),
        P(None, ("seq", "dp")),
        P(None, ("seq", "dp")),
        P(("seq", "dp")),
        P(None, ("seq", "dp")),
        P(None, ("seq", "dp")),
    )
    return jax.shard_map(
        on_device, mesh=mesh, in_specs=in_specs, out_specs=out_specs, check_vma=False
    )
```

time: 1200 us -> 240 us (0.20)
  waiting for transfers between devices: 871 us -> 53.6 us
  matrix products: 176 us -> 0 us
  Pallas kernels: 0 us -> 122 us
  blocking collectives: 58.1 us -> 0 us
  local copies, waits for them, and re-layouts: 45.6 us -> 8.27 us
  other arithmetic: 6.91 us -> 22.3 us
  between operations: 14.9 us -> 1.16 us
    reduce_scatter x6 -> x0, waiting for transfers between devices: 805 us -> none  [the longest x1 187 us: on_device(): lax.psum_scatter(terms[8], ('seq', 'dp'), scatter_dimension=1, tiled=True)]
    dot_general x35 -> x0, matrix products: 170 us -> none  [the longest x10 61 us: first_dot(): lax.dot_general(left_side, right_side, (((0,), (0,)), ((), ())), preferre...]
    pallas_call x0 -> x6, Pallas kernels: none -> 122 us  [call(): pl.pallas_call(body, grid_spec=grid, **rest)(*scalars, *arrays, *waits)]
    all_to_all x4 -> x1, waiting for transfers between devices: 66 us -> 7.74 us  [on_device(): lax.all_to_all(sums, ('seq', 'dp'), 0, 0, tiled=True)]
    unnamed x2 -> x0, blocking collectives: 58.1 us -> none
    ppermute x0 -> x21, waiting for transfers between devices: none -> 45.9 us  [the longest x15 42.4 us: swap_nodes(): lax.ppermute(values, 'seq', [(i, i ^ 1 << bit) for i in range(nodes)])]
    reshape x8 -> x2, local copies, waits for them, and re-layouts: 28.1 us -> 1.3 us  [the longest x1 1.21 us: both_cores(): return jnp.concatenate(sides, axis=2).reshape(count, -1)]
    ppermute x0 -> x21, starting transfers between devices: none -> 25 us  [the longest x15 23.3 us: swap_nodes(): lax.ppermute(values, 'seq', [(i, i ^ 1 << bit) for i in range(nodes)])]
  transfers between devices with their start and end apart: 10 -> 22, of which waited for: 10 -> 8; matrix products, arithmetic and copies ran while one was open for 8% -> 11% of each run, Pallas kernels for 0% -> 22%
where the time goes in v2:
time: 240 us; the launch traced here: 237 us
  Pallas kernels  122 us (51%)
  waiting for transfers between devices  53.6 us (22%)
  starting transfers between devices  29.6 us (12%)
  other arithmetic  22.3 us (9%)
  local copies, waits for them, and re-layouts  8.27 us (3%)
    pallas_call x6, Pallas kernels, call(): pl.pallas_call(body, grid_spec=grid, **rest)(*scalars, *arrays, *waits)  122 us
    ppermute x15, waiting for transfers between devices, swap_nodes(): lax.ppermute(values, 'seq', [(i, i ^ 1 << bit) for i in range(nodes)])  42.4 us
    ppermute x15, starting transfers between devices, swap_nodes(): lax.ppermute(values, 'seq', [(i, i ^ 1 << bit) for i in range(nodes)])  23.3 us
    convert_element_type x10, other arithmetic, add_low(): return (left.astype(f32) + right.astype(f32)).astype(bf16)  16.3 us
    all_to_all x1, waiting for transfers between devices, on_device(): lax.all_to_all(sums, ('seq', 'dp'), 0, 0, tiled=True)  7.74 us
    squeeze x5, other arithmetic, halve(): half[0]  4.94 us
  transfers between devices with their start and end apart: 22, of which 8 were waited for; matrix products, arithmetic and copies ran while one was open for 11% of the time, Pallas kernels for 22%

profile of v2, /device:TPU:0, one launch (start us, length us, event | category | flops | bytes accessed | tf_op | source)
XLA Modules:
  0.0 237.4 jit_solution(17568290720818119976)
XLA Ops:
  0.6 20.2 %front.1 = (bf16[512,1024]{1,0:T(8,128)(2,1)}, bf16[2,512,1024]{2,1,0:T(8,128)(2,1)}, bf16[512,1024]{1,0:T(8,128)(2,1)}, bf16[512,1024]{1,0:T(8,128)(2,1)}, bf16...) custom-call(s32[1,4]{1,0:T(1,128)} %refs_0_.5, ...), custom_call_target="tpu_custom_call" | custom-call | flops 1800000000 | bytes 6300000 | tf_op jit(solution)/shard_map/front/pallas_call | solution.py:42
  21.9 3.4 %collective-permute-done.refs_2_ = bf16[2,512,1024]{2,1,0:T(8,128)(2,1)S(1)} collective-permute-done((bf16[2,512,1024]{2,1,0:T(8,128)(2,1)}, bf16[2,512,1024]{2,1,0:T(8,128)(2,1)S(1)}, u32[]{:S(2)}, u32[]{:S(2)}) %collective-permute-start) | collective-permute-done | bytes 2097184 | tf_op jit(solution)/shard_map/ppermute | solution.py:663
  26.7 49.4 %feed.1 = (bf16[2,512,1024]{2,1,0:T(8,128)(2,1)}, bf16[2,512,1024]{2,1,0:T(8,128)(2,1)}, bf16[8,64,2048]{2,1,0:T(8,128)(2,1)}, bf16[8,64,2048]{2,1,0:T(8,128)(2,...) custom-call(s32[2]{0:T(128)} %pad_add_fusion.refs_0_, ...), custom_call_target="tpu_custom_call" | custom-call | flops 3400000000 | bytes 11900000 | tf_op jit(solution)/shard_map/feed/pallas_call | solution.py:42
  76.6 2.6 %collective-permute-start.2 = (bf16[8,64,2048]{2,1,0:T(8,128)(2,1)}, bf16[8,64,2048]{2,1,0:T(8,128)(2,1)}, u32[]{:S(2)}, u32[]{:S(2)}) collective-permute-start(bf16[8,64,2048]{2,1,0:T(8,128)(2,1)} %get-tuple-element.88), channel_id=1, source_target_pairs={{0,2},{2,0},{4,6},{6,4},{8,10},{10,8},{12,14},{14,12},{16,18},{18,... | collective-permute-start | bytes 6291464 | tf_op jit(solution)/shard_map/ppermute | solution.py:659
  82.2 22.2 %back.1 = (bf16[3,512,1024]{2,1,0:T(8,128)(2,1)}, f32[512,1024]{1,0:T(8,128)}, f32[8,1024]{1,0:T(8,128)}, bf16[8,4,32,640]{3,2,1,0:T(8,128)(2,1)}, bf16[8,4,32,6...) custom-call(s32[2]{0:T(128)} %pad_add_fusion.refs_0_, ...), custom_call_target="tpu_custom_call" | custom-call | flops 2000000000 | bytes 7000000 | tf_op jit(solution)/shard_map/back/pallas_call | solution.py:42
  105.1 9.5 %spread.2.refs_13_ = bf16[4096,1024]{1,0:T(8,128)(2,1)} custom-call(s32[1,4]{1,0:T(1,128)} %refs_0_.5, s32[4,1,128]{2,1,0:T(1,128)} %bitcast.89, bf16[4096,1024]{1,0:T(8,128)(2,1)} %bitcast.77, f32[512,128]{1,0:T(8,128)} %get-tuple-element.71.refs_4_.refs_3_.refs_6_, f32[512,1024]{1,0:T(8,128)} %get-tuple-element.72.refs_3_.refs_4_, ...), custom_call_target="tpu_custom_call" | custom-call | flops 800000000 | bytes 2800000 | tf_op jit(solution)/shard_map/spread/pallas_call | solution.py:42
  114.6 11.0 %last.1 = (f32[512,1024]{1,0:T(8,128)}, f32[8,1024]{1,0:T(8,128)}, f32[8,1024]{1,0:T(8,128)}) custom-call(bf16[8,128]{1,0:T(8,128)(2,1)} %bitcast.94, bf16[8,128]{1,0:T(8,128)(2,1)} %bitcast.96, bf16[512,1024]{1,0:T(8,128)(2,1)} %get-tuple-element.76.refs_2_, f32[512,1024]{1,0:T(8,128)} %get-tuple-element.72.refs_3_.refs_4_, ...), custom_call_target="tpu_custom_call" | custom-call | flops 900000000 | bytes 3150000 | tf_op jit(solution)/shard_map/last/pallas_call | solution.py:42
  125.7 2.5 %add_convert_fusion.2 = (bf16[4,64,2048]{2,1,0:T(8,128)(2,1)S(1)}, bf16[4,64,2048]{2,1,0:T(8,128)(2,1)S(1)}) fusion(bf16[8,64,2048]{2,1,0:T(8,128)(2,1)} %collective-permute-done.2, bf16[8,64,2048]{2,1,0:T(8,128)(2,1)S(1)} %copy-done.5), kind=kLoop, calls=%fused_computation.2 | loop fusion | flops 4194304 | bytes 6291456 | tf_op jit(solution)/shard_map/convert_element_type | solution.py:655
  128.2 2.6 %collective-permute-start.9 = (bf16[4,64,2048]{2,1,0:T(8,128)(2,1)S(1)}, bf16[4,64,2048]{2,1,0:T(8,128)(2,1)}, u32[]{:S(2)}, u32[]{:S(2)}) collective-permute-start(bf16[4,64,2048]{2,1,0:T(8,128)(2,1)S(1)} %get-tuple-element.165.refs_4_), channel_id=1, source_target_pairs={{0,4},{2,6},{4,0},{6,2},{8,12},{10,14},{12,8},{14,10},{16,20},{18,... | collective-permute-start | bytes 3145736 | tf_op jit(solution)/shard_map/ppermute | solution.py:659
  130.8 3.7 %fusion.1 = (bf16[4,128,1024]{2,1,0:T(8,128)(2,1)S(1)}, bf16[4,128,1024]{2,1,0:T(8,128)(2,1)}) fusion(bf16[2,4,128,1024]{3,2,1,0:T(8,128)(2,1)} %collective-permute-done.3, bf16[2,4,128,1024]{3,2,1,0:T(8,128)(2,1)S(1)} %copy-done.4), kind=kLoop, calls=%fused_computation.11 | loop fusion | flops 4194304 | bytes 6291456 | tf_op jit(solution)/shard_map/squeeze | solution.py:709
  136.3 2.1 add_convert_fusion.1.refs_6_
  138.5 1.7 collective-permute-start.7
  141.8 3.0 %add_convert_fusion.6 = (bf16[8,4,32,384]{3,2,1,0:T(8,128)(2,1)}, bf16[8,4,32,384]{3,2,1,0:T(8,128)(2,1)}) fusion(bf16[16,4,32,384]{3,2,1,0:T(8,128)(2,1)} %collective-permute-done.6, bf16[16,4,32,384]{3,2,1,0:T(8,128)(2,1)S(1)} %copy-done.7), kind=kLoop, calls=%fused_computation.6 | loop fusion | flops 3145728 | bytes 4718592 | tf_op jit(solution)/shard_map/convert_element_type | solution.py:655
  145.3 10.2 %spread.3 = f32[4096,1024]{1,0:T(8,128)} custom-call(s32[1,4]{1,0:T(1,128)} %refs_0_.5, s32[4,1,128]{2,1,0:T(1,128)} %bitcast.90, bf16[4096,1024]{1,0:T(8,128)(2,1)} %bitcast.75, f32[512,1024]{1,0:T(8,128)} %get-tuple-element.86.refs_3_, bf16[4,64,2048]{2,1,0:T(8,128)(2,1)} %copy-done.2, bf16[4,128,1024]{2,1,0:T(8,128)(2,1)} %get-tuple-element.167.refs_5_, ...), custom_call_target="tpu_custom_call" | custom-call | flops 800000000 | bytes 2800000 | tf_op jit(solution)/shard_map/spread/pallas_call | solution.py:42
  158.1 2.8 %collective-permute-done.8 = bf16[4,128,1024]{2,1,0:T(8,128)(2,1)} collective-permute-done((bf16[4,128,1024]{2,1,0:T(8,128)(2,1)}, bf16[4,128,1024]{2,1,0:T(8,128)(2,1)}, u32[]{:S(2)}, u32[]{:S(2)}) %collective-permute-start.8) | collective-permute-done | bytes 1048608 | tf_op jit(solution)/shard_map/ppermute | solution.py:659
  164.2 12.7 %collective-permute-done.13 = bf16[8,4,32,384]{3,2,1,0:T(8,128)(2,1)} collective-permute-done((bf16[8,4,32,384]{3,2,1,0:T(8,128)(2,1)}, bf16[8,4,32,384]{3,2,1,0:T(8,128)(2,1)}, u32[]{:S(2)}, u32[]{:S(2)}) %collective-permute-start.13) | collective-permute-done | bytes 786464 | tf_op jit(solution)/shard_map/ppermute | solution.py:659
  182.2 2.8 %collective-permute-start.19 = (bf16[64,2048]{1,0:T(8,128)(2,1)S(1)}, bf16[64,2048]{1,0:T(8,128)(2,1)S(1)}, u32[]{:S(2)}, u32[]{:S(2)}) collective-permute-start(bf16[64,2048]{1,0:T(8,128)(2,1)S(1)} %fusion.2), channel_id=1, source_target_pairs={{0,16},{2,18},{4,20},{6,22},{8,24},{10,26},{12,28},{14,30},{16,0},... | collective-permute-start | bytes 786440 | tf_op jit(solution)/shard_map/ppermute | solution.py:659
  185.0 12.1 %collective-permute-done.11 = bf16[2,128,1024]{2,1,0:T(8,128)(2,1)S(1)} collective-permute-done((bf16[2,128,1024]{2,1,0:T(8,128)(2,1)S(1)}, bf16[2,128,1024]{2,1,0:T(8,128)(2,1)S(1)}, u32[]{:S(2)}, u32[]{:S(2)}) %collective-permute-start.11) | collective-permute-done | bytes 524320 | tf_op jit(solution)/shard_map/ppermute | solution.py:659
  197.2 1.7 collective-permute-start.15
  199.7 2.5 %collective-permute-start.17 = (bf16[2,4,32,384]{3,2,1,0:T(8,128)(2,1)}, bf16[2,4,32,384]{3,2,1,0:T(8,128)(2,1)}, u32[]{:S(2)}, u32[]{:S(2)}) collective-permute-start(bf16[2,4,32,384]{3,2,1,0:T(8,128)(2,1)} %get-tuple-element.182), channel_id=1, source_target_pairs={{0,8},{2,10},{4,12},{6,14},{8,0},{10,2},{12,4},{14,6},{16,24},{18,... | collective-permute-start | bytes 589832 | tf_op jit(solution)/shard_map/ppermute | solution.py:659
  203.0 7.9 %collective-permute-done.15 = bf16[128,1024]{1,0:T(8,128)(2,1)S(1)} collective-permute-done((bf16[128,1024]{1,0:T(8,128)(2,1)S(1)}, bf16[128,1024]{1,0:T(8,128)(2,1)S(1)}, u32[]{:S(2)}, u32[]{:S(2)}) %collective-permute-start.15) | collective-permute-done | bytes 262176 | tf_op jit(solution)/shard_map/ppermute | solution.py:659
  214.2 6.7 %collective-permute-done.14 = bf16[2,4,32,640]{3,2,1,0:T(8,128)(2,1)S(1)} collective-permute-done((bf16[2,4,32,640]{3,2,1,0:T(8,128)(2,1)S(1)}, bf16[2,4,32,640]{3,2,1,0:T(8,128)(2,1)S(1)}, u32[]{:S(2)}, u32[]{:S(2)}) %collective-permute-start.14) | collective-permute-done | bytes 327712 | tf_op jit(solution)/shard_map/ppermute | solution.py:659
  221.7 4.7 %all-to-all-start = ((f32[32,3,32]{2,1,0:T(4,128)}), f32[32,3,32]{2,1,0:T(4,128)S(1)}, u32[]{:S(2)}, u32[]{:S(2)}) async-start(f32[32,3,32]{2,1,0:T(4,128)} %copy.28), calls=%async_computation | async-start | bytes 131072 | tf_op jit(solution)/shard_map/all_to_all | solution.py:819
  228.1 7.7 %all-to-all-done = f32[32,3,32]{2,1,0:T(4,128)S(1)} async-done(((f32[32,3,32]{2,1,0:T(4,128)}), f32[32,3,32]{2,1,0:T(4,128)S(1)}, u32[]{:S(2)}, u32[]{:S(2)}) %all-to-all-start) | async-done | bytes 12320 | tf_op jit(solution)/shard_map/all_to_all | solution.py:819
  (84 shorter events, 30.5 us)
Async XLA Ops:
  20.8 4.5 %collective-permute-start = (bf16[2,512,1024]{2,1,0:T(8,128)(2,1)}, bf16[2,512,1024]{2,1,0:T(8,128)(2,1)S(1)}, u32[]{:S(2)}, u32[]{:S(2)}) collective-permute-start(bf16[2,512,1024]{2,1,0:T(8,128)(2,1)} %get-tuple-element.73.refs_1_), channel_id=1, source_target_pairs={{0,1},{1,0},{2,3},{3,2},{4,5},{5,4},{6,7},{7,6},{8,9},{9,8},{10,11... | collective-permute-start | bytes 6291464 | tf_op jit(solution)/shard_map/ppermute | solution.py:663
  76.2 4.7 %collective-permute-start.1 = (bf16[2,512,1024]{2,1,0:T(8,128)(2,1)}, bf16[2,512,1024]{2,1,0:T(8,128)(2,1)S(1)}, u32[]{:S(2)}, u32[]{:S(2)}) collective-permute-start(bf16[2,512,1024]{2,1,0:T(8,128)(2,1)} %get-tuple-element.75), channel_id=1, source_target_pairs={{0,1},{1,0},{2,3},{3,2},{4,5},{5,4},{6,7},{7,6},{8,9},{9,8},{10,11... | collective-permute-start | bytes 6291464 | tf_op jit(solution)/shard_map/ppermute | solution.py:663
  76.6 49.1 %collective-permute-start.2 = (bf16[8,64,2048]{2,1,0:T(8,128)(2,1)}, bf16[8,64,2048]{2,1,0:T(8,128)(2,1)}, u32[]{:S(2)}, u32[]{:S(2)}) collective-permute-start(bf16[8,64,2048]{2,1,0:T(8,128)(2,1)} %get-tuple-element.88), channel_id=1, source_target_pairs={{0,2},{2,0},{4,6},{6,4},{8,10},{10,8},{12,14},{14,12},{16,18},{18,... | collective-permute-start | bytes 6291464 | tf_op jit(solution)/shard_map/ppermute | solution.py:659
  79.3 51.6 %collective-permute-start.3 = (bf16[2,4,128,1024]{3,2,1,0:T(8,128)(2,1)}, bf16[2,4,128,1024]{3,2,1,0:T(8,128)(2,1)}, u32[]{:S(2)}, u32[]{:S(2)}) collective-permute-start(bf16[2,4,128,1024]{3,2,1,0:T(8,128)(2,1)} %get-tuple-element.92), channel_id=1, source_target_pairs={{0,4},{2,6},{4,0},{6,2},{8,12},{10,14},{12,8},{14,10},{16,20},{18,... | collective-permute-start | bytes 6291464 | tf_op jit(solution)/shard_map/ppermute | solution.py:659
  104.4 31.9 %collective-permute-start.4 = (bf16[8,4,32,640]{3,2,1,0:T(8,128)(2,1)}, bf16[8,4,32,640]{3,2,1,0:T(8,128)(2,1)}, u32[]{:S(2)}, u32[]{:S(2)}) collective-permute-start(bf16[8,4,32,640]{3,2,1,0:T(8,128)(2,1)} %get-tuple-element.83.refs_7_), channel_id=1, source_target_pairs={{0,1},{1,0},{2,3},{3,2},{4,5},{5,4},{6,7},{7,6},{8,9},{9,8},{10,11... | collective-permute-start | bytes 3932168 | tf_op jit(solution)/shard_map/ppermute | solution.py:663
  104.6 31.7 %collective-permute-start.5 = (bf16[8,4,32,640]{3,2,1,0:T(8,128)(2,1)}, bf16[8,4,32,640]{3,2,1,0:T(8,128)(2,1)}, u32[]{:S(2)}, u32[]{:S(2)}) collective-permute-start(bf16[8,4,32,640]{3,2,1,0:T(8,128)(2,1)} %get-tuple-element.97), channel_id=1, source_target_pairs={{0,1},{1,0},{2,3},{3,2},{4,5},{5,4},{6,7},{7,6},{8,9},{9,8},{10,11... | collective-permute-start | bytes 3932168 | tf_op jit(solution)/shard_map/ppermute | solution.py:663
  104.9 36.9 %collective-permute-start.6 = (bf16[16,4,32,384]{3,2,1,0:T(8,128)(2,1)}, bf16[16,4,32,384]{3,2,1,0:T(8,128)(2,1)}, u32[]{:S(2)}, u32[]{:S(2)}) collective-permute-start(bf16[16,4,32,384]{3,2,1,0:T(8,128)(2,1)} %get-tuple-element.101), channel_id=1, source_target_pairs={{0,1},{1,0},{2,3},{3,2},{4,5},{5,4},{6,7},{7,6},{8,9},{9,8},{10,11... | collective-permute-start | bytes 4718600 | tf_op jit(solution)/shard_map/ppermute | solution.py:663
  114.6 11.2 %copy-start.5 = (bf16[8,64,2048]{2,1,0:T(8,128)(2,1)S(1)}, bf16[8,64,2048]{2,1,0:T(8,128)(2,1)}, u32[]{:S(2)}) copy-start(bf16[8,64,2048]{2,1,0:T(8,128)(2,1)} %get-tuple-element.89) | copy-start | bytes 6291460
  128.2 27.3 %collective-permute-start.9 = (bf16[4,64,2048]{2,1,0:T(8,128)(2,1)S(1)}, bf16[4,64,2048]{2,1,0:T(8,128)(2,1)}, u32[]{:S(2)}, u32[]{:S(2)}) collective-permute-start(bf16[4,64,2048]{2,1,0:T(8,128)(2,1)S(1)} %get-tuple-element.165.refs_4_), channel_id=1, source_target_pairs={{0,4},{2,6},{4,0},{6,2},{8,12},{10,14},{12,8},{14,10},{16,20},{18,... | collective-permute-start | bytes 3145736 | tf_op jit(solution)/shard_map/ppermute | solution.py:659
  134.6 26.3 %collective-permute-start.8 = (bf16[4,128,1024]{2,1,0:T(8,128)(2,1)}, bf16[4,128,1024]{2,1,0:T(8,128)(2,1)}, u32[]{:S(2)}, u32[]{:S(2)}) collective-permute-start(bf16[4,128,1024]{2,1,0:T(8,128)(2,1)} %get-tuple-element.167.refs_5_), channel_id=1, source_target_pairs={{0,2},{2,0},{4,6},{6,4},{8,10},{10,8},{12,14},{14,12},{16,18},{18,... | collective-permute-start | bytes 3145736 | tf_op jit(solution)/shard_map/ppermute | solution.py:659
  138.5 40.4 %collective-permute-start.7 = (bf16[8,4,32,640]{3,2,1,0:T(8,128)(2,1)S(1)}, bf16[8,4,32,640]{3,2,1,0:T(8,128)(2,1)}, u32[]{:S(2)}, u32[]{:S(2)}) collective-permute-start(bf16[8,4,32,640]{3,2,1,0:T(8,128)(2,1)S(1)} %add_convert_fusion.1.refs_6_), channel_id=1, source_target_pairs={{0,8},{2,10},{4,12},{6,14},{8,0},{10,2},{12,4},{14,6},{16,24},{18,... | collective-permute-start | bytes 3932168 | tf_op jit(solution)/shard_map/ppermute | solution.py:659
  144.9 32.0 %collective-permute-start.13 = (bf16[8,4,32,384]{3,2,1,0:T(8,128)(2,1)}, bf16[8,4,32,384]{3,2,1,0:T(8,128)(2,1)}, u32[]{:S(2)}, u32[]{:S(2)}) collective-permute-start(bf16[8,4,32,384]{3,2,1,0:T(8,128)(2,1)} %get-tuple-element.169.refs_7_), channel_id=1, source_target_pairs={{0,2},{2,0},{4,6},{6,4},{8,10},{10,8},{12,14},{14,12},{16,18},{18,... | collective-permute-start | bytes 2359304 | tf_op jit(solution)/shard_map/ppermute | solution.py:659
  157.1 19.8 %copy-start.3 = (bf16[8,4,32,384]{3,2,1,0:T(8,128)(2,1)S(1)}, bf16[8,4,32,384]{3,2,1,0:T(8,128)(2,1)}, u32[]{:S(2)}) copy-start(bf16[8,4,32,384]{3,2,1,0:T(8,128)(2,1)} %get-tuple-element.115) | copy-start | bytes 2359300
  157.1 25.0 %collective-permute-start.12 = (bf16[2,64,2048]{2,1,0:T(8,128)(2,1)S(1)}, bf16[2,64,2048]{2,1,0:T(8,128)(2,1)S(1)}, u32[]{:S(2)}, u32[]{:S(2)}) collective-permute-start(bf16[2,64,2048]{2,1,0:T(8,128)(2,1)S(1)} %get-tuple-element.173), channel_id=1, source_target_pairs={{0,8},{2,10},{4,12},{6,14},{8,0},{10,2},{12,4},{14,6},{16,24},{18,... | collective-permute-start | bytes 1572872 | tf_op jit(solution)/shard_map/ppermute | solution.py:659
  162.5 34.6 %collective-permute-start.11 = (bf16[2,128,1024]{2,1,0:T(8,128)(2,1)S(1)}, bf16[2,128,1024]{2,1,0:T(8,128)(2,1)S(1)}, u32[]{:S(2)}, u32[]{:S(2)}) collective-permute-start(bf16[2,128,1024]{2,1,0:T(8,128)(2,1)S(1)} %get-tuple-element.175), channel_id=1, source_target_pairs={{0,8},{2,10},{4,12},{6,14},{8,0},{10,2},{12,4},{14,6},{16,24},{18,... | collective-permute-start | bytes 1572872 | tf_op jit(solution)/shard_map/ppermute | solution.py:659
  178.2 20.7 %collective-permute-start.16 = (bf16[4,4,32,384]{3,2,1,0:T(8,128)(2,1)S(1)}, bf16[4,4,32,384]{3,2,1,0:T(8,128)(2,1)S(1)}, u32[]{:S(2)}, u32[]{:S(2)}) collective-permute-start(bf16[4,4,32,384]{3,2,1,0:T(8,128)(2,1)S(1)} %get-tuple-element.176), channel_id=1, source_target_pairs={{0,4},{2,6},{4,0},{6,2},{8,12},{10,14},{12,8},{14,10},{16,20},{18,... | collective-permute-start | bytes 1179656 | tf_op jit(solution)/shard_map/ppermute | solution.py:659
  180.5 31.5 %collective-permute-start.10 = (bf16[4,4,32,640]{3,2,1,0:T(8,128)(2,1)S(1)}, bf16[4,4,32,640]{3,2,1,0:T(8,128)(2,1)S(1)}, u32[]{:S(2)}, u32[]{:S(2)}) collective-permute-start(bf16[4,4,32,640]{3,2,1,0:T(8,128)(2,1)S(1)} %get-tuple-element.171), channel_id=1, source_target_pairs={{0,2},{2,0},{4,6},{6,4},{8,10},{10,8},{12,14},{14,12},{16,18},{18,... | collective-permute-start | bytes 1966088 | tf_op jit(solution)/shard_map/ppermute | solution.py:659
  182.2 20.0 %collective-permute-start.19 = (bf16[64,2048]{1,0:T(8,128)(2,1)S(1)}, bf16[64,2048]{1,0:T(8,128)(2,1)S(1)}, u32[]{:S(2)}, u32[]{:S(2)}) collective-permute-start(bf16[64,2048]{1,0:T(8,128)(2,1)S(1)} %fusion.2), channel_id=1, source_target_pairs={{0,16},{2,18},{4,20},{6,22},{8,24},{10,26},{12,28},{14,30},{16,0},... | collective-permute-start | bytes 786440 | tf_op jit(solution)/shard_map/ppermute | solution.py:659
  197.2 13.7 %collective-permute-start.15 = (bf16[128,1024]{1,0:T(8,128)(2,1)S(1)}, bf16[128,1024]{1,0:T(8,128)(2,1)S(1)}, u32[]{:S(2)}, u32[]{:S(2)}) collective-permute-start(bf16[128,1024]{1,0:T(8,128)(2,1)S(1)} %fusion.3), channel_id=1, source_target_pairs={{0,16},{2,18},{4,20},{6,22},{8,24},{10,26},{12,28},{14,30},{16,0},... | collective-permute-start | bytes 786440 | tf_op jit(solution)/shard_map/ppermute | solution.py:659
  199.7 12.3 %collective-permute-start.17 = (bf16[2,4,32,384]{3,2,1,0:T(8,128)(2,1)}, bf16[2,4,32,384]{3,2,1,0:T(8,128)(2,1)}, u32[]{:S(2)}, u32[]{:S(2)}) collective-permute-start(bf16[2,4,32,384]{3,2,1,0:T(8,128)(2,1)} %get-tuple-element.182), channel_id=1, source_target_pairs={{0,8},{2,10},{4,12},{6,14},{8,0},{10,2},{12,4},{14,6},{16,24},{18,... | collective-permute-start | bytes 589832 | tf_op jit(solution)/shard_map/ppermute | solution.py:659
  203.0 11.0 %collective-permute-start.20 = (f32[32,2048]{1,0:T(8,128)}, f32[32,2048]{1,0:T(8,128)S(1)}, u32[]{:S(2)}, u32[]{:S(2)}) collective-permute-start(f32[32,2048]{1,0:T(8,128)} %constant_dynamic-slice_fusion), channel_id=1, source_target_pairs={{0,1},{1,0},{2,3},{3,2},{4,5},{5,4},{6,7},{7,6},{8,9},{9,8},{10,11... | collective-permute-start | bytes 786440 | tf_op jit(solution)/shard_map/ppermute | solution.py:663
  212.2 8.7 %collective-permute-start.14 = (bf16[2,4,32,640]{3,2,1,0:T(8,128)(2,1)S(1)}, bf16[2,4,32,640]{3,2,1,0:T(8,128)(2,1)S(1)}, u32[]{:S(2)}, u32[]{:S(2)}) collective-permute-start(bf16[2,4,32,640]{3,2,1,0:T(8,128)(2,1)S(1)} %get-tuple-element.178), channel_id=1, source_target_pairs={{0,4},{2,6},{4,0},{6,2},{8,12},{10,14},{12,8},{14,10},{16,20},{18,... | collective-permute-start | bytes 983048 | tf_op jit(solution)/shard_map/ppermute | solution.py:659
  221.0 15.4 %collective-permute-start.18 = (bf16[4,32,1024]{2,1,0:T(8,128)(2,1)S(1)}, bf16[4,32,1024]{2,1,0:T(8,128)(2,1)S(1)}, u32[]{:S(2)}, u32[]{:S(2)}) collective-permute-start(bf16[4,32,1024]{2,1,0:T(8,128)(2,1)S(1)} %pad_maximum_fusion.1), channel_id=1, source_target_pairs={{0,16},{2,18},{4,20},{6,22},{8,24},{10,26},{12,28},{14,30},{16,0},... | collective-permute-start | bytes 786440 | tf_op jit(solution)/shard_map/ppermute | solution.py:659
  221.7 14.1 %all-to-all-start = ((f32[32,3,32]{2,1,0:T(4,128)}), f32[32,3,32]{2,1,0:T(4,128)S(1)}, u32[]{:S(2)}, u32[]{:S(2)}) async-start(f32[32,3,32]{2,1,0:T(4,128)} %copy.28), calls=%async_computation | async-start | bytes 131072 | tf_op jit(solution)/shard_map/all_to_all | solution.py:819
  (10 other events, 43.8 us)

commit v3 on v2

--- a/solution.py
+++ b/solution.py
@@ -11,12 +11,11 @@
 norm_eps = 1e-05
 f32 = jnp.float32
 bf16 = jnp.bfloat16
-VMEM_BYTES = 58 * 1024 * 1024
-
-
-def params(count=1):
+
+
+def params(mebibytes):
     return pltpu.CompilerParams(
-        dimension_semantics=("arbitrary",) * count, vmem_limit_bytes=VMEM_BYTES
+        dimension_semantics=("arbitrary",), vmem_limit_bytes=mebibytes * 1024 * 1024
     )
 
 
@@ -80,18 +79,44 @@
     def __init__(self, sems):
         self.sems, self.count, self.sent = sems, 0, []
 
+    def one(self, source, target):
+        self.count += 1
+        return pltpu.make_async_copy(source, target, self.sems.at[self.count - 1])
+
+    def group(self, turns, pair):
+        first = self.count
+        self.count += turns
+
+        def at(turn):
+            source, target = pair(turn)
+            return pltpu.make_async_copy(source, target, self.sems.at[first + turn])
+
+        return at
+
     def start(self, source, target):
-        copy = pltpu.make_async_copy(source, target, self.sems.at[self.count])
-        self.count += 1
+        copy = self.one(source, target)
         copy.start()
         return copy
 
     def send(self, source, target):
         self.sent.append(self.start(source, target))
+
+    def send_group(self, turns, pair):
+        at = self.group(turns, pair)
+        self.sent += [at(turn) for turn in range(turns)]
+        return at
 
     def finish(self):
         for copy in self.sent:
             copy.wait()
+
+
+def repeat(turns, body):
+    lax.fori_loop(0, turns, lambda turn, carry: body(turn), None)
+
+
+def block_of(turn, size):
+    return pl.ds(pl.multiple_of(turn * size, size), size)
 
 
 HBM = pl.BlockSpec(memory_space=pl.ANY)
@@ -124,15 +149,15 @@
     seqs, _, slots = index_ref.shape
     places, width = tokens.shape[1], tokens.shape[2]
     head = width // H
-    arriving = []
+    token_copy = copies.group(
+        seqs, lambda seq: (tokens_hbm.at[block_of(seq, places)], tokens.at[seq])
+    )
+    cotangent_copy = copies.group(
+        seqs, lambda seq: (cotangent_hbm.at[block_of(seq, places)], cotangent.at[seq])
+    )
     for seq in range(seqs):
-        part = pl.ds(seq * places, places)
-        arriving.append(
-            [
-                copies.start(tokens_hbm.at[part], tokens.at[seq]),
-                copies.start(cotangent_hbm.at[part], cotangent.at[seq]),
-            ]
-        )
+        token_copy(seq).start()
+        cotangent_copy(seq).start()
     weights = [
         copies.start(*pair)
         for pair in (
@@ -140,26 +165,31 @@
         )
     ]
     gain_one, router, gain_two = [flat_row(r) for r in (gain_one_ref, router_ref, gain_two_ref)]
-    slot_id = lax.broadcasted_iota(jnp.int32, (slots, places), 0)
-    place_id = lax.broadcasted_iota(jnp.int32, (slots, places), 1)
-    square = (slots, slots)
-    diagonal = lax.broadcasted_iota(jnp.int32, square, 0) == lax.broadcasted_iota(jnp.int32, square, 1)
-    for seq in range(seqs):
-        rows = slice(seq * slots, (seq + 1) * slots)
+
+    def gather(seq):
+        rows = block_of(seq, slots)
+        slot_id = lax.broadcasted_iota(jnp.int32, (slots, places), 0)
+        place_id = lax.broadcasted_iota(jnp.int32, (slots, places), 1)
+        square = (slots, slots)
+        diagonal = lax.broadcasted_iota(jnp.int32, square, 0) == lax.broadcasted_iota(
+            jnp.int32, square, 1
+        )
         routed = lax.div(lengths_ref[0, seq], 8)
         index = jnp.sum(jnp.where(diagonal, index_ref[seq], 0), axis=1, keepdims=True)
         pick = ((index == place_id) & (slot_id < routed)).astype(bf16)
-        arriving[seq][0].wait()
+        token_copy(seq).wait()
         wide = dot_nn(pick, tokens[seq])
         chosen[rows] = wide.astype(bf16)
         logit = jnp.sum(wide * router, axis=-1, keepdims=True)
         chance = 1.0 / (1.0 + jnp.exp(-logit))
         score[rows] = jnp.broadcast_to(chance, (slots, score.shape[1]))
         lefts[0, rows] = (wide * inv_rms(wide) * gain_one).astype(bf16)
-        arriving[seq][1].wait()
+        cotangent_copy(seq).wait()
         pull = dot_nn(pick, cotangent[seq])
         pulled[rows] = pull.astype(bf16)
         feed[1, rows] = (chance * pull).astype(bf16)
+
+    repeat(seqs, gather)
     copies.send(chosen, chosen_out)
     copies.send(pulled, pulled_out)
     copies.send(score, score_out)
@@ -175,11 +205,13 @@
     weights[2].wait()
     values[...] = dot_nn(first, value_w[...]).astype(bf16)
     copies.send(values, values_out)
-    stack = GROUP * slots
-    row_id = lax.broadcasted_iota(jnp.int32, (stack, slots), 0) % slots
-    col_id = lax.broadcasted_iota(jnp.int32, (stack, slots), 1)
-    for seq in range(seqs):
-        rows = slice(seq * slots, (seq + 1) * slots)
+    probs_copy = copies.send_group(seqs, lambda seq: (probs.at[seq], probs_out.at[seq]))
+
+    def attend(seq):
+        rows = block_of(seq, slots)
+        stack = GROUP * slots
+        row_id = lax.broadcasted_iota(jnp.int32, (stack, slots), 0) % slots
+        col_id = lax.broadcasted_iota(jnp.int32, (stack, slots), 1)
         allowed = (col_id <= row_id) & (col_id < lax.div(lengths_ref[0, seq], 8))
         for g in range(H // GROUP):
             lanes = slice(g * GROUP * head, (g + 1) * GROUP * head)
@@ -190,15 +222,20 @@
             probs[seq, g] = chances
             mixed = dot_nn(chances, values[rows, lanes])
             lefts[1, rows, lanes] = unstacked(mixed, head).astype(bf16)
-        copies.send(probs.at[seq], probs_out.at[seq])
+        probs_copy(seq).start()
+
+    repeat(seqs, attend)
     copies.send(lefts.at[1], lefts_out.at[1])
     weights[3].wait()
     attn[...] = dot_nn(lefts[1], out_w[...])
     copies.send(attn, attn_out)
-    for seq in range(seqs):
-        rows = slice(seq * slots, (seq + 1) * slots)
+
+    def after_attention(seq):
+        rows = block_of(seq, slots)
         after = chosen[rows].astype(f32) + attn[rows]
         feed[0, rows] = (after * inv_rms(after) * gain_two).astype(bf16)
+
+    repeat(seqs, after_attention)
     copies.send(feed.at[0], feed_out.at[0])
     copies.finish()
 
@@ -227,7 +264,7 @@
         + [pltpu.VMEM(*out) for out in outs]
         + [pltpu.SemaphoreType.DMA((2 * seqs + 4 + 11 + seqs,))],
         out_shape=[jax.ShapeDtypeStruct(*out) for out in outs],
-        compiler_params=params(),
+        compiler_params=params(58),
         name="front",
         cost_estimate=cost(18),
     )
@@ -345,11 +382,13 @@
     ]
     chunk = width // nodes
     down_spec = pl.BlockSpec((nodes // 2, chunk, block), lambda i, me: (0, 0, i))
-    rel = lambda i, me: lax.bitwise_xor(i, lax.div(me[1], flat))
-    up_spec = pl.BlockSpec(
-        (flat // 2, 1, size, width),
-        lambda i, me: (0, lax.rem(rel(i, me), 2) * 2 + lax.div(rel(i, me), 2), 0, 0),
-    )
+    near_first = orders[1][-2] < orders[1][-1]
+
+    def up_place(i, me):
+        rel = lax.bitwise_xor(i, lax.div(me[1], flat))
+        return (0, lax.rem(rel, 2) * 2 + lax.div(rel, 2) if near_first else rel, 0, 0)
+
+    up_spec = pl.BlockSpec((flat // 2, 1, size, width), up_place)
     pair = jax.ShapeDtypeStruct((2, rows, width), bf16)
     return call(
         functools.partial(feed_kernel, nodes=nodes, pieces=pieces, orders=orders),
@@ -372,7 +411,7 @@
         out_shape=[pair] * 2
         + [jax.ShapeDtypeStruct((nodes // 2, chunk, hidden // 2), bf16)] * 2
         + [jax.ShapeDtypeStruct((flat // 2, 4, size, width), bf16)] * 2,
-        compiler_params=params(),
+        compiler_params=params(62),
         name="feed",
         cost_estimate=cost(34),
     )
@@ -385,7 +424,7 @@
     send_b_out, keep_b_out,
     chosen, attn, score, pulled, own, other, queries, keys, values, probs, lefts, out_w,
     grads, after_grad, send_gone, send_stay, keep_gone, keep_stay, send_b, keep_b,
-    attn_grad, mix_grad, terms, sems,
+    mix_grad, terms, sems,
     *, nodes, orders,
 ):
     copies = Copies(sems)
@@ -406,26 +445,30 @@
     width = chosen.shape[1]
     head = width // H
     gain = flat_row(gain_ref)
+    gain_out[...] = jnp.zeros_like(gain_out)
     arrive("rows")
-    for seq in range(seqs):
-        rows = slice(seq * slots, (seq + 1) * slots)
+
+    def norm_grad(seq):
+        rows = block_of(seq, slots)
         after = chosen[rows].astype(f32) + attn[rows]
         inv = inv_rms(after)
         normed = after * inv
         arrived = add_low(own[rows], other[rows]).astype(f32)
-        total = fold(arrived * normed)
-        gain_out[...] = total if seq == 0 else gain_out[...] + total
+        gain_out[...] += fold(arrived * normed)
         weighted = arrived * gain
         back = inv * (weighted - normed * jnp.mean(weighted * normed, axis=-1, keepdims=True))
         after_grad[rows] = back
         delta = score[rows, :1] * pulled[rows].astype(f32)
-        attn_grad[rows] = (delta + back).astype(bf16)
+        grads[3, rows] = (delta + back).astype(bf16)
+
+    repeat(seqs, norm_grad)
     copies.send(after_grad, after_out)
     arrive("out")
-    mix_grad[...] = dot_nt(attn_grad[...], out_w[...]).astype(bf16)
+    mix_grad[...] = dot_nt(grads[3], out_w[...]).astype(bf16)
     arrive("heads")
-    for seq in range(seqs):
-        rows = slice(seq * slots, (seq + 1) * slots)
+
+    def attention_grad(seq):
+        rows = block_of(seq, slots)
         for g in range(groups):
             lanes = slice(g * GROUP * head, (g + 1) * GROUP * head)
             chances = probs[seq, g]
@@ -438,19 +481,22 @@
             grads[2, rows, lanes] = dot_tn(chances, stacked_grads).astype(bf16)
             grads[1, rows, lanes] = dot_tn(score_grad, stacked_queries).astype(bf16)
             grads[0, rows, lanes] = unstacked(dot_nn(score_grad, keys[rows, lanes]), head).astype(bf16)
-    copies.send(grads, grads_out)
+
+    repeat(seqs, attention_grad)
+    copies.send(grads.at[pl.ds(0, 3)], grads_out)
     arrive("lefts")
     half, cut = nodes // 2, send_gone.shape[3]
-    outs = (
-        (send_gone, send_gone_out), (keep_gone, keep_gone_out), (send_stay, send_stay_out),
-        (keep_stay, keep_stay_out), (send_b, send_b_out), (keep_b, keep_b_out),
-    )
-    for which in range(4):
-        if which < 3:
-            product = dot_tn(grads[which], lefts[0])
-        else:
-            product = dot_tn(attn_grad[...], lefts[1])
-        terms[...] = (product * 0.125 if which == 0 else product).astype(terms.dtype)
+    outs = [
+        copies.send_group(4, lambda i, held=held, out=out: (held.at[:, i], out.at[:, i]))
+        for held, out in (
+            (send_gone, send_gone_out), (keep_gone, keep_gone_out), (send_stay, send_stay_out),
+            (keep_stay, keep_stay_out), (send_b, send_b_out), (keep_b, keep_b_out),
+        )
+    ]
+
+    def weight_grad(which):
+        product = dot_tn(grads[which], lefts[lax.div(which, 3)])
+        terms[...] = (product * jnp.where(which == 0, 0.125, 1.0)).astype(terms.dtype)
         for rel, kept, sent in own_blocks(me_ref, terms, send_b.shape[2], nodes):
             spot = spot_of(rel, orders[0])
             (keep_stay, keep_gone)[spot // half][spot % half, which] = kept[:, :cut]
@@ -458,8 +504,10 @@
             spot = spot_of(rel, orders[1])
             keep_b[spot, which] = kept[:, cut:]
             send_b[spot, which] = sent[:, cut:]
-        for held, target in outs:
-            copies.send(held.at[:, which], target.at[:, which])
+        for out in outs:
+            out(which).start()
+
+    repeat(4, weight_grad)
     copies.finish()
 
 
@@ -485,14 +533,14 @@
         in_specs=[whole(gain)] + [HBM] * len(fetched),
         out_specs=[HBM, HBM, pl.BlockSpec((8, width), lambda *_: (0, 0))] + [HBM] * 6,
         scratch_shapes=held
-        + [pltpu.VMEM(*out) for out in outs + shapes]
-        + [pltpu.VMEM((rows, width), bf16)] * 2
+        + [pltpu.VMEM(*out) for out in [((4, rows, width), bf16), outs[1]] + shapes]
+        + [pltpu.VMEM((rows, width), bf16)]
         + [pltpu.VMEM((width, width), held_type(size))]
         + [pltpu.SemaphoreType.DMA((len(fetched) + 2 + 24,))],
         out_shape=[jax.ShapeDtypeStruct(*out) for out in outs]
         + [jax.ShapeDtypeStruct((8, width), f32)]
         + [jax.ShapeDtypeStruct(*shape) for shape in shapes],
-        compiler_params=params(),
+        compiler_params=params(62),
         name="back",
         cost_estimate=cost(20),
     )
@@ -502,14 +550,12 @@
     gain_ref, router_ref, chosen_hbm, attn_hbm, own_hbm, other_hbm, score_hbm, pulled_hbm, after_hbm,
     grads_hbm, query_hbm, key_hbm, value_hbm,
     chosen_grad_out, gain_out, router_out,
-    chosen, attn, own, other, score, pulled, after_grad, grads, query_w, key_w, value_w,
-    first_grad, chosen_grad, sems,
+    chosen, attn, own, other, score, pulled, after_grad, grads, weights, first_grad, chosen_grad, sems,
 ):
     copies = Copies(sems)
-    weights = ((query_hbm, query_w), (key_hbm, key_w), (value_hbm, value_w))
     pairs = [
-        (copies.start(grads_hbm.at[i], grads.at[i]), copies.start(*weight))
-        for i, weight in enumerate(weights)
+        (copies.start(grads_hbm.at[i], grads.at[i]), copies.start(weight, weights.at[i]))
+        for i, weight in enumerate((query_hbm, key_hbm, value_hbm))
     ]
     others = [
         copies.start(*pair)
@@ -519,20 +565,27 @@
         )
     ]
     gain, router = flat_row(gain_ref), flat_row(router_ref)
+    gain_out[...] = jnp.zeros_like(gain_out)
+    router_out[...] = jnp.zeros_like(router_out)
     for i, pair in enumerate(pairs):
         for copy in pair:
             copy.wait()
-        product = dot_nt(grads[i], weights[i][1][...])
+        product = dot_nt(grads[i], weights[i])
         if i == 0:
             first_grad[...] = product * 0.125
         else:
             first_grad[...] += product
     for copy in others:
         copy.wait()
-    rows = chosen.shape[0]
-    block = rows // 4
-    for i in range(4):
-        part = slice(i * block, (i + 1) * block)
+    turns = 4
+    block = chosen.shape[0] // turns
+    out = copies.send_group(
+        turns,
+        lambda i: (chosen_grad.at[block_of(i, block)], chosen_grad_out.at[block_of(i, block)]),
+    )
+
+    def rest(i):
+        part = block_of(i, block)
         wide = chosen[part].astype(f32)
         chance = score[part, :1]
         branch = attn[part] + add_low(own[part], other[part]).astype(f32)
@@ -547,10 +600,11 @@
             + after_grad[part]
             + logit_grad * router
         )
-        copies.send(chosen_grad.at[pl.ds(i * block, block)], chosen_grad_out.at[pl.ds(i * block, block)])
-        gain_sum, router_sum = fold(arrived * normed), fold(logit_grad * wide)
-        gain_out[...] = gain_sum if i == 0 else gain_out[...] + gain_sum
-        router_out[...] = router_sum if i == 0 else router_out[...] + router_sum
+        out(i).start()
+        gain_out[...] += fold(arrived * normed)
+        router_out[...] += fold(logit_grad * wide)
+
+    repeat(turns, rest)
     copies.finish()
 
 
@@ -559,8 +613,9 @@
 ):
     rows, width = chosen.shape
     fetched = [chosen, attn, own, other, score, pulled, after_grad, grads, wq, wk, wv]
-    held = [pltpu.VMEM(array.shape, array.dtype) for array in fetched]
+    held = [pltpu.VMEM(array.shape, array.dtype) for array in fetched[:-3]]
     held[2] = held[3] = pltpu.VMEM((rows, width), bf16)
+    held.append(pltpu.VMEM((3, width, width), bf16))
     sums = pl.BlockSpec((8, width), lambda *_: (0, 0))
     return call(
         last_kernel,
@@ -574,7 +629,7 @@
         + [pltpu.SemaphoreType.DMA((17,))],
         out_shape=[jax.ShapeDtypeStruct((rows, width), f32)]
         + [jax.ShapeDtypeStruct((8, width), f32)] * 2,
-        compiler_params=params(),
+        compiler_params=params(58),
         name="last",
         cost_estimate=cost(9),
     )
@@ -586,23 +641,31 @@
     copies = Copies(sems)
     seqs, _, slots = index_ref.shape
     count = base.shape[1]
-    arriving = []
+
+    def delta_copy(source, target):
+        top = source.shape[0] - 1
+        place = lambda row: source.at[top, row] if len(source.shape) == 3 else source.at[row]
+        return copies.group(
+            seqs, lambda seq: (place(block_of(seq, slots)), target.at[block_of(seq, slots)])
+        )
+
+    delta_copies = [delta_copy(*pair) for pair in zip(deltas_hbm, held)]
+    base_copy = copies.group(
+        seqs * pieces, lambda at: (base_hbm.at[block_of(at, count)], base.at[at])
+    )
     for seq in range(seqs):
-        row = pl.ds(seq * slots, slots)
-        steps = [
-            copies.start(
-                source.at[source.shape[0] - 1, row] if len(source.shape) == 3 else source.at[row],
-                target.at[row],
-            )
-            for source, target in zip(deltas_hbm, held)
-        ]
-        for piece in range(seq * pieces, (seq + 1) * pieces):
-            steps.append(copies.start(base_hbm.at[pl.ds(piece * count, count)], base.at[piece]))
-        arriving.append(steps)
-    for seq in range(seqs):
-        rows = slice(seq * slots, (seq + 1) * slots)
-        for copy in arriving[seq][:deltas]:
-            copy.wait()
+        for copy in delta_copies:
+            copy(seq).start()
+        for piece in range(pieces):
+            base_copy(seq * pieces + piece).start()
+    out_copy = copies.send_group(
+        seqs * pieces, lambda at: (out.at[at], out_hbm.at[block_of(at, count)])
+    )
+
+    def one(seq):
+        rows = block_of(seq, slots)
+        for copy in delta_copies:
+            copy(seq).wait()
         if deltas == 1:
             delta = held[0][rows]
         else:
@@ -617,10 +680,12 @@
             place = piece * count + lax.broadcasted_iota(jnp.int32, (count, slots), 0)
             pick = ((index_ref[seq] == place) & live).astype(bf16)
             at = seq * pieces + piece
-            arriving[seq][deltas + piece].wait()
+            base_copy(at).wait()
             added = dot_nn(jnp.concatenate([pick, pick], axis=1), both)
             out[at] = (base[at].astype(f32) + added).astype(out.dtype)
-            copies.send(out.at[at], out_hbm.at[pl.ds(at * count, count)])
+            out_copy(at).start()
+
+    repeat(seqs, one)
     copies.finish()
 
 
@@ -645,7 +710,7 @@
             pltpu.SemaphoreType.DMA((2 * steps + len(deltas) * seqs,)),
         ],
         out_shape=jax.ShapeDtypeStruct((rows, width), dtype),
-        compiler_params=params(),
+        compiler_params=params(58),
         name="spread",
         cost_estimate=cost(8),
     )
@@ -721,7 +786,9 @@
     def step(self, count=1, after=()):
         sent = []
         for _ in range(count):
-            sent = [part.step(after) for part in self.parts]
+            sent = []
+            for part in self.parts:
+                sent.append(part.step([*after, *sent]))
         return sent
 
     def final(self, after=()):
@@ -776,8 +843,8 @@
     feed_other = swap_cores(feed_own)
     order = lambda names: link_order(nodes, names)
     span = len(order("x"))
-    down_order, up_order = order("xynf"), order("yxnf")
-    square_orders = [order("nxyf"), order("xynf")]
+    down_order, up_order = order("nxfy"), order("xynf")
+    square_orders = [order("nxyf"), order("yxnf")]
     own_sums, other_sums, *terms = feed(
         me, feed_own, feed_other, w_up, w_down, nodes, [down_order, up_order]
     )
@@ -786,7 +853,7 @@
     up = Chain([Part.halved(*terms[2:], up_order, nodes)])
     grads, after_grad, gain_mlp_sum, *square_terms = back(
         me, chosen, attn_out, score, pulled, own_sums, got_sums, vectors[2], queries, keys, values, probs,
-        lefts, w_out, nodes, square_orders, width * 5 // 8,
+        lefts, w_out, nodes, square_orders, width // 2,
     )
     square = Chain(
         [

time: 240 us -> 210 us (0.88)
  waiting for transfers between devices: 53.6 us -> 42.2 us
  Pallas kernels: 122 us -> 111 us
  local copies, waits for them, and re-layouts: 8.27 us -> 4.86 us
    ppermute x15, waiting for transfers between devices: 42.4 us -> 29.8 us  [swap_nodes(): lax.ppermute(values, 'seq', [(i, i ^ 1 << bit) for i in range(nodes)])]
    pallas_call x6, Pallas kernels: 122 us -> 111 us  [call(): pl.pallas_call(body, grid_spec=grid, **rest)(*scalars, *arrays, *waits)]
    unnamed x27 -> x23, local copies, waits for them, and re-layouts: 3.84 us -> 1.14 us
    squeeze x5 -> x4, other arithmetic: 4.94 us -> 3.81 us  [halve(): half[0]]
  transfers between devices with their start and end apart: 22 -> 22, of which waited for: 8 -> 10; matrix products, arithmetic and copies ran while one was open for 11% -> 12% of each run, Pallas kernels for 22% -> 25%
where the time goes in v3:
time: 210 us; the launch traced here: 209 us
  Pallas kernels  111 us (53%)
  waiting for transfers between devices  42.2 us (20%)
  starting transfers between devices  28.6 us (14%)
  other arithmetic  21.4 us (10%)
  local copies, waits for them, and re-layouts  4.86 us (2%)
    pallas_call x6, Pallas kernels, call(): pl.pallas_call(body, grid_spec=grid, **rest)(*scalars, *arrays, *waits)  111 us
    ppermute x15, waiting for transfers between devices, swap_nodes(): lax.ppermute(values, 'seq', [(i, i ^ 1 << bit) for i in range(nodes)])  29.8 us
    ppermute x15, starting transfers between devices, swap_nodes(): lax.ppermute(values, 'seq', [(i, i ^ 1 << bit) for i in range(nodes)])  23 us
    convert_element_type x10, other arithmetic, add_low(): return (left.astype(f32) + right.astype(f32)).astype(bf16)  16.6 us
    all_to_all x1, waiting for transfers between devices, on_device(): lax.all_to_all(sums, ('seq', 'dp'), 0, 0, tiled=True)  8.77 us
  transfers between devices with their start and end apart: 22, of which 10 were waited for; matrix products, arithmetic and copies ran while one was open for 12% of the time, Pallas kernels for 25%

profile of v3, /device:TPU:0, one launch (start us, length us, event | category | flops | bytes accessed | tf_op | source)
XLA Modules:
  0.0 209.3 jit_solution(1294638929798248201)
XLA Ops:
  0.6 21.8 %front.1 = (bf16[512,1024]{1,0:T(8,128)(2,1)}, bf16[2,512,1024]{2,1,0:T(8,128)(2,1)}, bf16[512,1024]{1,0:T(8,128)(2,1)}, bf16[512,1024]{1,0:T(8,128)(2,1)}, bf16...) custom-call(s32[1,4]{1,0:T(1,128)} %refs_0_.5, ...), custom_call_target="tpu_custom_call" | custom-call | flops 1800000000 | bytes 6300000 | tf_op jit(solution)/shard_map/front/pallas_call | solution.py:41
  23.5 3.5 %collective-permute-done.refs_2_ = bf16[2,512,1024]{2,1,0:T(8,128)(2,1)} collective-permute-done((bf16[2,512,1024]{2,1,0:T(8,128)(2,1)}, bf16[2,512,1024]{2,1,0:T(8,128)(2,1)}, u32[]{:S(2)}, u32[]{:S(2)}) %collective-permute-start) | collective-permute-done | bytes 2097184 | tf_op jit(solution)/shard_map/ppermute | solution.py:728
  27.1 36.7 %feed.1 = (bf16[2,512,1024]{2,1,0:T(8,128)(2,1)}, bf16[2,512,1024]{2,1,0:T(8,128)(2,1)}, bf16[8,64,2048]{2,1,0:T(8,128)(2,1)}, bf16[8,64,2048]{2,1,0:T(8,128)(2,...) custom-call(s32[2]{0:T(128)} %pad_add_fusion.refs_0_, ...), custom_call_target="tpu_custom_call" | custom-call | flops 3400000000 | bytes 11900000 | tf_op jit(solution)/shard_map/feed/pallas_call | solution.py:41
  64.2 2.7 %collective-permute-start.2 = (bf16[8,64,2048]{2,1,0:T(8,128)(2,1)}, bf16[8,64,2048]{2,1,0:T(8,128)(2,1)}, u32[]{:S(2)}, u32[]{:S(2)}) collective-permute-start(bf16[8,64,2048]{2,1,0:T(8,128)(2,1)} %get-tuple-element.88), channel_id=1, source_target_pairs={{0,8},{2,10},{4,12},{6,14},{8,0},{10,2},{12,4},{14,6},{16,24},{18,... | collective-permute-start | bytes 6291464 | tf_op jit(solution)/shard_map/ppermute | solution.py:724
  68.3 22.4 %back.1 = (bf16[3,512,1024]{2,1,0:T(8,128)(2,1)}, f32[512,1024]{1,0:T(8,128)}, f32[8,1024]{1,0:T(8,128)}, bf16[8,4,32,512]{3,2,1,0:T(8,128)(2,1)}, bf16[8,4,32,5...) custom-call(s32[2]{0:T(128)} %pad_add_fusion.refs_0_, ...), custom_call_target="tpu_custom_call" | custom-call | flops 2000000000 | bytes 7000000 | tf_op jit(solution)/shard_map/back/pallas_call | solution.py:41
  91.7 9.5 %spread.2.refs_13_ = bf16[4096,1024]{1,0:T(8,128)(2,1)} custom-call(s32[1,4]{1,0:T(1,128)} %refs_0_.5, s32[4,1,128]{2,1,0:T(1,128)} %bitcast.89, bf16[4096,1024]{1,0:T(8,128)(2,1)} %bitcast.77, f32[512,128]{1,0:T(8,128)} %get-tuple-element.71.refs_4_.refs_3_.refs_6_, f32[512,1024]{1,0:T(8,128)} %get-tuple-element.72.refs_3_.refs_4_, ...), custom_call_target="tpu_custom_call" | custom-call | flops 800000000 | bytes 2800000 | tf_op jit(solution)/shard_map/spread/pallas_call | solution.py:41
  101.2 10.7 %last.1 = (f32[512,1024]{1,0:T(8,128)}, f32[8,1024]{1,0:T(8,128)}, f32[8,1024]{1,0:T(8,128)}) custom-call(bf16[8,128]{1,0:T(8,128)(2,1)} %bitcast.94, bf16[8,128]{1,0:T(8,128)(2,1)} %bitcast.96, bf16[512,1024]{1,0:T(8,128)(2,1)} %get-tuple-element.76.refs_2_, f32[512,1024]{1,0:T(8,128)} %get-tuple-element.72.refs_3_.refs_4_, ...), custom_call_target="tpu_custom_call" | custom-call | flops 900000000 | bytes 3150000 | tf_op jit(solution)/shard_map/last/pallas_call | solution.py:41
  113.3 2.6 %add_convert_fusion.1 = (bf16[4,64,2048]{2,1,0:T(8,128)(2,1)S(1)}, bf16[4,64,2048]{2,1,0:T(8,128)(2,1)S(1)}) fusion(bf16[8,64,2048]{2,1,0:T(8,128)(2,1)} %collective-permute-done.2, bf16[8,64,2048]{2,1,0:T(8,128)(2,1)S(1)} %copy-done.5), kind=kLoop, calls=%fused_computation.1 | loop fusion | flops 4194304 | bytes 6291456 | tf_op jit(solution)/shard_map/convert_element_type | solution.py:720
  115.9 1.8 collective-permute-start.9
  117.7 3.5 %fusion.1 = (bf16[4,128,1024]{2,1,0:T(8,128)(2,1)S(1)}, bf16[4,128,1024]{2,1,0:T(8,128)(2,1)}) fusion(bf16[2,4,128,1024]{3,2,1,0:T(8,128)(2,1)} %collective-permute-done.3, bf16[2,4,128,1024]{3,2,1,0:T(8,128)(2,1)S(1)} %copy-done.4), kind=kLoop, calls=%fused_computation.9 | loop fusion | flops 4194304 | bytes 6291456 | tf_op jit(solution)/shard_map/squeeze | solution.py:774
  121.3 1.6 collective-permute-start.8
  123.0 2.0 add_convert_fusion.5.refs_6_
  128.3 3.8 %add_convert_fusion = (bf16[8,4,32,512]{3,2,1,0:T(8,128)(2,1)}, bf16[8,4,32,512]{3,2,1,0:T(8,128)(2,1)}) fusion(bf16[16,4,32,512]{3,2,1,0:T(8,128)(2,1)} %collective-permute-done.6, bf16[16,4,32,512]{3,2,1,0:T(8,128)(2,1)S(1)} %copy-done.3), kind=kLoop, calls=%fused_computation | loop fusion | flops 4194304 | bytes 6291456 | tf_op jit(solution)/shard_map/convert_element_type | solution.py:720
  132.5 10.2 %spread.3 = f32[4096,1024]{1,0:T(8,128)} custom-call(s32[1,4]{1,0:T(1,128)} %refs_0_.5, s32[4,1,128]{2,1,0:T(1,128)} %bitcast.90, bf16[4096,1024]{1,0:T(8,128)(2,1)} %bitcast.75, f32[512,1024]{1,0:T(8,128)} %get-tuple-element.86.refs_3_, bf16[4,64,2048]{2,1,0:T(8,128)(2,1)} %copy-done.1, bf16[4,128,1024]{2,1,0:T(8,128)(2,1)} %get-tuple-element.167.refs_5_, ...), custom_call_target="tpu_custom_call" | custom-call | flops 800000000 | bytes 2800000 | tf_op jit(solution)/shard_map/spread/pallas_call | solution.py:41
  144.3 2.8 %collective-permute-start.12 = (bf16[2,64,2048]{2,1,0:T(8,128)(2,1)S(1)}, bf16[2,64,2048]{2,1,0:T(8,128)(2,1)S(1)}, u32[]{:S(2)}, u32[]{:S(2)}) collective-permute-start(bf16[2,64,2048]{2,1,0:T(8,128)(2,1)S(1)} %get-tuple-element.173), channel_id=1, source_target_pairs={{0,16},{2,18},{4,20},{6,22},{8,24},{10,26},{12,28},{14,30},{16,0},... | collective-permute-start | bytes 1572872 | tf_op jit(solution)/shard_map/ppermute | solution.py:724
  150.8 5.4 %collective-permute-done.7 = bf16[8,4,32,512]{3,2,1,0:T(8,128)(2,1)} collective-permute-done((bf16[8,4,32,512]{3,2,1,0:T(8,128)(2,1)S(1)}, bf16[8,4,32,512]{3,2,1,0:T(8,128)(2,1)}, u32[]{:S(2)}, u32[]{:S(2)}) %collective-permute-start.7) | collective-permute-done | bytes 1048608 | tf_op jit(solution)/shard_map/ppermute | solution.py:724
  158.3 10.3 %collective-permute-done.13 = bf16[8,4,32,512]{3,2,1,0:T(8,128)(2,1)} collective-permute-done((bf16[8,4,32,512]{3,2,1,0:T(8,128)(2,1)}, bf16[8,4,32,512]{3,2,1,0:T(8,128)(2,1)}, u32[]{:S(2)}, u32[]{:S(2)}) %collective-permute-start.13) | collective-permute-done | bytes 1048608 | tf_op jit(solution)/shard_map/ppermute | solution.py:724
  171.0 1.7 collective-permute-start.19
  172.7 2.6 %collective-permute-start.15 = (bf16[128,1024]{1,0:T(8,128)(2,1)S(1)}, bf16[128,1024]{1,0:T(8,128)(2,1)S(1)}, u32[]{:S(2)}, u32[]{:S(2)}) collective-permute-start(bf16[128,1024]{1,0:T(8,128)(2,1)S(1)} %fusion.3), channel_id=1, source_target_pairs={{0,16},{2,18},{4,20},{6,22},{8,24},{10,26},{12,28},{14,30},{16,0},... | collective-permute-start | bytes 786440 | tf_op jit(solution)/shard_map/ppermute | solution.py:724
  176.0 3.7 %collective-permute-done.19 = bf16[64,2048]{1,0:T(8,128)(2,1)S(1)} collective-permute-done((bf16[64,2048]{1,0:T(8,128)(2,1)S(1)}, bf16[64,2048]{1,0:T(8,128)(2,1)S(1)}, u32[]{:S(2)}, u32[]{:S(2)}) %collective-permute-start.19) | collective-permute-done | bytes 262176 | tf_op jit(solution)/shard_map/ppermute | solution.py:724
  179.9 2.9 %collective-permute-done.16 = bf16[4,4,32,512]{3,2,1,0:T(8,128)(2,1)S(1)} collective-permute-done((bf16[4,4,32,512]{3,2,1,0:T(8,128)(2,1)S(1)}, bf16[4,4,32,512]{3,2,1,0:T(8,128)(2,1)S(1)}, u32[]{:S(2)}, u32[]{:S(2)}) %collective-permute-start.16) | collective-permute-done | bytes 524320 | tf_op jit(solution)/shard_map/ppermute | solution.py:724
  187.1 4.2 %collective-permute-done.17 = bf16[2,4,32,512]{3,2,1,0:T(8,128)(2,1)S(1)} collective-permute-done((bf16[2,4,32,512]{3,2,1,0:T(8,128)(2,1)S(1)}, bf16[2,4,32,512]{3,2,1,0:T(8,128)(2,1)S(1)}, u32[]{:S(2)}, u32[]{:S(2)}) %collective-permute-start.17) | collective-permute-done | bytes 262176 | tf_op jit(solution)/shard_map/ppermute | solution.py:724
  193.8 3.6 %all-to-all-start = ((f32[32,3,32]{2,1,0:T(4,128)}), f32[32,3,32]{2,1,0:T(4,128)S(1)}, u32[]{:S(2)}, u32[]{:S(2)}) async-start(f32[32,3,32]{2,1,0:T(4,128)} %copy.28), calls=%async_computation | async-start | bytes 131072 | tf_op jit(solution)/shard_map/all_to_all | solution.py:886
  199.1 8.8 %all-to-all-done = f32[32,3,32]{2,1,0:T(4,128)S(1)} async-done(((f32[32,3,32]{2,1,0:T(4,128)}), f32[32,3,32]{2,1,0:T(4,128)S(1)}, u32[]{:S(2)}, u32[]{:S(2)}) %all-to-all-start) | async-done | bytes 12320 | tf_op jit(solution)/shard_map/all_to_all | solution.py:886
  (79 shorter events, 29.6 us)
Async XLA Ops:
  22.4 4.7 %collective-permute-start = (bf16[2,512,1024]{2,1,0:T(8,128)(2,1)}, bf16[2,512,1024]{2,1,0:T(8,128)(2,1)}, u32[]{:S(2)}, u32[]{:S(2)}) collective-permute-start(bf16[2,512,1024]{2,1,0:T(8,128)(2,1)} %get-tuple-element.73.refs_1_), channel_id=1, source_target_pairs={{0,1},{1,0},{2,3},{3,2},{4,5},{5,4},{6,7},{7,6},{8,9},{9,8},{10,11... | collective-permute-start | bytes 6291464 | tf_op jit(solution)/shard_map/ppermute | solution.py:728
  63.8 4.6 %collective-permute-start.1 = (bf16[2,512,1024]{2,1,0:T(8,128)(2,1)}, bf16[2,512,1024]{2,1,0:T(8,128)(2,1)}, u32[]{:S(2)}, u32[]{:S(2)}) collective-permute-start(bf16[2,512,1024]{2,1,0:T(8,128)(2,1)} %get-tuple-element.75), channel_id=1, source_target_pairs={{0,1},{1,0},{2,3},{3,2},{4,5},{5,4},{6,7},{7,6},{8,9},{9,8},{10,11... | collective-permute-start | bytes 6291464 | tf_op jit(solution)/shard_map/ppermute | solution.py:728
  64.2 49.1 %collective-permute-start.2 = (bf16[8,64,2048]{2,1,0:T(8,128)(2,1)}, bf16[8,64,2048]{2,1,0:T(8,128)(2,1)}, u32[]{:S(2)}, u32[]{:S(2)}) collective-permute-start(bf16[8,64,2048]{2,1,0:T(8,128)(2,1)} %get-tuple-element.88), channel_id=1, source_target_pairs={{0,8},{2,10},{4,12},{6,14},{8,0},{10,2},{12,4},{14,6},{16,24},{18,... | collective-permute-start | bytes 6291464 | tf_op jit(solution)/shard_map/ppermute | solution.py:724
  66.9 50.8 %collective-permute-start.3 = (bf16[2,4,128,1024]{3,2,1,0:T(8,128)(2,1)}, bf16[2,4,128,1024]{3,2,1,0:T(8,128)(2,1)}, u32[]{:S(2)}, u32[]{:S(2)}) collective-permute-start(bf16[2,4,128,1024]{3,2,1,0:T(8,128)(2,1)} %get-tuple-element.92), channel_id=1, source_target_pairs={{0,2},{2,0},{4,6},{6,4},{8,10},{10,8},{12,14},{14,12},{16,18},{18,... | collective-permute-start | bytes 6291464 | tf_op jit(solution)/shard_map/ppermute | solution.py:724
  90.7 37.5 %collective-permute-start.6 = (bf16[16,4,32,512]{3,2,1,0:T(8,128)(2,1)}, bf16[16,4,32,512]{3,2,1,0:T(8,128)(2,1)}, u32[]{:S(2)}, u32[]{:S(2)}) collective-permute-start(bf16[16,4,32,512]{3,2,1,0:T(8,128)(2,1)} %get-tuple-element.101), channel_id=1, source_target_pairs={{0,1},{1,0},{2,3},{3,2},{4,5},{5,4},{6,7},{7,6},{8,9},{9,8},{10,11... | collective-permute-start | bytes 6291464 | tf_op jit(solution)/shard_map/ppermute | solution.py:728
  91.2 31.8 %collective-permute-start.4 = (bf16[8,4,32,512]{3,2,1,0:T(8,128)(2,1)}, bf16[8,4,32,512]{3,2,1,0:T(8,128)(2,1)}, u32[]{:S(2)}, u32[]{:S(2)}) collective-permute-start(bf16[8,4,32,512]{3,2,1,0:T(8,128)(2,1)} %get-tuple-element.83.refs_7_), channel_id=1, source_target_pairs={{0,1},{1,0},{2,3},{3,2},{4,5},{5,4},{6,7},{7,6},{8,9},{9,8},{10,11... | collective-permute-start | bytes 3145736 | tf_op jit(solution)/shard_map/ppermute | solution.py:728
  91.3 31.7 %collective-permute-start.5 = (bf16[8,4,32,512]{3,2,1,0:T(8,128)(2,1)}, bf16[8,4,32,512]{3,2,1,0:T(8,128)(2,1)}, u32[]{:S(2)}, u32[]{:S(2)}) collective-permute-start(bf16[8,4,32,512]{3,2,1,0:T(8,128)(2,1)} %get-tuple-element.97), channel_id=1, source_target_pairs={{0,1},{1,0},{2,3},{3,2},{4,5},{5,4},{6,7},{7,6},{8,9},{9,8},{10,11... | collective-permute-start | bytes 3145736 | tf_op jit(solution)/shard_map/ppermute | solution.py:728
  101.2 12.2 %copy-start.5 = (bf16[8,64,2048]{2,1,0:T(8,128)(2,1)S(1)}, bf16[8,64,2048]{2,1,0:T(8,128)(2,1)}, u32[]{:S(2)}) copy-start(bf16[8,64,2048]{2,1,0:T(8,128)(2,1)} %get-tuple-element.89) | copy-start | bytes 6291460
  115.9 26.8 %collective-permute-start.9 = (bf16[4,64,2048]{2,1,0:T(8,128)(2,1)S(1)}, bf16[4,64,2048]{2,1,0:T(8,128)(2,1)}, u32[]{:S(2)}, u32[]{:S(2)}) collective-permute-start(bf16[4,64,2048]{2,1,0:T(8,128)(2,1)S(1)} %get-tuple-element.165.refs_4_), channel_id=1, source_target_pairs={{0,2},{2,0},{4,6},{6,4},{8,10},{10,8},{12,14},{14,12},{16,18},{18,... | collective-permute-start | bytes 3145736 | tf_op jit(solution)/shard_map/ppermute | solution.py:724
  121.3 26.4 %collective-permute-start.8 = (bf16[4,128,1024]{2,1,0:T(8,128)(2,1)}, bf16[4,128,1024]{2,1,0:T(8,128)(2,1)}, u32[]{:S(2)}, u32[]{:S(2)}) collective-permute-start(bf16[4,128,1024]{2,1,0:T(8,128)(2,1)} %get-tuple-element.167.refs_5_), channel_id=1, source_target_pairs={{0,4},{2,6},{4,0},{6,2},{8,12},{10,14},{12,8},{14,10},{16,20},{18,... | collective-permute-start | bytes 3145736 | tf_op jit(solution)/shard_map/ppermute | solution.py:724
  125.1 31.1 %collective-permute-start.7 = (bf16[8,4,32,512]{3,2,1,0:T(8,128)(2,1)S(1)}, bf16[8,4,32,512]{3,2,1,0:T(8,128)(2,1)}, u32[]{:S(2)}, u32[]{:S(2)}) collective-permute-start(bf16[8,4,32,512]{3,2,1,0:T(8,128)(2,1)S(1)} %add_convert_fusion.5.refs_6_), channel_id=1, source_target_pairs={{0,8},{2,10},{4,12},{6,14},{8,0},{10,2},{12,4},{14,6},{16,24},{18,... | collective-permute-start | bytes 3145736 | tf_op jit(solution)/shard_map/ppermute | solution.py:724
  132.0 36.6 %collective-permute-start.13 = (bf16[8,4,32,512]{3,2,1,0:T(8,128)(2,1)}, bf16[8,4,32,512]{3,2,1,0:T(8,128)(2,1)}, u32[]{:S(2)}, u32[]{:S(2)}) collective-permute-start(bf16[8,4,32,512]{3,2,1,0:T(8,128)(2,1)} %get-tuple-element.169.refs_7_), channel_id=1, source_target_pairs={{0,4},{2,6},{4,0},{6,2},{8,12},{10,14},{12,8},{14,10},{16,20},{18,... | collective-permute-start | bytes 3145736 | tf_op jit(solution)/shard_map/ppermute | solution.py:724
  144.3 26.6 %collective-permute-start.12 = (bf16[2,64,2048]{2,1,0:T(8,128)(2,1)S(1)}, bf16[2,64,2048]{2,1,0:T(8,128)(2,1)S(1)}, u32[]{:S(2)}, u32[]{:S(2)}) collective-permute-start(bf16[2,64,2048]{2,1,0:T(8,128)(2,1)S(1)} %get-tuple-element.173), channel_id=1, source_target_pairs={{0,16},{2,18},{4,20},{6,22},{8,24},{10,26},{12,28},{14,30},{16,0},... | collective-permute-start | bytes 1572872 | tf_op jit(solution)/shard_map/ppermute | solution.py:724
  149.2 19.4 %copy-start.2 = (bf16[8,4,32,512]{3,2,1,0:T(8,128)(2,1)S(1)}, bf16[8,4,32,512]{3,2,1,0:T(8,128)(2,1)}, u32[]{:S(2)}) copy-start(bf16[8,4,32,512]{3,2,1,0:T(8,128)(2,1)} %get-tuple-element.115) | copy-start | bytes 3145732
  149.3 23.4 %collective-permute-start.11 = (bf16[2,128,1024]{2,1,0:T(8,128)(2,1)S(1)}, bf16[2,128,1024]{2,1,0:T(8,128)(2,1)S(1)}, u32[]{:S(2)}, u32[]{:S(2)}) collective-permute-start(bf16[2,128,1024]{2,1,0:T(8,128)(2,1)S(1)} %get-tuple-element.175), channel_id=1, source_target_pairs={{0,8},{2,10},{4,12},{6,14},{8,0},{10,2},{12,4},{14,6},{16,24},{18,... | collective-permute-start | bytes 1572872 | tf_op jit(solution)/shard_map/ppermute | solution.py:724
  157.8 17.6 %collective-permute-start.10 = (bf16[4,4,32,512]{3,2,1,0:T(8,128)(2,1)S(1)}, bf16[4,4,32,512]{3,2,1,0:T(8,128)(2,1)S(1)}, u32[]{:S(2)}, u32[]{:S(2)}) collective-permute-start(bf16[4,4,32,512]{3,2,1,0:T(8,128)(2,1)S(1)} %get-tuple-element.171), channel_id=1, source_target_pairs={{0,2},{2,0},{4,6},{6,4},{8,10},{10,8},{12,14},{14,12},{16,18},{18,... | collective-permute-start | bytes 1572872 | tf_op jit(solution)/shard_map/ppermute | solution.py:724
  170.2 12.5 %collective-permute-start.16 = (bf16[4,4,32,512]{3,2,1,0:T(8,128)(2,1)S(1)}, bf16[4,4,32,512]{3,2,1,0:T(8,128)(2,1)S(1)}, u32[]{:S(2)}, u32[]{:S(2)}) collective-permute-start(bf16[4,4,32,512]{3,2,1,0:T(8,128)(2,1)S(1)} %get-tuple-element.176), channel_id=1, source_target_pairs={{0,2},{2,0},{4,6},{6,4},{8,10},{10,8},{12,14},{14,12},{16,18},{18,... | collective-permute-start | bytes 1572872 | tf_op jit(solution)/shard_map/ppermute | solution.py:724
  171.0 8.7 %collective-permute-start.19 = (bf16[64,2048]{1,0:T(8,128)(2,1)S(1)}, bf16[64,2048]{1,0:T(8,128)(2,1)S(1)}, u32[]{:S(2)}, u32[]{:S(2)}) collective-permute-start(bf16[64,2048]{1,0:T(8,128)(2,1)S(1)} %fusion.2), channel_id=1, source_target_pairs={{0,4},{2,6},{4,0},{6,2},{8,12},{10,14},{12,8},{14,10},{16,20},{18,... | collective-permute-start | bytes 786440 | tf_op jit(solution)/shard_map/ppermute | solution.py:724
  172.7 13.1 %collective-permute-start.15 = (bf16[128,1024]{1,0:T(8,128)(2,1)S(1)}, bf16[128,1024]{1,0:T(8,128)(2,1)S(1)}, u32[]{:S(2)}, u32[]{:S(2)}) collective-permute-start(bf16[128,1024]{1,0:T(8,128)(2,1)S(1)} %fusion.3), channel_id=1, source_target_pairs={{0,16},{2,18},{4,20},{6,22},{8,24},{10,26},{12,28},{14,30},{16,0},... | collective-permute-start | bytes 786440 | tf_op jit(solution)/shard_map/ppermute | solution.py:724
  175.5 10.4 %collective-permute-start.14 = (bf16[2,4,32,512]{3,2,1,0:T(8,128)(2,1)S(1)}, bf16[2,4,32,512]{3,2,1,0:T(8,128)(2,1)S(1)}, u32[]{:S(2)}, u32[]{:S(2)}) collective-permute-start(bf16[2,4,32,512]{3,2,1,0:T(8,128)(2,1)S(1)} %get-tuple-element.179), channel_id=1, source_target_pairs={{0,4},{2,6},{4,0},{6,2},{8,12},{10,14},{12,8},{14,10},{16,20},{18,... | collective-permute-start | bytes 786440 | tf_op jit(solution)/shard_map/ppermute | solution.py:724
  179.8 7.1 %collective-permute-start.20 = (f32[32,2048]{1,0:T(8,128)S(1)}, f32[32,2048]{1,0:T(8,128)S(1)}, u32[]{:S(2)}, u32[]{:S(2)}) collective-permute-start(f32[32,2048]{1,0:T(8,128)S(1)} %constant_dynamic-slice_fusion), channel_id=1, source_target_pairs={{0,1},{1,0},{2,3},{3,2},{4,5},{5,4},{6,7},{7,6},{8,9},{9,8},{10,11... | collective-permute-start | bytes 786440 | tf_op jit(solution)/shard_map/ppermute | solution.py:728
  183.0 8.4 %collective-permute-start.17 = (bf16[2,4,32,512]{3,2,1,0:T(8,128)(2,1)S(1)}, bf16[2,4,32,512]{3,2,1,0:T(8,128)(2,1)S(1)}, u32[]{:S(2)}, u32[]{:S(2)}) collective-permute-start(bf16[2,4,32,512]{3,2,1,0:T(8,128)(2,1)S(1)} %get-tuple-element.180), channel_id=1, source_target_pairs={{0,8},{2,10},{4,12},{6,14},{8,0},{10,2},{12,4},{14,6},{16,24},{18,... | collective-permute-start | bytes 786440 | tf_op jit(solution)/shard_map/ppermute | solution.py:724
  191.5 16.9 %collective-permute-start.18 = (bf16[4,32,1024]{2,1,0:T(8,128)(2,1)S(1)}, bf16[4,32,1024]{2,1,0:T(8,128)(2,1)S(1)}, u32[]{:S(2)}, u32[]{:S(2)}) collective-permute-start(bf16[4,32,1024]{2,1,0:T(8,128)(2,1)S(1)} %pad_maximum_fusion.1), channel_id=1, source_target_pairs={{0,16},{2,18},{4,20},{6,22},{8,24},{10,26},{12,28},{14,30},{16,0},... | collective-permute-start | bytes 786440 | tf_op jit(solution)/shard_map/ppermute | solution.py:724
  193.8 14.1 %all-to-all-start = ((f32[32,3,32]{2,1,0:T(4,128)}), f32[32,3,32]{2,1,0:T(4,128)S(1)}, u32[]{:S(2)}, u32[]{:S(2)}) async-start(f32[32,3,32]{2,1,0:T(4,128)} %copy.28), calls=%async_computation | async-start | bytes 131072 | tf_op jit(solution)/shard_map/all_to_all | solution.py:886
  (8 other events, 39.0 us)

commit v4 on v3

--- a/solution.py
+++ b/solution.py
@@ -111,8 +111,8 @@
             copy.wait()
 
 
-def repeat(turns, body):
-    lax.fori_loop(0, turns, lambda turn, carry: body(turn), None)
+def repeat(turns, body, unroll=1):
+    lax.fori_loop(0, turns, lambda turn, carry: body(turn), None, unroll=unroll)
 
 
 def block_of(turn, size):
@@ -189,7 +189,7 @@
         pulled[rows] = pull.astype(bf16)
         feed[1, rows] = (chance * pull).astype(bf16)
 
-    repeat(seqs, gather)
+    repeat(seqs, gather, 2)
     copies.send(chosen, chosen_out)
     copies.send(pulled, pulled_out)
     copies.send(score, score_out)
@@ -224,7 +224,7 @@
             lefts[1, rows, lanes] = unstacked(mixed, head).astype(bf16)
         probs_copy(seq).start()
 
-    repeat(seqs, attend)
+    repeat(seqs, attend, 2)
     copies.send(lefts.at[1], lefts_out.at[1])
     weights[3].wait()
     attn[...] = dot_nn(lefts[1], out_w[...])
@@ -482,7 +482,7 @@
             grads[1, rows, lanes] = dot_tn(score_grad, stacked_queries).astype(bf16)
             grads[0, rows, lanes] = unstacked(dot_nn(score_grad, keys[rows, lanes]), head).astype(bf16)
 
-    repeat(seqs, attention_grad)
+    repeat(seqs, attention_grad, 2)
     copies.send(grads.at[pl.ds(0, 3)], grads_out)
     arrive("lefts")
     half, cut = nodes // 2, send_gone.shape[3]

time: 210 us -> 208 us (level)
  no operation moved by 1% of the time
where the time goes in v4:
time: 208 us
  Pallas kernels  110 us (53%)
  waiting for transfers between devices  42 us (20%)
  starting transfers between devices  28.6 us (14%)
  other arithmetic  21.4 us (10%)
  local copies, waits for them, and re-layouts  4.86 us (2%)
    pallas_call x6, Pallas kernels, call(): pl.pallas_call(body, grid_spec=grid, **rest)(*scalars, *arrays, *waits)  110 us
    ppermute x15, waiting for transfers between devices, swap_nodes(): lax.ppermute(values, 'seq', [(i, i ^ 1 << bit) for i in range(nodes)])  29.8 us
    ppermute x15, starting transfers between devices, swap_nodes(): lax.ppermute(values, 'seq', [(i, i ^ 1 << bit) for i in range(nodes)])  23.1 us
    convert_element_type x10, other arithmetic, add_low(): return (left.astype(f32) + right.astype(f32)).astype(bf16)  16.6 us
    all_to_all x1, waiting for transfers between devices, on_device(): lax.all_to_all(sums, ('seq', 'dp'), 0, 0, tiled=True)  8.67 us
  transfers between devices with their start and end apart: 22, of which 10 were waited for; matrix products, arithmetic and copies ran while one was open for 12% of the time, Pallas kernels for 25%

profile of v4, /device:TPU:0, one launch (start us, length us, event | category | flops | bytes accessed | tf_op | source)
XLA Modules:
  0.0 207.8 jit_solution(1757810953223875177)
XLA Ops:
  0.6 20.6 %front.1 = (bf16[512,1024]{1,0:T(8,128)(2,1)}, bf16[2,512,1024]{2,1,0:T(8,128)(2,1)}, bf16[512,1024]{1,0:T(8,128)(2,1)}, bf16[512,1024]{1,0:T(8,128)(2,1)}, bf16...) custom-call(s32[1,4]{1,0:T(1,128)} %refs_0_.5, ...), custom_call_target="tpu_custom_call" | custom-call | flops 1800000000 | bytes 6300000 | tf_op jit(solution)/shard_map/front/pallas_call | solution.py:41
  22.3 3.5 %collective-permute-done.refs_2_ = bf16[2,512,1024]{2,1,0:T(8,128)(2,1)} collective-permute-done((bf16[2,512,1024]{2,1,0:T(8,128)(2,1)}, bf16[2,512,1024]{2,1,0:T(8,128)(2,1)}, u32[]{:S(2)}, u32[]{:S(2)}) %collective-permute-start) | collective-permute-done | bytes 2097184 | tf_op jit(solution)/shard_map/ppermute | solution.py:728
  25.9 36.7 %feed.1 = (bf16[2,512,1024]{2,1,0:T(8,128)(2,1)}, bf16[2,512,1024]{2,1,0:T(8,128)(2,1)}, bf16[8,64,2048]{2,1,0:T(8,128)(2,1)}, bf16[8,64,2048]{2,1,0:T(8,128)(2,...) custom-call(s32[2]{0:T(128)} %pad_add_fusion.refs_0_, ...), custom_call_target="tpu_custom_call" | custom-call | flops 3400000000 | bytes 11900000 | tf_op jit(solution)/shard_map/feed/pallas_call | solution.py:41
  63.0 2.7 %collective-permute-start.2 = (bf16[8,64,2048]{2,1,0:T(8,128)(2,1)}, bf16[8,64,2048]{2,1,0:T(8,128)(2,1)}, u32[]{:S(2)}, u32[]{:S(2)}) collective-permute-start(bf16[8,64,2048]{2,1,0:T(8,128)(2,1)} %get-tuple-element.88), channel_id=1, source_target_pairs={{0,8},{2,10},{4,12},{6,14},{8,0},{10,2},{12,4},{14,6},{16,24},{18,... | collective-permute-start | bytes 6291464 | tf_op jit(solution)/shard_map/ppermute | solution.py:724
  67.2 22.3 %back.1 = (bf16[3,512,1024]{2,1,0:T(8,128)(2,1)}, f32[512,1024]{1,0:T(8,128)}, f32[8,1024]{1,0:T(8,128)}, bf16[8,4,32,512]{3,2,1,0:T(8,128)(2,1)}, bf16[8,4,32,5...) custom-call(s32[2]{0:T(128)} %pad_add_fusion.refs_0_, ...), custom_call_target="tpu_custom_call" | custom-call | flops 2000000000 | bytes 7000000 | tf_op jit(solution)/shard_map/back/pallas_call | solution.py:41
  90.4 9.5 %spread.2.refs_13_ = bf16[4096,1024]{1,0:T(8,128)(2,1)} custom-call(s32[1,4]{1,0:T(1,128)} %refs_0_.5, s32[4,1,128]{2,1,0:T(1,128)} %bitcast.89, bf16[4096,1024]{1,0:T(8,128)(2,1)} %bitcast.77, f32[512,128]{1,0:T(8,128)} %get-tuple-element.71.refs_4_.refs_3_.refs_6_, f32[512,1024]{1,0:T(8,128)} %get-tuple-element.72.refs_3_.refs_4_, ...), custom_call_target="tpu_custom_call" | custom-call | flops 800000000 | bytes 2800000 | tf_op jit(solution)/shard_map/spread/pallas_call | solution.py:41
  99.9 10.7 %last.1 = (f32[512,1024]{1,0:T(8,128)}, f32[8,1024]{1,0:T(8,128)}, f32[8,1024]{1,0:T(8,128)}) custom-call(bf16[8,128]{1,0:T(8,128)(2,1)} %bitcast.94, bf16[8,128]{1,0:T(8,128)(2,1)} %bitcast.96, bf16[512,1024]{1,0:T(8,128)(2,1)} %get-tuple-element.76.refs_2_, f32[512,1024]{1,0:T(8,128)} %get-tuple-element.72.refs_3_.refs_4_, ...), custom_call_target="tpu_custom_call" | custom-call | flops 900000000 | bytes 3150000 | tf_op jit(solution)/shard_map/last/pallas_call | solution.py:41
  112.2 2.6 %add_convert_fusion.1 = (bf16[4,64,2048]{2,1,0:T(8,128)(2,1)S(1)}, bf16[4,64,2048]{2,1,0:T(8,128)(2,1)S(1)}) fusion(bf16[8,64,2048]{2,1,0:T(8,128)(2,1)} %collective-permute-done.2, bf16[8,64,2048]{2,1,0:T(8,128)(2,1)S(1)} %copy-done.5), kind=kLoop, calls=%fused_computation.1 | loop fusion | flops 4194304 | bytes 6291456 | tf_op jit(solution)/shard_map/convert_element_type | solution.py:720
  114.8 1.8 collective-permute-start.9
  116.6 3.5 %fusion.1 = (bf16[4,128,1024]{2,1,0:T(8,128)(2,1)S(1)}, bf16[4,128,1024]{2,1,0:T(8,128)(2,1)}) fusion(bf16[2,4,128,1024]{3,2,1,0:T(8,128)(2,1)} %collective-permute-done.3, bf16[2,4,128,1024]{3,2,1,0:T(8,128)(2,1)S(1)} %copy-done.4), kind=kLoop, calls=%fused_computation.9 | loop fusion | flops 4194304 | bytes 6291456 | tf_op jit(solution)/shard_map/squeeze | solution.py:774
  121.8 2.0 add_convert_fusion.5.refs_6_
  127.1 3.8 %add_convert_fusion = (bf16[8,4,32,512]{3,2,1,0:T(8,128)(2,1)}, bf16[8,4,32,512]{3,2,1,0:T(8,128)(2,1)}) fusion(bf16[16,4,32,512]{3,2,1,0:T(8,128)(2,1)} %collective-permute-done.6, bf16[16,4,32,512]{3,2,1,0:T(8,128)(2,1)S(1)} %copy-done.3), kind=kLoop, calls=%fused_computation | loop fusion | flops 4194304 | bytes 6291456 | tf_op jit(solution)/shard_map/convert_element_type | solution.py:720
  131.3 10.2 %spread.3 = f32[4096,1024]{1,0:T(8,128)} custom-call(s32[1,4]{1,0:T(1,128)} %refs_0_.5, s32[4,1,128]{2,1,0:T(1,128)} %bitcast.90, bf16[4096,1024]{1,0:T(8,128)(2,1)} %bitcast.75, f32[512,1024]{1,0:T(8,128)} %get-tuple-element.86.refs_3_, bf16[4,64,2048]{2,1,0:T(8,128)(2,1)} %copy-done.1, bf16[4,128,1024]{2,1,0:T(8,128)(2,1)} %get-tuple-element.167.refs_5_, ...), custom_call_target="tpu_custom_call" | custom-call | flops 800000000 | bytes 2800000 | tf_op jit(solution)/shard_map/spread/pallas_call | solution.py:41
  143.2 2.8 %collective-permute-start.12 = (bf16[2,64,2048]{2,1,0:T(8,128)(2,1)S(1)}, bf16[2,64,2048]{2,1,0:T(8,128)(2,1)S(1)}, u32[]{:S(2)}, u32[]{:S(2)}) collective-permute-start(bf16[2,64,2048]{2,1,0:T(8,128)(2,1)S(1)} %get-tuple-element.173), channel_id=1, source_target_pairs={{0,16},{2,18},{4,20},{6,22},{8,24},{10,26},{12,28},{14,30},{16,0},... | collective-permute-start | bytes 1572872 | tf_op jit(solution)/shard_map/ppermute | solution.py:724
  149.7 5.4 %collective-permute-done.7 = bf16[8,4,32,512]{3,2,1,0:T(8,128)(2,1)} collective-permute-done((bf16[8,4,32,512]{3,2,1,0:T(8,128)(2,1)S(1)}, bf16[8,4,32,512]{3,2,1,0:T(8,128)(2,1)}, u32[]{:S(2)}, u32[]{:S(2)}) %collective-permute-start.7) | collective-permute-done | bytes 1048608 | tf_op jit(solution)/shard_map/ppermute | solution.py:724
  157.2 10.2 %collective-permute-done.13 = bf16[8,4,32,512]{3,2,1,0:T(8,128)(2,1)} collective-permute-done((bf16[8,4,32,512]{3,2,1,0:T(8,128)(2,1)}, bf16[8,4,32,512]{3,2,1,0:T(8,128)(2,1)}, u32[]{:S(2)}, u32[]{:S(2)}) %collective-permute-start.13) | collective-permute-done | bytes 1048608 | tf_op jit(solution)/shard_map/ppermute | solution.py:724
  169.7 1.6 collective-permute-start.19
  171.4 2.7 %collective-permute-start.15 = (bf16[128,1024]{1,0:T(8,128)(2,1)S(1)}, bf16[128,1024]{1,0:T(8,128)(2,1)S(1)}, u32[]{:S(2)}, u32[]{:S(2)}) collective-permute-start(bf16[128,1024]{1,0:T(8,128)(2,1)S(1)} %fusion.3), channel_id=1, source_target_pairs={{0,16},{2,18},{4,20},{6,22},{8,24},{10,26},{12,28},{14,30},{16,0},... | collective-permute-start | bytes 786440 | tf_op jit(solution)/shard_map/ppermute | solution.py:724
  174.8 3.7 %collective-permute-done.19 = bf16[64,2048]{1,0:T(8,128)(2,1)S(1)} collective-permute-done((bf16[64,2048]{1,0:T(8,128)(2,1)S(1)}, bf16[64,2048]{1,0:T(8,128)(2,1)S(1)}, u32[]{:S(2)}, u32[]{:S(2)}) %collective-permute-start.19) | collective-permute-done | bytes 262176 | tf_op jit(solution)/shard_map/ppermute | solution.py:724
  178.6 2.8 %collective-permute-done.16 = bf16[4,4,32,512]{3,2,1,0:T(8,128)(2,1)S(1)} collective-permute-done((bf16[4,4,32,512]{3,2,1,0:T(8,128)(2,1)S(1)}, bf16[4,4,32,512]{3,2,1,0:T(8,128)(2,1)S(1)}, u32[]{:S(2)}, u32[]{:S(2)}) %collective-permute-start.16) | collective-permute-done | bytes 524320 | tf_op jit(solution)/shard_map/ppermute | solution.py:724
  185.7 4.2 %collective-permute-done.17 = bf16[2,4,32,512]{3,2,1,0:T(8,128)(2,1)S(1)} collective-permute-done((bf16[2,4,32,512]{3,2,1,0:T(8,128)(2,1)S(1)}, bf16[2,4,32,512]{3,2,1,0:T(8,128)(2,1)S(1)}, u32[]{:S(2)}, u32[]{:S(2)}) %collective-permute-start.17) | collective-permute-done | bytes 262176 | tf_op jit(solution)/shard_map/ppermute | solution.py:724
  190.1 1.6 collective-permute-start.18
  192.4 3.6 %all-to-all-start = ((f32[32,3,32]{2,1,0:T(4,128)}), f32[32,3,32]{2,1,0:T(4,128)S(1)}, u32[]{:S(2)}, u32[]{:S(2)}) async-start(f32[32,3,32]{2,1,0:T(4,128)} %copy.28), calls=%async_computation | async-start | bytes 131072 | tf_op jit(solution)/shard_map/all_to_all | solution.py:886
  197.7 8.7 %all-to-all-done = f32[32,3,32]{2,1,0:T(4,128)S(1)} async-done(((f32[32,3,32]{2,1,0:T(4,128)}), f32[32,3,32]{2,1,0:T(4,128)S(1)}, u32[]{:S(2)}, u32[]{:S(2)}) %all-to-all-start) | async-done | bytes 12320 | tf_op jit(solution)/shard_map/all_to_all | solution.py:886
  (79 shorter events, 29.7 us)
Async XLA Ops:
  21.2 4.7 %collective-permute-start = (bf16[2,512,1024]{2,1,0:T(8,128)(2,1)}, bf16[2,512,1024]{2,1,0:T(8,128)(2,1)}, u32[]{:S(2)}, u32[]{:S(2)}) collective-permute-start(bf16[2,512,1024]{2,1,0:T(8,128)(2,1)} %get-tuple-element.73.refs_1_), channel_id=1, source_target_pairs={{0,1},{1,0},{2,3},{3,2},{4,5},{5,4},{6,7},{7,6},{8,9},{9,8},{10,11... | collective-permute-start | bytes 6291464 | tf_op jit(solution)/shard_map/ppermute | solution.py:728
  62.6 4.6 %collective-permute-start.1 = (bf16[2,512,1024]{2,1,0:T(8,128)(2,1)}, bf16[2,512,1024]{2,1,0:T(8,128)(2,1)}, u32[]{:S(2)}, u32[]{:S(2)}) collective-permute-start(bf16[2,512,1024]{2,1,0:T(8,128)(2,1)} %get-tuple-element.75), channel_id=1, source_target_pairs={{0,1},{1,0},{2,3},{3,2},{4,5},{5,4},{6,7},{7,6},{8,9},{9,8},{10,11... | collective-permute-start | bytes 6291464 | tf_op jit(solution)/shard_map/ppermute | solution.py:728
  63.0 49.1 %collective-permute-start.2 = (bf16[8,64,2048]{2,1,0:T(8,128)(2,1)}, bf16[8,64,2048]{2,1,0:T(8,128)(2,1)}, u32[]{:S(2)}, u32[]{:S(2)}) collective-permute-start(bf16[8,64,2048]{2,1,0:T(8,128)(2,1)} %get-tuple-element.88), channel_id=1, source_target_pairs={{0,8},{2,10},{4,12},{6,14},{8,0},{10,2},{12,4},{14,6},{16,24},{18,... | collective-permute-start | bytes 6291464 | tf_op jit(solution)/shard_map/ppermute | solution.py:724
  65.7 50.9 %collective-permute-start.3 = (bf16[2,4,128,1024]{3,2,1,0:T(8,128)(2,1)}, bf16[2,4,128,1024]{3,2,1,0:T(8,128)(2,1)}, u32[]{:S(2)}, u32[]{:S(2)}) collective-permute-start(bf16[2,4,128,1024]{3,2,1,0:T(8,128)(2,1)} %get-tuple-element.92), channel_id=1, source_target_pairs={{0,2},{2,0},{4,6},{6,4},{8,10},{10,8},{12,14},{14,12},{16,18},{18,... | collective-permute-start | bytes 6291464 | tf_op jit(solution)/shard_map/ppermute | solution.py:724
  89.5 37.6 %collective-permute-start.6 = (bf16[16,4,32,512]{3,2,1,0:T(8,128)(2,1)}, bf16[16,4,32,512]{3,2,1,0:T(8,128)(2,1)}, u32[]{:S(2)}, u32[]{:S(2)}) collective-permute-start(bf16[16,4,32,512]{3,2,1,0:T(8,128)(2,1)} %get-tuple-element.101), channel_id=1, source_target_pairs={{0,1},{1,0},{2,3},{3,2},{4,5},{5,4},{6,7},{7,6},{8,9},{9,8},{10,11... | collective-permute-start | bytes 6291464 | tf_op jit(solution)/shard_map/ppermute | solution.py:728
  89.9 31.9 %collective-permute-start.4 = (bf16[8,4,32,512]{3,2,1,0:T(8,128)(2,1)}, bf16[8,4,32,512]{3,2,1,0:T(8,128)(2,1)}, u32[]{:S(2)}, u32[]{:S(2)}) collective-permute-start(bf16[8,4,32,512]{3,2,1,0:T(8,128)(2,1)} %get-tuple-element.83.refs_7_), channel_id=1, source_target_pairs={{0,1},{1,0},{2,3},{3,2},{4,5},{5,4},{6,7},{7,6},{8,9},{9,8},{10,11... | collective-permute-start | bytes 3145736 | tf_op jit(solution)/shard_map/ppermute | solution.py:728
  90.1 31.8 %collective-permute-start.5 = (bf16[8,4,32,512]{3,2,1,0:T(8,128)(2,1)}, bf16[8,4,32,512]{3,2,1,0:T(8,128)(2,1)}, u32[]{:S(2)}, u32[]{:S(2)}) collective-permute-start(bf16[8,4,32,512]{3,2,1,0:T(8,128)(2,1)} %get-tuple-element.97), channel_id=1, source_target_pairs={{0,1},{1,0},{2,3},{3,2},{4,5},{5,4},{6,7},{7,6},{8,9},{9,8},{10,11... | collective-permute-start | bytes 3145736 | tf_op jit(solution)/shard_map/ppermute | solution.py:728
  99.9 12.3 %copy-start.5 = (bf16[8,64,2048]{2,1,0:T(8,128)(2,1)S(1)}, bf16[8,64,2048]{2,1,0:T(8,128)(2,1)}, u32[]{:S(2)}) copy-start(bf16[8,64,2048]{2,1,0:T(8,128)(2,1)} %get-tuple-element.89) | copy-start | bytes 6291460
  114.8 26.8 %collective-permute-start.9 = (bf16[4,64,2048]{2,1,0:T(8,128)(2,1)S(1)}, bf16[4,64,2048]{2,1,0:T(8,128)(2,1)}, u32[]{:S(2)}, u32[]{:S(2)}) collective-permute-start(bf16[4,64,2048]{2,1,0:T(8,128)(2,1)S(1)} %get-tuple-element.165.refs_4_), channel_id=1, source_target_pairs={{0,2},{2,0},{4,6},{6,4},{8,10},{10,8},{12,14},{14,12},{16,18},{18,... | collective-permute-start | bytes 3145736 | tf_op jit(solution)/shard_map/ppermute | solution.py:724
  120.1 26.4 %collective-permute-start.8 = (bf16[4,128,1024]{2,1,0:T(8,128)(2,1)}, bf16[4,128,1024]{2,1,0:T(8,128)(2,1)}, u32[]{:S(2)}, u32[]{:S(2)}) collective-permute-start(bf16[4,128,1024]{2,1,0:T(8,128)(2,1)} %get-tuple-element.167.refs_5_), channel_id=1, source_target_pairs={{0,4},{2,6},{4,0},{6,2},{8,12},{10,14},{12,8},{14,10},{16,20},{18,... | collective-permute-start | bytes 3145736 | tf_op jit(solution)/shard_map/ppermute | solution.py:724
  123.9 31.2 %collective-permute-start.7 = (bf16[8,4,32,512]{3,2,1,0:T(8,128)(2,1)S(1)}, bf16[8,4,32,512]{3,2,1,0:T(8,128)(2,1)}, u32[]{:S(2)}, u32[]{:S(2)}) collective-permute-start(bf16[8,4,32,512]{3,2,1,0:T(8,128)(2,1)S(1)} %add_convert_fusion.5.refs_6_), channel_id=1, source_target_pairs={{0,8},{2,10},{4,12},{6,14},{8,0},{10,2},{12,4},{14,6},{16,24},{18,... | collective-permute-start | bytes 3145736 | tf_op jit(solution)/shard_map/ppermute | solution.py:724
  130.9 36.5 %collective-permute-start.13 = (bf16[8,4,32,512]{3,2,1,0:T(8,128)(2,1)}, bf16[8,4,32,512]{3,2,1,0:T(8,128)(2,1)}, u32[]{:S(2)}, u32[]{:S(2)}) collective-permute-start(bf16[8,4,32,512]{3,2,1,0:T(8,128)(2,1)} %get-tuple-element.169.refs_7_), channel_id=1, source_target_pairs={{0,4},{2,6},{4,0},{6,2},{8,12},{10,14},{12,8},{14,10},{16,20},{18,... | collective-permute-start | bytes 3145736 | tf_op jit(solution)/shard_map/ppermute | solution.py:724
  143.2 26.5 %collective-permute-start.12 = (bf16[2,64,2048]{2,1,0:T(8,128)(2,1)S(1)}, bf16[2,64,2048]{2,1,0:T(8,128)(2,1)S(1)}, u32[]{:S(2)}, u32[]{:S(2)}) collective-permute-start(bf16[2,64,2048]{2,1,0:T(8,128)(2,1)S(1)} %get-tuple-element.173), channel_id=1, source_target_pairs={{0,16},{2,18},{4,20},{6,22},{8,24},{10,26},{12,28},{14,30},{16,0},... | collective-permute-start | bytes 1572872 | tf_op jit(solution)/shard_map/ppermute | solution.py:724
  148.1 19.3 %copy-start.2 = (bf16[8,4,32,512]{3,2,1,0:T(8,128)(2,1)S(1)}, bf16[8,4,32,512]{3,2,1,0:T(8,128)(2,1)}, u32[]{:S(2)}) copy-start(bf16[8,4,32,512]{3,2,1,0:T(8,128)(2,1)} %get-tuple-element.115) | copy-start | bytes 3145732
  148.1 23.2 %collective-permute-start.11 = (bf16[2,128,1024]{2,1,0:T(8,128)(2,1)S(1)}, bf16[2,128,1024]{2,1,0:T(8,128)(2,1)S(1)}, u32[]{:S(2)}, u32[]{:S(2)}) collective-permute-start(bf16[2,128,1024]{2,1,0:T(8,128)(2,1)S(1)} %get-tuple-element.175), channel_id=1, source_target_pairs={{0,8},{2,10},{4,12},{6,14},{8,0},{10,2},{12,4},{14,6},{16,24},{18,... | collective-permute-start | bytes 1572872 | tf_op jit(solution)/shard_map/ppermute | solution.py:724
  156.6 17.5 %collective-permute-start.10 = (bf16[4,4,32,512]{3,2,1,0:T(8,128)(2,1)S(1)}, bf16[4,4,32,512]{3,2,1,0:T(8,128)(2,1)S(1)}, u32[]{:S(2)}, u32[]{:S(2)}) collective-permute-start(bf16[4,4,32,512]{3,2,1,0:T(8,128)(2,1)S(1)} %get-tuple-element.171), channel_id=1, source_target_pairs={{0,2},{2,0},{4,6},{6,4},{8,10},{10,8},{12,14},{14,12},{16,18},{18,... | collective-permute-start | bytes 1572872 | tf_op jit(solution)/shard_map/ppermute | solution.py:724
  169.0 12.4 %collective-permute-start.16 = (bf16[4,4,32,512]{3,2,1,0:T(8,128)(2,1)S(1)}, bf16[4,4,32,512]{3,2,1,0:T(8,128)(2,1)S(1)}, u32[]{:S(2)}, u32[]{:S(2)}) collective-permute-start(bf16[4,4,32,512]{3,2,1,0:T(8,128)(2,1)S(1)} %get-tuple-element.176), channel_id=1, source_target_pairs={{0,2},{2,0},{4,6},{6,4},{8,10},{10,8},{12,14},{14,12},{16,18},{18,... | collective-permute-start | bytes 1572872 | tf_op jit(solution)/shard_map/ppermute | solution.py:724
  169.7 8.7 %collective-permute-start.19 = (bf16[64,2048]{1,0:T(8,128)(2,1)S(1)}, bf16[64,2048]{1,0:T(8,128)(2,1)S(1)}, u32[]{:S(2)}, u32[]{:S(2)}) collective-permute-start(bf16[64,2048]{1,0:T(8,128)(2,1)S(1)} %fusion.2), channel_id=1, source_target_pairs={{0,4},{2,6},{4,0},{6,2},{8,12},{10,14},{12,8},{14,10},{16,20},{18,... | collective-permute-start | bytes 786440 | tf_op jit(solution)/shard_map/ppermute | solution.py:724
  171.4 13.0 %collective-permute-start.15 = (bf16[128,1024]{1,0:T(8,128)(2,1)S(1)}, bf16[128,1024]{1,0:T(8,128)(2,1)S(1)}, u32[]{:S(2)}, u32[]{:S(2)}) collective-permute-start(bf16[128,1024]{1,0:T(8,128)(2,1)S(1)} %fusion.3), channel_id=1, source_target_pairs={{0,16},{2,18},{4,20},{6,22},{8,24},{10,26},{12,28},{14,30},{16,0},... | collective-permute-start | bytes 786440 | tf_op jit(solution)/shard_map/ppermute | solution.py:724
  174.3 10.3 %collective-permute-start.14 = (bf16[2,4,32,512]{3,2,1,0:T(8,128)(2,1)S(1)}, bf16[2,4,32,512]{3,2,1,0:T(8,128)(2,1)S(1)}, u32[]{:S(2)}, u32[]{:S(2)}) collective-permute-start(bf16[2,4,32,512]{3,2,1,0:T(8,128)(2,1)S(1)} %get-tuple-element.179), channel_id=1, source_target_pairs={{0,4},{2,6},{4,0},{6,2},{8,12},{10,14},{12,8},{14,10},{16,20},{18,... | collective-permute-start | bytes 786440 | tf_op jit(solution)/shard_map/ppermute | solution.py:724
  178.6 7.0 %collective-permute-start.20 = (f32[32,2048]{1,0:T(8,128)S(1)}, f32[32,2048]{1,0:T(8,128)S(1)}, u32[]{:S(2)}, u32[]{:S(2)}) collective-permute-start(f32[32,2048]{1,0:T(8,128)S(1)} %constant_dynamic-slice_fusion), channel_id=1, source_target_pairs={{0,1},{1,0},{2,3},{3,2},{4,5},{5,4},{6,7},{7,6},{8,9},{9,8},{10,11... | collective-permute-start | bytes 786440 | tf_op jit(solution)/shard_map/ppermute | solution.py:728
  181.6 8.3 %collective-permute-start.17 = (bf16[2,4,32,512]{3,2,1,0:T(8,128)(2,1)S(1)}, bf16[2,4,32,512]{3,2,1,0:T(8,128)(2,1)S(1)}, u32[]{:S(2)}, u32[]{:S(2)}) collective-permute-start(bf16[2,4,32,512]{3,2,1,0:T(8,128)(2,1)S(1)} %get-tuple-element.180), channel_id=1, source_target_pairs={{0,8},{2,10},{4,12},{6,14},{8,0},{10,2},{12,4},{14,6},{16,24},{18,... | collective-permute-start | bytes 786440 | tf_op jit(solution)/shard_map/ppermute | solution.py:724
  190.1 16.8 %collective-permute-start.18 = (bf16[4,32,1024]{2,1,0:T(8,128)(2,1)S(1)}, bf16[4,32,1024]{2,1,0:T(8,128)(2,1)S(1)}, u32[]{:S(2)}, u32[]{:S(2)}) collective-permute-start(bf16[4,32,1024]{2,1,0:T(8,128)(2,1)S(1)} %pad_maximum_fusion.1), channel_id=1, source_target_pairs={{0,16},{2,18},{4,20},{6,22},{8,24},{10,26},{12,28},{14,30},{16,0},... | collective-permute-start | bytes 786440 | tf_op jit(solution)/shard_map/ppermute | solution.py:724
  192.4 14.0 %all-to-all-start = ((f32[32,3,32]{2,1,0:T(4,128)}), f32[32,3,32]{2,1,0:T(4,128)S(1)}, u32[]{:S(2)}, u32[]{:S(2)}) async-start(f32[32,3,32]{2,1,0:T(4,128)} %copy.28), calls=%async_computation | async-start | bytes 131072 | tf_op jit(solution)/shard_map/all_to_all | solution.py:886
  (8 other events, 39.1 us)

commit v5 on v4

--- a/solution.py
+++ b/solution.py
@@ -230,13 +230,17 @@
     attn[...] = dot_nn(lefts[1], out_w[...])
     copies.send(attn, attn_out)
 
+    feed_copy = copies.send_group(
+        seqs, lambda seq: (feed.at[0, block_of(seq, slots)], feed_out.at[0, block_of(seq, slots)])
+    )
+
     def after_attention(seq):
         rows = block_of(seq, slots)
         after = chosen[rows].astype(f32) + attn[rows]
         feed[0, rows] = (after * inv_rms(after) * gain_two).astype(bf16)
+        feed_copy(seq).start()
 
     repeat(seqs, after_attention)
-    copies.send(feed.at[0], feed_out.at[0])
     copies.finish()
 
 
@@ -262,7 +266,7 @@
         scratch_shapes=[pltpu.VMEM((seqs, places, width), bf16)] * 2
         + [pltpu.VMEM((width, width), bf16)] * 4
         + [pltpu.VMEM(*out) for out in outs]
-        + [pltpu.SemaphoreType.DMA((2 * seqs + 4 + 11 + seqs,))],
+        + [pltpu.SemaphoreType.DMA((2 * seqs + 4 + 10 + 2 * seqs,))],
         out_shape=[jax.ShapeDtypeStruct(*out) for out in outs],
         compiler_params=params(58),
         name="front",

time: 208 us -> 208 us (level)
  no operation moved by 1% of the time
where the time goes in v5:
time: 208 us
  Pallas kernels  110 us (53%)
  waiting for transfers between devices  42 us (20%)
  starting transfers between devices  28.6 us (14%)
  other arithmetic  21.4 us (10%)
  local copies, waits for them, and re-layouts  4.86 us (2%)
    pallas_call x6, Pallas kernels, call(): pl.pallas_call(body, grid_spec=grid, **rest)(*scalars, *arrays, *waits)  110 us
    ppermute x15, waiting for transfers between devices, swap_nodes(): lax.ppermute(values, 'seq', [(i, i ^ 1 << bit) for i in range(nodes)])  29.8 us
    ppermute x15, starting transfers between devices, swap_nodes(): lax.ppermute(values, 'seq', [(i, i ^ 1 << bit) for i in range(nodes)])  23.1 us
    convert_element_type x10, other arithmetic, add_low(): return (left.astype(f32) + right.astype(f32)).astype(bf16)  16.6 us
    all_to_all x1, waiting for transfers between devices, on_device(): lax.all_to_all(sums, ('seq', 'dp'), 0, 0, tiled=True)  8.67 us
  transfers between devices with their start and end apart: 22, of which 10 were waited for; matrix products, arithmetic and copies ran while one was open for 12% of the time, Pallas kernels for 25%

profile of v5, /device:TPU:0, one launch (start us, length us, event | category | flops | bytes accessed | tf_op | source)
XLA Modules:
  0.0 207.9 jit_solution(10567716342713122822)
XLA Ops:
  0.6 20.6 %front.1 = (bf16[512,1024]{1,0:T(8,128)(2,1)}, bf16[2,512,1024]{2,1,0:T(8,128)(2,1)}, bf16[512,1024]{1,0:T(8,128)(2,1)}, bf16[512,1024]{1,0:T(8,128)(2,1)}, bf16...) custom-call(s32[1,4]{1,0:T(1,128)} %refs_0_.5, ...), custom_call_target="tpu_custom_call" | custom-call | flops 1800000000 | bytes 6300000 | tf_op jit(solution)/shard_map/front/pallas_call | solution.py:41
  22.4 3.5 %collective-permute-done.refs_2_ = bf16[2,512,1024]{2,1,0:T(8,128)(2,1)} collective-permute-done((bf16[2,512,1024]{2,1,0:T(8,128)(2,1)}, bf16[2,512,1024]{2,1,0:T(8,128)(2,1)}, u32[]{:S(2)}, u32[]{:S(2)}) %collective-permute-start) | collective-permute-done | bytes 2097184 | tf_op jit(solution)/shard_map/ppermute | solution.py:732
  25.9 36.7 %feed.1 = (bf16[2,512,1024]{2,1,0:T(8,128)(2,1)}, bf16[2,512,1024]{2,1,0:T(8,128)(2,1)}, bf16[8,64,2048]{2,1,0:T(8,128)(2,1)}, bf16[8,64,2048]{2,1,0:T(8,128)(2,...) custom-call(s32[2]{0:T(128)} %pad_add_fusion.refs_0_, ...), custom_call_target="tpu_custom_call" | custom-call | flops 3400000000 | bytes 11900000 | tf_op jit(solution)/shard_map/feed/pallas_call | solution.py:41
  63.0 2.7 %collective-permute-start.2 = (bf16[8,64,2048]{2,1,0:T(8,128)(2,1)}, bf16[8,64,2048]{2,1,0:T(8,128)(2,1)}, u32[]{:S(2)}, u32[]{:S(2)}) collective-permute-start(bf16[8,64,2048]{2,1,0:T(8,128)(2,1)} %get-tuple-element.88), channel_id=1, source_target_pairs={{0,8},{2,10},{4,12},{6,14},{8,0},{10,2},{12,4},{14,6},{16,24},{18,... | collective-permute-start | bytes 6291464 | tf_op jit(solution)/shard_map/ppermute | solution.py:728
  67.2 22.3 %back.1 = (bf16[3,512,1024]{2,1,0:T(8,128)(2,1)}, f32[512,1024]{1,0:T(8,128)}, f32[8,1024]{1,0:T(8,128)}, bf16[8,4,32,512]{3,2,1,0:T(8,128)(2,1)}, bf16[8,4,32,5...) custom-call(s32[2]{0:T(128)} %pad_add_fusion.refs_0_, ...), custom_call_target="tpu_custom_call" | custom-call | flops 2000000000 | bytes 7000000 | tf_op jit(solution)/shard_map/back/pallas_call | solution.py:41
  90.4 9.5 %spread.2.refs_13_ = bf16[4096,1024]{1,0:T(8,128)(2,1)} custom-call(s32[1,4]{1,0:T(1,128)} %refs_0_.5, s32[4,1,128]{2,1,0:T(1,128)} %bitcast.89, bf16[4096,1024]{1,0:T(8,128)(2,1)} %bitcast.77, f32[512,128]{1,0:T(8,128)} %get-tuple-element.71.refs_4_.refs_3_.refs_6_, f32[512,1024]{1,0:T(8,128)} %get-tuple-element.72.refs_3_.refs_4_, ...), custom_call_target="tpu_custom_call" | custom-call | flops 800000000 | bytes 2800000 | tf_op jit(solution)/shard_map/spread/pallas_call | solution.py:41
  99.9 10.7 %last.1 = (f32[512,1024]{1,0:T(8,128)}, f32[8,1024]{1,0:T(8,128)}, f32[8,1024]{1,0:T(8,128)}) custom-call(bf16[8,128]{1,0:T(8,128)(2,1)} %bitcast.94, bf16[8,128]{1,0:T(8,128)(2,1)} %bitcast.96, bf16[512,1024]{1,0:T(8,128)(2,1)} %get-tuple-element.76.refs_2_, f32[512,1024]{1,0:T(8,128)} %get-tuple-element.72.refs_3_.refs_4_, ...), custom_call_target="tpu_custom_call" | custom-call | flops 900000000 | bytes 3150000 | tf_op jit(solution)/shard_map/last/pallas_call | solution.py:41
  112.2 2.6 %add_convert_fusion.1 = (bf16[4,64,2048]{2,1,0:T(8,128)(2,1)S(1)}, bf16[4,64,2048]{2,1,0:T(8,128)(2,1)S(1)}) fusion(bf16[8,64,2048]{2,1,0:T(8,128)(2,1)} %collective-permute-done.2, bf16[8,64,2048]{2,1,0:T(8,128)(2,1)S(1)} %copy-done.5), kind=kLoop, calls=%fused_computation.1 | loop fusion | flops 4194304 | bytes 6291456 | tf_op jit(solution)/shard_map/convert_element_type | solution.py:724
  114.8 1.8 collective-permute-start.9
  116.6 3.5 %fusion.1 = (bf16[4,128,1024]{2,1,0:T(8,128)(2,1)S(1)}, bf16[4,128,1024]{2,1,0:T(8,128)(2,1)}) fusion(bf16[2,4,128,1024]{3,2,1,0:T(8,128)(2,1)} %collective-permute-done.3, bf16[2,4,128,1024]{3,2,1,0:T(8,128)(2,1)S(1)} %copy-done.4), kind=kLoop, calls=%fused_computation.9 | loop fusion | flops 4194304 | bytes 6291456 | tf_op jit(solution)/shard_map/squeeze | solution.py:778
  121.9 2.0 add_convert_fusion.5.refs_6_
  127.2 3.8 %add_convert_fusion = (bf16[8,4,32,512]{3,2,1,0:T(8,128)(2,1)}, bf16[8,4,32,512]{3,2,1,0:T(8,128)(2,1)}) fusion(bf16[16,4,32,512]{3,2,1,0:T(8,128)(2,1)} %collective-permute-done.6, bf16[16,4,32,512]{3,2,1,0:T(8,128)(2,1)S(1)} %copy-done.3), kind=kLoop, calls=%fused_computation | loop fusion | flops 4194304 | bytes 6291456 | tf_op jit(solution)/shard_map/convert_element_type | solution.py:724
  131.3 10.2 %spread.3 = f32[4096,1024]{1,0:T(8,128)} custom-call(s32[1,4]{1,0:T(1,128)} %refs_0_.5, s32[4,1,128]{2,1,0:T(1,128)} %bitcast.90, bf16[4096,1024]{1,0:T(8,128)(2,1)} %bitcast.75, f32[512,1024]{1,0:T(8,128)} %get-tuple-element.86.refs_3_, bf16[4,64,2048]{2,1,0:T(8,128)(2,1)} %copy-done.1, bf16[4,128,1024]{2,1,0:T(8,128)(2,1)} %get-tuple-element.167.refs_5_, ...), custom_call_target="tpu_custom_call" | custom-call | flops 800000000 | bytes 2800000 | tf_op jit(solution)/shard_map/spread/pallas_call | solution.py:41
  143.2 2.8 %collective-permute-start.12 = (bf16[2,64,2048]{2,1,0:T(8,128)(2,1)S(1)}, bf16[2,64,2048]{2,1,0:T(8,128)(2,1)S(1)}, u32[]{:S(2)}, u32[]{:S(2)}) collective-permute-start(bf16[2,64,2048]{2,1,0:T(8,128)(2,1)S(1)} %get-tuple-element.173), channel_id=1, source_target_pairs={{0,16},{2,18},{4,20},{6,22},{8,24},{10,26},{12,28},{14,30},{16,0},... | collective-permute-start | bytes 1572872 | tf_op jit(solution)/shard_map/ppermute | solution.py:728
  149.7 5.4 %collective-permute-done.7 = bf16[8,4,32,512]{3,2,1,0:T(8,128)(2,1)} collective-permute-done((bf16[8,4,32,512]{3,2,1,0:T(8,128)(2,1)S(1)}, bf16[8,4,32,512]{3,2,1,0:T(8,128)(2,1)}, u32[]{:S(2)}, u32[]{:S(2)}) %collective-permute-start.7) | collective-permute-done | bytes 1048608 | tf_op jit(solution)/shard_map/ppermute | solution.py:728
  157.2 10.2 %collective-permute-done.13 = bf16[8,4,32,512]{3,2,1,0:T(8,128)(2,1)} collective-permute-done((bf16[8,4,32,512]{3,2,1,0:T(8,128)(2,1)}, bf16[8,4,32,512]{3,2,1,0:T(8,128)(2,1)}, u32[]{:S(2)}, u32[]{:S(2)}) %collective-permute-start.13) | collective-permute-done | bytes 1048608 | tf_op jit(solution)/shard_map/ppermute | solution.py:728
  169.8 1.6 collective-permute-start.19
  171.5 2.7 %collective-permute-start.15 = (bf16[128,1024]{1,0:T(8,128)(2,1)S(1)}, bf16[128,1024]{1,0:T(8,128)(2,1)S(1)}, u32[]{:S(2)}, u32[]{:S(2)}) collective-permute-start(bf16[128,1024]{1,0:T(8,128)(2,1)S(1)} %fusion.3), channel_id=1, source_target_pairs={{0,16},{2,18},{4,20},{6,22},{8,24},{10,26},{12,28},{14,30},{16,0},... | collective-permute-start | bytes 786440 | tf_op jit(solution)/shard_map/ppermute | solution.py:728
  174.8 3.7 %collective-permute-done.19 = bf16[64,2048]{1,0:T(8,128)(2,1)S(1)} collective-permute-done((bf16[64,2048]{1,0:T(8,128)(2,1)S(1)}, bf16[64,2048]{1,0:T(8,128)(2,1)S(1)}, u32[]{:S(2)}, u32[]{:S(2)}) %collective-permute-start.19) | collective-permute-done | bytes 262176 | tf_op jit(solution)/shard_map/ppermute | solution.py:728
  178.6 2.8 %collective-permute-done.16 = bf16[4,4,32,512]{3,2,1,0:T(8,128)(2,1)S(1)} collective-permute-done((bf16[4,4,32,512]{3,2,1,0:T(8,128)(2,1)S(1)}, bf16[4,4,32,512]{3,2,1,0:T(8,128)(2,1)S(1)}, u32[]{:S(2)}, u32[]{:S(2)}) %collective-permute-start.16) | collective-permute-done | bytes 524320 | tf_op jit(solution)/shard_map/ppermute | solution.py:728
  185.7 4.2 %collective-permute-done.17 = bf16[2,4,32,512]{3,2,1,0:T(8,128)(2,1)S(1)} collective-permute-done((bf16[2,4,32,512]{3,2,1,0:T(8,128)(2,1)S(1)}, bf16[2,4,32,512]{3,2,1,0:T(8,128)(2,1)S(1)}, u32[]{:S(2)}, u32[]{:S(2)}) %collective-permute-start.17) | collective-permute-done | bytes 262176 | tf_op jit(solution)/shard_map/ppermute | solution.py:728
  190.1 1.6 collective-permute-start.18
  192.5 3.6 %all-to-all-start = ((f32[32,3,32]{2,1,0:T(4,128)}), f32[32,3,32]{2,1,0:T(4,128)S(1)}, u32[]{:S(2)}, u32[]{:S(2)}) async-start(f32[32,3,32]{2,1,0:T(4,128)} %copy.28), calls=%async_computation | async-start | bytes 131072 | tf_op jit(solution)/shard_map/all_to_all | solution.py:890
  197.8 8.7 %all-to-all-done = f32[32,3,32]{2,1,0:T(4,128)S(1)} async-done(((f32[32,3,32]{2,1,0:T(4,128)}), f32[32,3,32]{2,1,0:T(4,128)S(1)}, u32[]{:S(2)}, u32[]{:S(2)}) %all-to-all-start) | async-done | bytes 12320 | tf_op jit(solution)/shard_map/all_to_all | solution.py:890
  (79 shorter events, 29.7 us)
Async XLA Ops:
  21.2 4.7 %collective-permute-start = (bf16[2,512,1024]{2,1,0:T(8,128)(2,1)}, bf16[2,512,1024]{2,1,0:T(8,128)(2,1)}, u32[]{:S(2)}, u32[]{:S(2)}) collective-permute-start(bf16[2,512,1024]{2,1,0:T(8,128)(2,1)} %get-tuple-element.73.refs_1_), channel_id=1, source_target_pairs={{0,1},{1,0},{2,3},{3,2},{4,5},{5,4},{6,7},{7,6},{8,9},{9,8},{10,11... | collective-permute-start | bytes 6291464 | tf_op jit(solution)/shard_map/ppermute | solution.py:732
  62.6 4.6 %collective-permute-start.1 = (bf16[2,512,1024]{2,1,0:T(8,128)(2,1)}, bf16[2,512,1024]{2,1,0:T(8,128)(2,1)}, u32[]{:S(2)}, u32[]{:S(2)}) collective-permute-start(bf16[2,512,1024]{2,1,0:T(8,128)(2,1)} %get-tuple-element.75), channel_id=1, source_target_pairs={{0,1},{1,0},{2,3},{3,2},{4,5},{5,4},{6,7},{7,6},{8,9},{9,8},{10,11... | collective-permute-start | bytes 6291464 | tf_op jit(solution)/shard_map/ppermute | solution.py:732
  63.0 49.1 %collective-permute-start.2 = (bf16[8,64,2048]{2,1,0:T(8,128)(2,1)}, bf16[8,64,2048]{2,1,0:T(8,128)(2,1)}, u32[]{:S(2)}, u32[]{:S(2)}) collective-permute-start(bf16[8,64,2048]{2,1,0:T(8,128)(2,1)} %get-tuple-element.88), channel_id=1, source_target_pairs={{0,8},{2,10},{4,12},{6,14},{8,0},{10,2},{12,4},{14,6},{16,24},{18,... | collective-permute-start | bytes 6291464 | tf_op jit(solution)/shard_map/ppermute | solution.py:728
  65.7 50.9 %collective-permute-start.3 = (bf16[2,4,128,1024]{3,2,1,0:T(8,128)(2,1)}, bf16[2,4,128,1024]{3,2,1,0:T(8,128)(2,1)}, u32[]{:S(2)}, u32[]{:S(2)}) collective-permute-start(bf16[2,4,128,1024]{3,2,1,0:T(8,128)(2,1)} %get-tuple-element.92), channel_id=1, source_target_pairs={{0,2},{2,0},{4,6},{6,4},{8,10},{10,8},{12,14},{14,12},{16,18},{18,... | collective-permute-start | bytes 6291464 | tf_op jit(solution)/shard_map/ppermute | solution.py:728
  89.5 37.6 %collective-permute-start.6 = (bf16[16,4,32,512]{3,2,1,0:T(8,128)(2,1)}, bf16[16,4,32,512]{3,2,1,0:T(8,128)(2,1)}, u32[]{:S(2)}, u32[]{:S(2)}) collective-permute-start(bf16[16,4,32,512]{3,2,1,0:T(8,128)(2,1)} %get-tuple-element.101), channel_id=1, source_target_pairs={{0,1},{1,0},{2,3},{3,2},{4,5},{5,4},{6,7},{7,6},{8,9},{9,8},{10,11... | collective-permute-start | bytes 6291464 | tf_op jit(solution)/shard_map/ppermute | solution.py:732
  89.9 31.9 %collective-permute-start.4 = (bf16[8,4,32,512]{3,2,1,0:T(8,128)(2,1)}, bf16[8,4,32,512]{3,2,1,0:T(8,128)(2,1)}, u32[]{:S(2)}, u32[]{:S(2)}) collective-permute-start(bf16[8,4,32,512]{3,2,1,0:T(8,128)(2,1)} %get-tuple-element.83.refs_7_), channel_id=1, source_target_pairs={{0,1},{1,0},{2,3},{3,2},{4,5},{5,4},{6,7},{7,6},{8,9},{9,8},{10,11... | collective-permute-start | bytes 3145736 | tf_op jit(solution)/shard_map/ppermute | solution.py:732
  90.1 31.8 %collective-permute-start.5 = (bf16[8,4,32,512]{3,2,1,0:T(8,128)(2,1)}, bf16[8,4,32,512]{3,2,1,0:T(8,128)(2,1)}, u32[]{:S(2)}, u32[]{:S(2)}) collective-permute-start(bf16[8,4,32,512]{3,2,1,0:T(8,128)(2,1)} %get-tuple-element.97), channel_id=1, source_target_pairs={{0,1},{1,0},{2,3},{3,2},{4,5},{5,4},{6,7},{7,6},{8,9},{9,8},{10,11... | collective-permute-start | bytes 3145736 | tf_op jit(solution)/shard_map/ppermute | solution.py:732
  99.9 12.3 %copy-start.5 = (bf16[8,64,2048]{2,1,0:T(8,128)(2,1)S(1)}, bf16[8,64,2048]{2,1,0:T(8,128)(2,1)}, u32[]{:S(2)}) copy-start(bf16[8,64,2048]{2,1,0:T(8,128)(2,1)} %get-tuple-element.89) | copy-start | bytes 6291460
  114.8 26.8 %collective-permute-start.9 = (bf16[4,64,2048]{2,1,0:T(8,128)(2,1)S(1)}, bf16[4,64,2048]{2,1,0:T(8,128)(2,1)}, u32[]{:S(2)}, u32[]{:S(2)}) collective-permute-start(bf16[4,64,2048]{2,1,0:T(8,128)(2,1)S(1)} %get-tuple-element.165.refs_4_), channel_id=1, source_target_pairs={{0,2},{2,0},{4,6},{6,4},{8,10},{10,8},{12,14},{14,12},{16,18},{18,... | collective-permute-start | bytes 3145736 | tf_op jit(solution)/shard_map/ppermute | solution.py:728
  120.1 26.4 %collective-permute-start.8 = (bf16[4,128,1024]{2,1,0:T(8,128)(2,1)}, bf16[4,128,1024]{2,1,0:T(8,128)(2,1)}, u32[]{:S(2)}, u32[]{:S(2)}) collective-permute-start(bf16[4,128,1024]{2,1,0:T(8,128)(2,1)} %get-tuple-element.167.refs_5_), channel_id=1, source_target_pairs={{0,4},{2,6},{4,0},{6,2},{8,12},{10,14},{12,8},{14,10},{16,20},{18,... | collective-permute-start | bytes 3145736 | tf_op jit(solution)/shard_map/ppermute | solution.py:728
  123.9 31.2 %collective-permute-start.7 = (bf16[8,4,32,512]{3,2,1,0:T(8,128)(2,1)S(1)}, bf16[8,4,32,512]{3,2,1,0:T(8,128)(2,1)}, u32[]{:S(2)}, u32[]{:S(2)}) collective-permute-start(bf16[8,4,32,512]{3,2,1,0:T(8,128)(2,1)S(1)} %add_convert_fusion.5.refs_6_), channel_id=1, source_target_pairs={{0,8},{2,10},{4,12},{6,14},{8,0},{10,2},{12,4},{14,6},{16,24},{18,... | collective-permute-start | bytes 3145736 | tf_op jit(solution)/shard_map/ppermute | solution.py:728
  130.9 36.5 %collective-permute-start.13 = (bf16[8,4,32,512]{3,2,1,0:T(8,128)(2,1)}, bf16[8,4,32,512]{3,2,1,0:T(8,128)(2,1)}, u32[]{:S(2)}, u32[]{:S(2)}) collective-permute-start(bf16[8,4,32,512]{3,2,1,0:T(8,128)(2,1)} %get-tuple-element.169.refs_7_), channel_id=1, source_target_pairs={{0,4},{2,6},{4,0},{6,2},{8,12},{10,14},{12,8},{14,10},{16,20},{18,... | collective-permute-start | bytes 3145736 | tf_op jit(solution)/shard_map/ppermute | solution.py:728
  143.2 26.5 %collective-permute-start.12 = (bf16[2,64,2048]{2,1,0:T(8,128)(2,1)S(1)}, bf16[2,64,2048]{2,1,0:T(8,128)(2,1)S(1)}, u32[]{:S(2)}, u32[]{:S(2)}) collective-permute-start(bf16[2,64,2048]{2,1,0:T(8,128)(2,1)S(1)} %get-tuple-element.173), channel_id=1, source_target_pairs={{0,16},{2,18},{4,20},{6,22},{8,24},{10,26},{12,28},{14,30},{16,0},... | collective-permute-start | bytes 1572872 | tf_op jit(solution)/shard_map/ppermute | solution.py:728
  148.1 19.3 %copy-start.2 = (bf16[8,4,32,512]{3,2,1,0:T(8,128)(2,1)S(1)}, bf16[8,4,32,512]{3,2,1,0:T(8,128)(2,1)}, u32[]{:S(2)}) copy-start(bf16[8,4,32,512]{3,2,1,0:T(8,128)(2,1)} %get-tuple-element.115) | copy-start | bytes 3145732
  148.1 23.2 %collective-permute-start.11 = (bf16[2,128,1024]{2,1,0:T(8,128)(2,1)S(1)}, bf16[2,128,1024]{2,1,0:T(8,128)(2,1)S(1)}, u32[]{:S(2)}, u32[]{:S(2)}) collective-permute-start(bf16[2,128,1024]{2,1,0:T(8,128)(2,1)S(1)} %get-tuple-element.175), channel_id=1, source_target_pairs={{0,8},{2,10},{4,12},{6,14},{8,0},{10,2},{12,4},{14,6},{16,24},{18,... | collective-permute-start | bytes 1572872 | tf_op jit(solution)/shard_map/ppermute | solution.py:728
  156.7 17.5 %collective-permute-start.10 = (bf16[4,4,32,512]{3,2,1,0:T(8,128)(2,1)S(1)}, bf16[4,4,32,512]{3,2,1,0:T(8,128)(2,1)S(1)}, u32[]{:S(2)}, u32[]{:S(2)}) collective-permute-start(bf16[4,4,32,512]{3,2,1,0:T(8,128)(2,1)S(1)} %get-tuple-element.171), channel_id=1, source_target_pairs={{0,2},{2,0},{4,6},{6,4},{8,10},{10,8},{12,14},{14,12},{16,18},{18,... | collective-permute-start | bytes 1572872 | tf_op jit(solution)/shard_map/ppermute | solution.py:728
  169.0 12.4 %collective-permute-start.16 = (bf16[4,4,32,512]{3,2,1,0:T(8,128)(2,1)S(1)}, bf16[4,4,32,512]{3,2,1,0:T(8,128)(2,1)S(1)}, u32[]{:S(2)}, u32[]{:S(2)}) collective-permute-start(bf16[4,4,32,512]{3,2,1,0:T(8,128)(2,1)S(1)} %get-tuple-element.176), channel_id=1, source_target_pairs={{0,2},{2,0},{4,6},{6,4},{8,10},{10,8},{12,14},{14,12},{16,18},{18,... | collective-permute-start | bytes 1572872 | tf_op jit(solution)/shard_map/ppermute | solution.py:728
  169.8 8.7 %collective-permute-start.19 = (bf16[64,2048]{1,0:T(8,128)(2,1)S(1)}, bf16[64,2048]{1,0:T(8,128)(2,1)S(1)}, u32[]{:S(2)}, u32[]{:S(2)}) collective-permute-start(bf16[64,2048]{1,0:T(8,128)(2,1)S(1)} %fusion.2), channel_id=1, source_target_pairs={{0,4},{2,6},{4,0},{6,2},{8,12},{10,14},{12,8},{14,10},{16,20},{18,... | collective-permute-start | bytes 786440 | tf_op jit(solution)/shard_map/ppermute | solution.py:728
  171.5 13.0 %collective-permute-start.15 = (bf16[128,1024]{1,0:T(8,128)(2,1)S(1)}, bf16[128,1024]{1,0:T(8,128)(2,1)S(1)}, u32[]{:S(2)}, u32[]{:S(2)}) collective-permute-start(bf16[128,1024]{1,0:T(8,128)(2,1)S(1)} %fusion.3), channel_id=1, source_target_pairs={{0,16},{2,18},{4,20},{6,22},{8,24},{10,26},{12,28},{14,30},{16,0},... | collective-permute-start | bytes 786440 | tf_op jit(solution)/shard_map/ppermute | solution.py:728
  174.3 10.3 %collective-permute-start.14 = (bf16[2,4,32,512]{3,2,1,0:T(8,128)(2,1)S(1)}, bf16[2,4,32,512]{3,2,1,0:T(8,128)(2,1)S(1)}, u32[]{:S(2)}, u32[]{:S(2)}) collective-permute-start(bf16[2,4,32,512]{3,2,1,0:T(8,128)(2,1)S(1)} %get-tuple-element.179), channel_id=1, source_target_pairs={{0,4},{2,6},{4,0},{6,2},{8,12},{10,14},{12,8},{14,10},{16,20},{18,... | collective-permute-start | bytes 786440 | tf_op jit(solution)/shard_map/ppermute | solution.py:728
  178.6 7.0 %collective-permute-start.20 = (f32[32,2048]{1,0:T(8,128)S(1)}, f32[32,2048]{1,0:T(8,128)S(1)}, u32[]{:S(2)}, u32[]{:S(2)}) collective-permute-start(f32[32,2048]{1,0:T(8,128)S(1)} %constant_dynamic-slice_fusion), channel_id=1, source_target_pairs={{0,1},{1,0},{2,3},{3,2},{4,5},{5,4},{6,7},{7,6},{8,9},{9,8},{10,11... | collective-permute-start | bytes 786440 | tf_op jit(solution)/shard_map/ppermute | solution.py:732
  181.6 8.3 %collective-permute-start.17 = (bf16[2,4,32,512]{3,2,1,0:T(8,128)(2,1)S(1)}, bf16[2,4,32,512]{3,2,1,0:T(8,128)(2,1)S(1)}, u32[]{:S(2)}, u32[]{:S(2)}) collective-permute-start(bf16[2,4,32,512]{3,2,1,0:T(8,128)(2,1)S(1)} %get-tuple-element.180), channel_id=1, source_target_pairs={{0,8},{2,10},{4,12},{6,14},{8,0},{10,2},{12,4},{14,6},{16,24},{18,... | collective-permute-start | bytes 786440 | tf_op jit(solution)/shard_map/ppermute | solution.py:728
  190.1 16.8 %collective-permute-start.18 = (bf16[4,32,1024]{2,1,0:T(8,128)(2,1)S(1)}, bf16[4,32,1024]{2,1,0:T(8,128)(2,1)S(1)}, u32[]{:S(2)}, u32[]{:S(2)}) collective-permute-start(bf16[4,32,1024]{2,1,0:T(8,128)(2,1)S(1)} %pad_maximum_fusion.1), channel_id=1, source_target_pairs={{0,16},{2,18},{4,20},{6,22},{8,24},{10,26},{12,28},{14,30},{16,0},... | collective-permute-start | bytes 786440 | tf_op jit(solution)/shard_map/ppermute | solution.py:728
  192.5 14.0 %all-to-all-start = ((f32[32,3,32]{2,1,0:T(4,128)}), f32[32,3,32]{2,1,0:T(4,128)S(1)}, u32[]{:S(2)}, u32[]{:S(2)}) async-start(f32[32,3,32]{2,1,0:T(4,128)} %copy.28), calls=%async_computation | async-start | bytes 131072 | tf_op jit(solution)/shard_map/all_to_all | solution.py:890
  (8 other events, 39.1 us)
